TPU v7x, 512 devices: a whole 4x8x8 slice. The times are simulated.
512 devices in a mesh: gx: 64 (over z, y), gz: 8 (over x, core).
Axes of the slice: x: 4, y: 8, z: 8, core: 2. Of those that a mesh axis runs over, the one named last changes fastest.
Arguments:
- flow: float32 [4, 64, 2048, 128], P(None, 'gz', 'gx'), may hold values from -6 to 6
- fluid: float32 [64, 2048, 128], P('gz', 'gx'), may hold values from 0.2 to 5
- density: float32 [64, 2048, 128], P('gz', 'gx'), may hold values from 0.35 to 0.92
- thickness: float32 [2048, 128], P('gx'), may hold values from 0.5 to 4
- bed: float32 [2048, 128], P('gx'), may hold values from -6 to 6
- smb: float32 [2048, 128], P('gx'), may hold values from -3 to 3
- mask: int32 [2048, 128], P('gx'), may hold values from 0 to 2
Outputs:
- flow_out: float32 [4, 64, 2048, 128], P(None, 'gz', 'gx')
- new_thickness: float32 [2048, 128], P('gx')
- overburden: float32 [64, 2048, 128], P('gz', 'gx')
Inputs may be any that keep to these rules, and one draw needn't show every extreme that they name: `mask`: 0 marks an ice-free column, 1 grounded ice, 2 floating ice.
All inputs are finite; a program needn't handle non-finite values.
Results may differ from a plain program's by a relative error of at most 0.00002.
Values sent between devices are 32-bit elements; how exact they have to be, the bound alone decides.
No kernel may reach another device: no remote copies, remote signals or barrier semaphores. Data moves between devices by JAX's collectives and lax.ppermute only.
A program may use at most 64 MiB of HBM per device.

v0:
```python
import jax
import jax.numpy as jnp
from jax import lax
from jax.sharding import PartitionSpec as P

ITERS = 2


REGULAR = 0.01
FRICTION = 2.0
VELOCITY_STEP = 0.2
PRESSURE_STEP = 0.2
TIME_STEP = 0.5


def with_halo(cells, sides, width):
    for axis, dim in sides:
        count = lax.axis_size(axis)
        ends = count - 1
        head = lax.slice_in_dim(cells, 0, width, axis=dim)
        tail = lax.slice_in_dim(cells, cells.shape[dim] - width, cells.shape[dim], axis=dim)
        cells = jnp.concatenate(
            [
                lax.ppermute(tail, axis, [(i, (i + 1) % count) for i in range(ends)]),
                cells,
                lax.ppermute(head, axis, [((i + 1) % count, i) for i in range(ends)]),
            ],
            axis=dim,
        )
    return cells


def sent_to_all(value, axis):
    copies = jnp.broadcast_to(value, (lax.axis_size(axis), *value.shape))
    return lax.all_to_all(copies, axis, split_axis=0, concat_axis=0, tiled=True)


def taken_together(value, axis):
    return sent_to_all(value, axis).sum(axis=0)


def joined_by_halves(pieces, combine):
    while len(jax.tree.leaves(pieces)[0]) > 1:
        pieces = jax.vmap(combine)(*(pieces[side::2] for side in (0, 1)))
    return pieces[0]


def prefix(value, axis, combine, identity):
    count, place = (lax.axis_size(axis), lax.axis_index(axis))
    passed = jnp.arange(count) > place

    def kept(part, zero, own):
        part = jnp.where(
            passed.reshape(-1, *(1 for _ in own.shape)), part, jnp.asarray(zero, own.dtype)
        )
        return part[::-1]

    pieces = sent_to_all(value, axis)
    return joined_by_halves(kept(pieces, identity, value), combine)


def central(field, direction):
    lead = field.ndim - 3
    upper = []
    lower = []
    for number in range(field.ndim):
        extent = field.shape[number]
        if number == lead + direction:
            upper.append(slice(2, extent))
            lower.append(slice(0, extent - 2))
        else:
            upper.append(slice(1, extent - 1))
            lower.append(slice(1, extent - 1))
    return 0.5 * (field[tuple(upper)] - field[tuple(lower)])


def stresses(padded, fluidity):
    speed_x = padded[0]
    speed_y = padded[1]
    speed_z = padded[2]
    strain_xx = central(speed_x, 1)
    strain_yy = central(speed_y, 2)
    strain_zz = central(speed_z, 0)
    strain_xy = 0.5 * (central(speed_x, 2) + central(speed_y, 1))
    strain_xz = 0.5 * (central(speed_x, 0) + central(speed_z, 1))
    strain_yz = 0.5 * (central(speed_y, 0) + central(speed_z, 2))
    second = 0.5 * (strain_xx * strain_xx + strain_yy * strain_yy + strain_zz * strain_zz)
    second = second + strain_xy * strain_xy + strain_xz * strain_xz + strain_yz * strain_yz
    viscous = 0.5 * jnp.power(fluidity, -1.0 / 3.0) * jnp.power(second + REGULAR, -1.0 / 3.0)
    stress = (
        2.0
        * viscous[None]
        * jnp.stack([strain_xx, strain_yy, strain_zz, strain_xy, strain_xz, strain_yz])
    )
    return (stress, viscous, strain_xx + strain_yy + strain_zz)


def momentum(stress_padded, pressure_padded):
    force_x = (
        central(stress_padded[0], 1)
        + central(stress_padded[3], 2)
        + central(stress_padded[4], 0)
        - central(pressure_padded, 1)
    )
    force_y = (
        central(stress_padded[3], 1)
        + central(stress_padded[1], 2)
        + central(stress_padded[5], 0)
        - central(pressure_padded, 2)
    )
    force_z = (
        central(stress_padded[4], 1)
        + central(stress_padded[5], 2)
        + central(stress_padded[2], 0)
        - central(pressure_padded, 0)
    )
    return (force_x, force_y, force_z)


def advance(state, forces, viscous, dilation, slope_x, slope_y, ice, grounded, bottom):
    force_x = forces[0] - slope_x[None] - FRICTION * grounded[None] * bottom * state[0]
    force_y = forces[1] - slope_y[None] - FRICTION * grounded[None] * bottom * state[1]
    force_z = forces[2]
    moved = jnp.stack(
        [
            state[0] + VELOCITY_STEP * force_x / viscous,
            state[1] + VELOCITY_STEP * force_y / viscous,
            state[2] + VELOCITY_STEP * force_z / viscous,
            state[3] - PRESSURE_STEP * viscous * dilation,
        ]
    )
    return moved * ice[None, None]


def widen_last(field):
    widths = [(0, 0)] * (field.ndim - 1) + [(1, 1)]
    return jnp.pad(field, widths)


def add_levels(earlier, later):
    return earlier + later


def body(flow, fluid, density, thickness, bed, smb, mask):
    levels = flow.shape[1]
    columns = flow.shape[2]
    level_devices = lax.axis_size("gz")
    level_index = lax.axis_index("gz")
    column_index = lax.axis_index("gx")
    levels_total = levels * level_devices
    columns_total = columns * lax.axis_size("gx")
    surface = with_halo(bed + thickness, (("gx", 0),), 1)
    surface = widen_last(surface)
    slope_x = 0.5 * (surface[2:, 1:-1] - surface[:-2, 1:-1])
    slope_y = 0.5 * (surface[1:-1, 2:] - surface[1:-1, :-2])
    ice = (mask > 0).astype(jnp.float32)
    grounded = (mask == 1).astype(jnp.float32)
    level_place = level_index * levels + jnp.arange(levels, dtype=jnp.int32)
    bottom = (level_place == 0).astype(jnp.float32)[:, None, None]
    state = flow
    fluid_wide = with_halo(fluid, (("gx", 1), ("gz", 0)), 1)
    level_rim = level_index * levels - 1 + jnp.arange(levels + 2, dtype=jnp.int32)
    column_rim = column_index * columns - 1 + jnp.arange(columns + 2, dtype=jnp.int32)
    inside_level = ((level_rim >= 0) & (level_rim < levels_total)).astype(jnp.float32)
    inside_column = ((column_rim >= 0) & (column_rim < columns_total)).astype(jnp.float32)
    inside = inside_level[:, None] * inside_column[None, :]
    fluid_wide = jnp.where(inside[:, :, None] > 0.5, fluid_wide, 1.0)
    for sweep in range(ITERS):
        padded = with_halo(state, (("gx", 2), ("gz", 1)), 2)
        padded = widen_last(padded)
        stress, viscous, dilation = stresses(padded, fluid_wide)
        stress = stress * inside[None, :, :, None]
        forces = momentum(widen_last(stress), padded[3, 1:-1, 1:-1, :])
        state = advance(
            state,
            forces,
            viscous[1:-1, 1:-1, :],
            dilation[1:-1, 1:-1, :],
            slope_x,
            slope_y,
            ice,
            grounded,
            bottom,
        )
    partial_flux = jnp.sum(state[:2], axis=1)
    total_flux = taken_together(partial_flux, "gz")
    fluxes = thickness[None] * total_flux / levels_total
    flux_padded = with_halo(fluxes, (("gx", 1),), 1)
    flux_padded = widen_last(flux_padded)
    spread = 0.5 * (flux_padded[0, 2:, 1:-1] - flux_padded[0, :-2, 1:-1])
    spread = spread + 0.5 * (flux_padded[1, 1:-1, 2:] - flux_padded[1, 1:-1, :-2])
    new_thickness = thickness + TIME_STEP * (smb - spread)
    column_sum = jnp.sum(density, axis=0)
    above = prefix(column_sum, "gz", add_levels, jnp.zeros_like(column_sum))
    suffix = jnp.flip(jnp.cumsum(jnp.flip(density, 0), 0), 0) - density
    overburden = new_thickness[None] * (above[None] + suffix + 0.5 * density) / levels_total
    return (state, new_thickness, overburden)


def solution(mesh):
    placed = (
        P(None, "gz", "gx", None),
        P("gz", "gx", None),
        P("gz", "gx", None),
        P("gx", None),
        P("gx", None),
        P("gx", None),
        P("gx", None),
    )
    return jax.shard_map(
        body,
        mesh=mesh,
        in_specs=placed,
        out_specs=(P(None, "gz", "gx", None), P("gx", None), P("gz", "gx", None)),
        check_vma=False,
    )
```

profile of v0, /device:TPU:256, one launch (start us, length us, event | category | flops | bytes accessed | tf_op | source)
XLA Modules:
  0.0 111.6 jit_solution(9268617033723085171)
XLA Ops:
  0.6 0.0 copy-start
  0.6 0.0 copy-start.1
  0.7 1.1 fusion.127
  1.7 3.5 %collective-permute-start.4 = (f32[4,8,2,128]{3,2,1,0:T(2,128)S(1)}, f32[4,8,2,128]{3,2,1,0:T(2,128)S(1)}, u32[]{:S(2)}, u32[]{:S(2)}) collective-permute-start(f32[4,8,2,128]{3,2,1,0:T(2,128)S(1)} %get-tuple-element.47), channel_id=1, source_target_pairs={{0,8},{8,16},{16,24},{24,32},{32,40},{40,48},{48,56},{56,64},{64,7... | collective-permute-start | bytes 98312 | tf_op jit(solution)/shard_map/ppermute | solution.py:24
  5.2 5.7 %collective-permute-start.5 = (f32[4,8,2,128]{3,2,1,0:T(2,128)S(1)}, f32[4,8,2,128]{3,2,1,0:T(2,128)S(1)}, u32[]{:S(2)}, u32[]{:S(2)}) collective-permute-start(f32[4,8,2,128]{3,2,1,0:T(2,128)S(1)} %get-tuple-element.48), channel_id=1, source_target_pairs={{8,0},{16,8},{24,16},{32,24},{40,32},{48,40},{56,48},{64,56},{72,6... | collective-permute-start | bytes 98312 | tf_op jit(solution)/shard_map/ppermute | solution.py:26
  10.9 0.8 fusion.129
  11.7 1.9 %collective-permute-start = (f32[8,1,128]{2,1,0:T(1,128)S(1)}, f32[8,1,128]{2,1,0:T(1,128)S(1)}, u32[]{:S(2)}, u32[]{:S(2)}) collective-permute-start(f32[8,1,128]{2,1,0:T(1,128)S(1)} %get-tuple-element.53), channel_id=1, source_target_pairs={{0,8},{8,16},{16,24},{24,32},{32,40},{40,48},{48,56},{56,64},{64,7... | collective-permute-start | bytes 12296 | tf_op jit(solution)/shard_map/ppermute | solution.py:24
  13.6 0.7 add.217
  14.4 7.2 %collective-permute-start.8 = (f32[1,128]{1,0:T(1,128)S(1)}, f32[1,128]{1,0:T(1,128)S(1)}, u32[]{:S(2)}, u32[]{:S(2)}) collective-permute-start(f32[1,128]{1,0:T(1,128)S(1)} %get-tuple-element.58), channel_id=1, source_target_pairs={{8,0},{16,8},{24,16},{32,24},{40,32},{48,40},{56,48},{64,56},{72,6... | collective-permute-start | bytes 1544 | tf_op jit(solution)/shard_map/ppermute | solution.py:26
  21.6 1.9 %collective-permute-start.9 = (f32[1,128]{1,0:T(1,128)S(1)}, f32[1,128]{1,0:T(1,128)S(1)}, u32[]{:S(2)}, u32[]{:S(2)}) collective-permute-start(f32[1,128]{1,0:T(1,128)S(1)} %get-tuple-element.57), channel_id=1, source_target_pairs={{0,8},{8,16},{16,24},{24,32},{32,40},{40,48},{48,56},{56,64},{64,7... | collective-permute-start | bytes 1544 | tf_op jit(solution)/shard_map/ppermute | solution.py:24
  23.5 0.9 reduce_sum.29
  24.5 0.7 broadcast_in_dim.28
  25.1 4.3 %all-to-all-start.1 = ((f32[8,32,128]{2,1,0:T(8,128)}), f32[8,32,128]{2,1,0:T(8,128)S(1)}, u32[]{:S(2)}, u32[]{:S(2)}) async-start(f32[8,32,128]{2,1,0:T(8,128)} %broadcast_in_dim.28), calls=%async_computation.1 | async-start | bytes 262144 | tf_op jit(solution)/shard_map/all_to_all | solution.py:35
  29.4 0.1 broadcast_compare_fusion
  29.5 0.1 broadcast_multiply_fusion.2
  29.6 0.7 compare_select_fusion
  30.3 0.7 compare_convert_fusion
  31.0 0.9 rev.8
  32.0 0.2 fusion.132
  32.2 7.2 %collective-permute-start.1 = (f32[8,1,128]{2,1,0:T(1,128)S(1)}, f32[8,1,128]{2,1,0:T(1,128)S(1)}, u32[]{:S(2)}, u32[]{:S(2)}) collective-permute-start(f32[8,1,128]{2,1,0:T(1,128)S(1)} %get-tuple-element.54), channel_id=1, source_target_pairs={{8,0},{16,8},{24,16},{32,24},{40,32},{48,40},{56,48},{64,56},{72,6... | collective-permute-start | bytes 12296 | tf_op jit(solution)/shard_map/ppermute | solution.py:26
  39.5 0.1 select_maximum_fusion.10
  39.6 0.1 fusion.111
  39.7 1.0 pad_maximum_fusion.5
  40.7 2.1 %collective-permute-start.6 = (f32[4,2,36,128]{3,2,1,0:T(8,128)S(1)}, f32[4,2,36,128]{3,2,1,0:T(8,128)S(1)}, u32[]{:S(2)}, u32[]{:S(2)}) collective-permute-start(f32[4,2,36,128]{3,2,1,0:T(8,128)S(1)} %get-tuple-element.43), channel_id=1, source_target_pairs={{0,1},{1,2},{2,3},{3,4},{4,5},{5,6},{6,7},{8,9},{9,10},{10,11},{11... | collective-permute-start | bytes 442376 | tf_op jit(solution)/shard_map/ppermute | solution.py:24
  42.8 1.3 %collective-permute-start.7 = (f32[4,2,36,128]{3,2,1,0:T(8,128)S(1)}, f32[4,2,36,128]{3,2,1,0:T(8,128)S(1)}, u32[]{:S(2)}, u32[]{:S(2)}) collective-permute-start(f32[4,2,36,128]{3,2,1,0:T(8,128)S(1)} %get-tuple-element.44), channel_id=1, source_target_pairs={{1,0},{2,1},{3,2},{4,3},{5,4},{6,5},{7,6},{9,8},{10,9},{11,10},{12... | collective-permute-start | bytes 442376 | tf_op jit(solution)/shard_map/ppermute | solution.py:26
  44.2 4.4 %collective-permute-start.2 = (f32[1,34,128]{2,1,0:T(8,128)S(1)}, f32[1,34,128]{2,1,0:T(8,128)S(1)}, u32[]{:S(2)}, u32[]{:S(2)}) collective-permute-start(f32[1,34,128]{2,1,0:T(8,128)S(1)} %get-tuple-element.49), channel_id=1, source_target_pairs={{0,1},{1,2},{2,3},{3,4},{4,5},{5,6},{6,7},{8,9},{9,10},{10,11},{11... | collective-permute-start | bytes 52232 | tf_op jit(solution)/shard_map/ppermute | solution.py:24
  48.6 1.3 %collective-permute-start.3 = (f32[1,34,128]{2,1,0:T(8,128)S(1)}, f32[1,34,128]{2,1,0:T(8,128)S(1)}, u32[]{:S(2)}, u32[]{:S(2)}) collective-permute-start(f32[1,34,128]{2,1,0:T(8,128)S(1)} %get-tuple-element.50), channel_id=1, source_target_pairs={{1,0},{2,1},{3,2},{4,3},{5,4},{6,5},{7,6},{9,8},{10,9},{11,10},{12... | collective-permute-start | bytes 52232 | tf_op jit(solution)/shard_map/ppermute | solution.py:26
  50.0 0.7 select_maximum_fusion.4
  50.7 0.1 slice_bitcast_fusion.3
  50.9 2.1 %collective-permute-done.3 = f32[1,34,128]{2,1,0:T(8,128)S(1)} collective-permute-done((f32[1,34,128]{2,1,0:T(8,128)S(1)}, f32[1,34,128]{2,1,0:T(8,128)S(1)}, u32[]{:S(2)}, u32[]{:S(2)}) %collective-permute-start.3) | collective-permute-done | bytes 17440 | tf_op jit(solution)/shard_map/ppermute | solution.py:26
  53.0 1.1 %broadcast_multiply_fusion.1 = (f32[10,34,128]{2,1,0:T(8,128)S(1)}, f32[10,34,128]{2,1,0:T(8,128)S(1)}, f32[10,34,128]{2,1,0:T(8,128)S(1)}, f32[10,34,128]{2,1,0...) fusion(f32[1,34,128]{2,1,0:T(8,128)S(1)} %collective-permute-do, ...), kind=kLoop, calls=%fused_computation.215 | loop fusion | flops 1697280 | bytes 4700500 | tf_op jit(solution)/shard_map/mul | solution.py:91
  54.2 0.3 multiply_multiply_fusion.1
  54.5 0.7 fusion.1
  55.2 0.3 fusion.85
  55.5 0.3 fusion.42
  55.9 0.4 fusion.37
  56.3 1.9 %collective-permute-start.10 = (f32[4,8,2,128]{3,2,1,0:T(2,128)S(1)}, f32[4,8,2,128]{3,2,1,0:T(2,128)S(1)}, u32[]{:S(2)}, u32[]{:S(2)}) collective-permute-start(f32[4,8,2,128]{3,2,1,0:T(2,128)S(1)} %get-tuple-element.45), channel_id=1, source_target_pairs={{0,8},{8,16},{16,24},{24,32},{32,40},{40,48},{48,56},{56,64},{64,7... | collective-permute-start | bytes 98312 | tf_op jit(solution)/shard_map/ppermute | solution.py:24
  58.3 7.2 %collective-permute-start.11 = (f32[4,8,2,128]{3,2,1,0:T(2,128)S(1)}, f32[4,8,2,128]{3,2,1,0:T(2,128)S(1)}, u32[]{:S(2)}, u32[]{:S(2)}) collective-permute-start(f32[4,8,2,128]{3,2,1,0:T(2,128)S(1)} %get-tuple-element.46), channel_id=1, source_target_pairs={{8,0},{16,8},{24,16},{32,24},{40,32},{48,40},{56,48},{64,56},{72,6... | collective-permute-start | bytes 98312 | tf_op jit(solution)/shard_map/ppermute | solution.py:26
  65.5 0.1 broadcast_select_fusion
  65.6 1.5 %collective-permute-done.11 = f32[4,8,2,128]{3,2,1,0:T(2,128)S(1)} collective-permute-done((f32[4,8,2,128]{3,2,1,0:T(2,128)S(1)}, f32[4,8,2,128]{3,2,1,0:T(2,128)S(1)}, u32[]{:S(2)}, u32[]{:S(2)}) %collective-permute-start.11) | collective-permute-done | bytes 32800 | tf_op jit(solution)/shard_map/ppermute | solution.py:26
  67.1 3.3 %collective-permute-start.12 = (f32[4,2,36,128]{3,2,1,0:T(8,128)S(1)}, f32[4,2,36,128]{3,2,1,0:T(8,128)S(1)}, u32[]{:S(2)}, u32[]{:S(2)}) collective-permute-start(f32[4,2,36,128]{3,2,1,0:T(8,128)S(1)} %get-tuple-element.41), channel_id=1, source_target_pairs={{0,1},{1,2},{2,3},{3,4},{4,5},{5,6},{6,7},{8,9},{9,10},{10,11},{11... | collective-permute-start | bytes 442376 | tf_op jit(solution)/shard_map/ppermute | solution.py:24
  70.4 1.3 %collective-permute-start.13 = (f32[4,2,36,128]{3,2,1,0:T(8,128)S(1)}, f32[4,2,36,128]{3,2,1,0:T(8,128)S(1)}, u32[]{:S(2)}, u32[]{:S(2)}) collective-permute-start(f32[4,2,36,128]{3,2,1,0:T(8,128)S(1)} %get-tuple-element.42), channel_id=1, source_target_pairs={{1,0},{2,1},{3,2},{4,3},{5,4},{6,5},{7,6},{9,8},{10,9},{11,10},{12... | collective-permute-start | bytes 442376 | tf_op jit(solution)/shard_map/ppermute | solution.py:26
  71.8 2.6 %collective-permute-done.13 = f32[4,2,36,128]{3,2,1,0:T(8,128)S(1)} collective-permute-done((f32[4,2,36,128]{3,2,1,0:T(8,128)S(1)}, f32[4,2,36,128]{3,2,1,0:T(8,128)S(1)}, u32[]{:S(2)}, u32[]{:S(2)}) %collective-permute-start.13) | collective-permute-done | bytes 147488 | tf_op jit(solution)/shard_map/ppermute | solution.py:26
  74.4 0.7 select_maximum_fusion
  75.1 0.1 slice_bitcast_fusion
  75.2 1.1 %broadcast_multiply_fusion = (f32[10,34,128]{2,1,0:T(8,128)S(1)}, f32[10,34,128]{2,1,0:T(8,128)S(1)}, f32[10,34,128]{2,1,0:T(8,128)S(1)}, f32[10,34,128]{2,1,0:T...) fusion(f32[1,34,128]{2,1,0:T(8,128)S(1)} %collective-permute-do, ...), kind=kLoop, calls=%fused_computation.214 | loop fusion | flops 1697280 | bytes 4700500 | tf_op jit(solution)/shard_map/mul | solution.py:91
  76.5 0.3 multiply_multiply_fusion
  76.7 0.7 fusion.7
  77.4 0.3 fusion.52
  77.8 0.3 fusion.61
  78.1 0.0 copy-start.4
  78.1 0.4 fusion.47
  78.5 0.0 copy-start.3
  78.6 0.0 copy-start.2
  78.6 0.7 broadcast_in_dim.26
  79.3 7.4 %all-to-all-start = ((f32[8,2,32,128]{3,2,1,0:T(8,128)}), f32[8,2,32,128]{3,2,1,0:T(8,128)S(1)}, u32[]{:S(2)}, u32[]{:S(2)}) async-start(f32[8,2,32,128]{3,2,1,0:T(8,128)} %broadcast_in_dim.26), calls=%async_computation | async-start | bytes 524288 | tf_op jit(solution)/shard_map/all_to_all | solution.py:35
  86.8 7.5 %all-to-all-done = f32[8,2,32,128]{3,2,1,0:T(8,128)S(1)} async-done(((f32[8,2,32,128]{3,2,1,0:T(8,128)}), f32[8,2,32,128]{3,2,1,0:T(8,128)S(1)}, u32[]{:S(2)}, u32[]{:S(2)}) %all-to-all-start) | async-done | bytes 262176 | tf_op jit(solution)/shard_map/all_to_all | solution.py:35
  94.3 7.5 %collective-permute-start.14 = (f32[2,1,128]{2,1,0:T(1,128)S(1)}, f32[2,1,128]{2,1,0:T(1,128)S(1)}, u32[]{:S(2)}, u32[]{:S(2)}) collective-permute-start(f32[2,1,128]{2,1,0:T(1,128)S(1)} %get-tuple-element.56), channel_id=1, source_target_pairs={{8,0},{16,8},{24,16},{32,24},{40,32},{48,40},{56,48},{64,56},{72,6... | collective-permute-start | bytes 3080 | tf_op jit(solution)/shard_map/ppermute | solution.py:26
  101.9 1.9 %collective-permute-start.15 = (f32[2,1,128]{2,1,0:T(1,128)S(1)}, f32[2,1,128]{2,1,0:T(1,128)S(1)}, u32[]{:S(2)}, u32[]{:S(2)}) collective-permute-start(f32[2,1,128]{2,1,0:T(1,128)S(1)} %get-tuple-element.55), channel_id=1, source_target_pairs={{0,8},{8,16},{16,24},{24,32},{32,40},{40,48},{48,56},{56,64},{64,7... | collective-permute-start | bytes 3080 | tf_op jit(solution)/shard_map/ppermute | solution.py:24
  103.9 6.8 %collective-permute-done.15 = f32[2,1,128]{2,1,0:T(1,128)S(1)} collective-permute-done((f32[2,1,128]{2,1,0:T(1,128)S(1)}, f32[2,1,128]{2,1,0:T(1,128)S(1)}, u32[]{:S(2)}, u32[]{:S(2)}) %collective-permute-start.15) | collective-permute-done | bytes 1056 | tf_op jit(solution)/shard_map/ppermute | solution.py:24
  110.7 0.1 select_maximum_fusion.8
  110.8 0.1 fusion.109
  110.9 0.0 copy-start.5
  110.9 0.7 multiply_multiply_fusion.6
  (53 shorter events, 0.6 us)
Async XLA Ops:
  0.6 49.3 %copy-start = (f32[4,8,32,128]{3,2,1,0:T(8,128)S(1)}, f32[4,8,32,128]{3,2,1,0:T(8,128)}, u32[]{:S(2)}) copy-start(f32[4,8,32,128]{3,2,1,0:T(8,128)} %param.7) | copy-start | bytes 1572868
  0.6 43.5 %copy-start.1 = (f32[8,32,128]{2,1,0:T(8,128)S(1)}, f32[8,32,128]{2,1,0:T(8,128)}, u32[]{:S(2)}) copy-start(f32[8,32,128]{2,1,0:T(8,128)} %param.8) | copy-start | bytes 393220
  1.7 37.9 %collective-permute-start.4 = (f32[4,8,2,128]{3,2,1,0:T(2,128)S(1)}, f32[4,8,2,128]{3,2,1,0:T(2,128)S(1)}, u32[]{:S(2)}, u32[]{:S(2)}) collective-permute-start(f32[4,8,2,128]{3,2,1,0:T(2,128)S(1)} %get-tuple-element.47), channel_id=1, source_target_pairs={{0,8},{8,16},{16,24},{24,32},{32,40},{40,48},{48,56},{56,64},{64,7... | collective-permute-start | bytes 98312 | tf_op jit(solution)/shard_map/ppermute | solution.py:24
  5.2 34.4 %collective-permute-start.5 = (f32[4,8,2,128]{3,2,1,0:T(2,128)S(1)}, f32[4,8,2,128]{3,2,1,0:T(2,128)S(1)}, u32[]{:S(2)}, u32[]{:S(2)}) collective-permute-start(f32[4,8,2,128]{3,2,1,0:T(2,128)S(1)} %get-tuple-element.48), channel_id=1, source_target_pairs={{8,0},{16,8},{24,16},{32,24},{40,32},{48,40},{56,48},{64,56},{72,6... | collective-permute-start | bytes 98312 | tf_op jit(solution)/shard_map/ppermute | solution.py:26
  11.7 32.4 %collective-permute-start = (f32[8,1,128]{2,1,0:T(1,128)S(1)}, f32[8,1,128]{2,1,0:T(1,128)S(1)}, u32[]{:S(2)}, u32[]{:S(2)}) collective-permute-start(f32[8,1,128]{2,1,0:T(1,128)S(1)} %get-tuple-element.53), channel_id=1, source_target_pairs={{0,8},{8,16},{16,24},{24,32},{32,40},{40,48},{48,56},{56,64},{64,7... | collective-permute-start | bytes 12296 | tf_op jit(solution)/shard_map/ppermute | solution.py:24
  14.4 17.9 %collective-permute-start.8 = (f32[1,128]{1,0:T(1,128)S(1)}, f32[1,128]{1,0:T(1,128)S(1)}, u32[]{:S(2)}, u32[]{:S(2)}) collective-permute-start(f32[1,128]{1,0:T(1,128)S(1)} %get-tuple-element.58), channel_id=1, source_target_pairs={{8,0},{16,8},{24,16},{32,24},{40,32},{48,40},{56,48},{64,56},{72,6... | collective-permute-start | bytes 1544 | tf_op jit(solution)/shard_map/ppermute | solution.py:26
  21.6 17.9 %collective-permute-start.9 = (f32[1,128]{1,0:T(1,128)S(1)}, f32[1,128]{1,0:T(1,128)S(1)}, u32[]{:S(2)}, u32[]{:S(2)}) collective-permute-start(f32[1,128]{1,0:T(1,128)S(1)} %get-tuple-element.57), channel_id=1, source_target_pairs={{0,8},{8,16},{16,24},{24,32},{32,40},{40,48},{48,56},{56,64},{64,7... | collective-permute-start | bytes 1544 | tf_op jit(solution)/shard_map/ppermute | solution.py:24
  25.1 40.4 %all-to-all-start.1 = ((f32[8,32,128]{2,1,0:T(8,128)}), f32[8,32,128]{2,1,0:T(8,128)S(1)}, u32[]{:S(2)}, u32[]{:S(2)}) async-start(f32[8,32,128]{2,1,0:T(8,128)} %broadcast_in_dim.28), calls=%async_computation.1 | async-start | bytes 262144 | tf_op jit(solution)/shard_map/all_to_all | solution.py:35
  32.2 11.9 %collective-permute-start.1 = (f32[8,1,128]{2,1,0:T(1,128)S(1)}, f32[8,1,128]{2,1,0:T(1,128)S(1)}, u32[]{:S(2)}, u32[]{:S(2)}) collective-permute-start(f32[8,1,128]{2,1,0:T(1,128)S(1)} %get-tuple-element.54), channel_id=1, source_target_pairs={{8,0},{16,8},{24,16},{32,24},{40,32},{48,40},{56,48},{64,56},{72,6... | collective-permute-start | bytes 12296 | tf_op jit(solution)/shard_map/ppermute | solution.py:26
  40.7 9.3 %collective-permute-start.6 = (f32[4,2,36,128]{3,2,1,0:T(8,128)S(1)}, f32[4,2,36,128]{3,2,1,0:T(8,128)S(1)}, u32[]{:S(2)}, u32[]{:S(2)}) collective-permute-start(f32[4,2,36,128]{3,2,1,0:T(8,128)S(1)} %get-tuple-element.43), channel_id=1, source_target_pairs={{0,1},{1,2},{2,3},{3,4},{4,5},{5,6},{6,7},{8,9},{9,10},{10,11},{11... | collective-permute-start | bytes 442376 | tf_op jit(solution)/shard_map/ppermute | solution.py:24
  42.8 7.1 %collective-permute-start.7 = (f32[4,2,36,128]{3,2,1,0:T(8,128)S(1)}, f32[4,2,36,128]{3,2,1,0:T(8,128)S(1)}, u32[]{:S(2)}, u32[]{:S(2)}) collective-permute-start(f32[4,2,36,128]{3,2,1,0:T(8,128)S(1)} %get-tuple-element.44), channel_id=1, source_target_pairs={{1,0},{2,1},{3,2},{4,3},{5,4},{6,5},{7,6},{9,8},{10,9},{11,10},{12... | collective-permute-start | bytes 442376 | tf_op jit(solution)/shard_map/ppermute | solution.py:26
  44.2 6.7 %collective-permute-start.2 = (f32[1,34,128]{2,1,0:T(8,128)S(1)}, f32[1,34,128]{2,1,0:T(8,128)S(1)}, u32[]{:S(2)}, u32[]{:S(2)}) collective-permute-start(f32[1,34,128]{2,1,0:T(8,128)S(1)} %get-tuple-element.49), channel_id=1, source_target_pairs={{0,1},{1,2},{2,3},{3,4},{4,5},{5,6},{6,7},{8,9},{9,10},{10,11},{11... | collective-permute-start | bytes 52232 | tf_op jit(solution)/shard_map/ppermute | solution.py:24
  48.6 4.3 %collective-permute-start.3 = (f32[1,34,128]{2,1,0:T(8,128)S(1)}, f32[1,34,128]{2,1,0:T(8,128)S(1)}, u32[]{:S(2)}, u32[]{:S(2)}) collective-permute-start(f32[1,34,128]{2,1,0:T(8,128)S(1)} %get-tuple-element.50), channel_id=1, source_target_pairs={{1,0},{2,1},{3,2},{4,3},{5,4},{6,5},{7,6},{9,8},{10,9},{11,10},{12... | collective-permute-start | bytes 52232 | tf_op jit(solution)/shard_map/ppermute | solution.py:26
  56.3 9.3 %collective-permute-start.10 = (f32[4,8,2,128]{3,2,1,0:T(2,128)S(1)}, f32[4,8,2,128]{3,2,1,0:T(2,128)S(1)}, u32[]{:S(2)}, u32[]{:S(2)}) collective-permute-start(f32[4,8,2,128]{3,2,1,0:T(2,128)S(1)} %get-tuple-element.45), channel_id=1, source_target_pairs={{0,8},{8,16},{16,24},{24,32},{32,40},{40,48},{48,56},{56,64},{64,7... | collective-permute-start | bytes 98312 | tf_op jit(solution)/shard_map/ppermute | solution.py:24
  58.3 8.8 %collective-permute-start.11 = (f32[4,8,2,128]{3,2,1,0:T(2,128)S(1)}, f32[4,8,2,128]{3,2,1,0:T(2,128)S(1)}, u32[]{:S(2)}, u32[]{:S(2)}) collective-permute-start(f32[4,8,2,128]{3,2,1,0:T(2,128)S(1)} %get-tuple-element.46), channel_id=1, source_target_pairs={{8,0},{16,8},{24,16},{32,24},{40,32},{48,40},{56,48},{64,56},{72,6... | collective-permute-start | bytes 98312 | tf_op jit(solution)/shard_map/ppermute | solution.py:26
  67.1 4.6 %collective-permute-start.12 = (f32[4,2,36,128]{3,2,1,0:T(8,128)S(1)}, f32[4,2,36,128]{3,2,1,0:T(8,128)S(1)}, u32[]{:S(2)}, u32[]{:S(2)}) collective-permute-start(f32[4,2,36,128]{3,2,1,0:T(8,128)S(1)} %get-tuple-element.41), channel_id=1, source_target_pairs={{0,1},{1,2},{2,3},{3,4},{4,5},{5,6},{6,7},{8,9},{9,10},{10,11},{11... | collective-permute-start | bytes 442376 | tf_op jit(solution)/shard_map/ppermute | solution.py:24
  70.4 3.9 %collective-permute-start.13 = (f32[4,2,36,128]{3,2,1,0:T(8,128)S(1)}, f32[4,2,36,128]{3,2,1,0:T(8,128)S(1)}, u32[]{:S(2)}, u32[]{:S(2)}) collective-permute-start(f32[4,2,36,128]{3,2,1,0:T(8,128)S(1)} %get-tuple-element.42), channel_id=1, source_target_pairs={{1,0},{2,1},{3,2},{4,3},{5,4},{6,5},{7,6},{9,8},{10,9},{11,10},{12... | collective-permute-start | bytes 442376 | tf_op jit(solution)/shard_map/ppermute | solution.py:26
  78.1 16.2 %copy-start.4 = (f32[32,128]{1,0:T(8,128)S(1)}, f32[32,128]{1,0:T(8,128)}, u32[]{:S(2)}) copy-start(f32[32,128]{1,0:T(8,128)} %param.10) | copy-start | bytes 49156
  78.5 32.3 %copy-start.6 = (f32[32,128]{1,0:T(8,128)S(1)}, f32[32,128]{1,0:T(8,128)}, u32[]{:S(2)}) copy-start(f32[32,128]{1,0:T(8,128)} %param.12) | copy-start | bytes 49156
  78.5 32.4 %copy-start.3 = (f32[8,32,128]{2,1,0:T(8,128)S(1)}, f32[8,32,128]{2,1,0:T(8,128)}, u32[]{:S(2)}) copy-start(f32[8,32,128]{2,1,0:T(8,128)} %param.9) | copy-start | bytes 393220
  78.6 33.0 %copy-start.2 = (f32[4,8,32,128]{3,2,1,0:T(8,128)}, f32[4,8,32,128]{3,2,1,0:T(8,128)S(1)}, u32[]{:S(2)}) copy-start(f32[4,8,32,128]{3,2,1,0:T(8,128)S(1)} %maximum_multiply_fusion.1) | copy-start | bytes 1572868
  79.3 14.9 %all-to-all-start = ((f32[8,2,32,128]{3,2,1,0:T(8,128)}), f32[8,2,32,128]{3,2,1,0:T(8,128)S(1)}, u32[]{:S(2)}, u32[]{:S(2)}) async-start(f32[8,2,32,128]{3,2,1,0:T(8,128)} %broadcast_in_dim.26), calls=%async_computation | async-start | bytes 524288 | tf_op jit(solution)/shard_map/all_to_all | solution.py:35
  94.3 9.5 %collective-permute-start.14 = (f32[2,1,128]{2,1,0:T(1,128)S(1)}, f32[2,1,128]{2,1,0:T(1,128)S(1)}, u32[]{:S(2)}, u32[]{:S(2)}) collective-permute-start(f32[2,1,128]{2,1,0:T(1,128)S(1)} %get-tuple-element.56), channel_id=1, source_target_pairs={{8,0},{16,8},{24,16},{32,24},{40,32},{48,40},{56,48},{64,56},{72,6... | collective-permute-start | bytes 3080 | tf_op jit(solution)/shard_map/ppermute | solution.py:26
  101.9 8.8 %collective-permute-start.15 = (f32[2,1,128]{2,1,0:T(1,128)S(1)}, f32[2,1,128]{2,1,0:T(1,128)S(1)}, u32[]{:S(2)}, u32[]{:S(2)}) collective-permute-start(f32[2,1,128]{2,1,0:T(1,128)S(1)} %get-tuple-element.55), channel_id=1, source_target_pairs={{0,8},{8,16},{16,24},{24,32},{32,40},{40,48},{48,56},{56,64},{64,7... | collective-permute-start | bytes 3080 | tf_op jit(solution)/shard_map/ppermute | solution.py:24
  110.9 0.7 copy-start.5
where the time goes:
time: 113 us; the launch traced here: 112 us
  starting transfers between devices  71.5 us (63%)
  waiting for transfers between devices  20.6 us (18%)
  other arithmetic  12.1 us (11%)
  local copies, waits for them, and re-layouts  6.09 us (5%)
  between operations  1.28 us (1%)
    ppermute x8, starting transfers between devices, with_halo(): lax.ppermute(head, axis, [((i + 1) % count, i) for i in range(ends)])  38.8 us
    ppermute x8, starting transfers between devices, with_halo(): lax.ppermute(tail, axis, [(i, (i + 1) % count) for i in range(ends)])  21 us
    all_to_all x2, starting transfers between devices, sent_to_all(): return lax.all_to_all(copies, axis, split_axis=0, concat_axis=0, tiled=True)  11.7 us
    all_to_all x2, waiting for transfers between devices, sent_to_all(): return lax.all_to_all(copies, axis, split_axis=0, concat_axis=0, tiled=True)  7.51 us
    ppermute x8, waiting for transfers between devices, with_halo(): lax.ppermute(tail, axis, [(i, (i + 1) % count) for i in range(ends)])  6.85 us
    ppermute x8, waiting for transfers between devices, with_halo(): lax.ppermute(head, axis, [((i + 1) % count, i) for i in range(ends)])  6.2 us
  transfers between devices with their start and end apart: 18, of which 5 were waited for; matrix products, arithmetic and copies ran while one was open for 10% of the time, Pallas kernels for 0%

commit v1 on v0

v1 whole, which is shorter than its diff:
```python
import jax
import jax.numpy as jnp
from jax import lax
from jax.experimental import pallas as pl
from jax.experimental.pallas import tpu as pltpu
from jax.sharding import PartitionSpec as P

REGULAR = 0.01

DEEP = 4
WIDE = 5
WINDOW = 4
MARGIN = 8
VMEM_LIMIT = 24 * 1024 * 1024


def call(kernel, outs, scratch=(), aliases=None, cost=None):
    return pl.pallas_call(
        kernel,
        out_shape=outs,
        scratch_shapes=scratch,
        input_output_aliases=aliases or {},
        compiler_params=pltpu.CompilerParams(vmem_limit_bytes=VMEM_LIMIT),
        cost_estimate=cost,
    )


def f32(*shape):
    return jax.ShapeDtypeStruct(shape, jnp.float32)


def pack_columns(flow, fluid, bed, thickness, mask, low, high):
    parts, levels, columns, _ = flow.shape
    for out, start in ((low, 0), (high, columns - WIDE)):
        edge = slice(start, start + WIDE)
        place = 0
        for part in range(parts):
            for level in range(levels):
                out[place : place + WIDE, :] = flow[part, level, edge, :]
                place += WIDE
        for level in range(levels):
            out[place : place + WIDE, :] = fluid[level, edge, :]
            place += WIDE
        height = thickness[edge, :]
        out[place : place + WIDE, :] = bed[edge, :] + height
        out[place + WIDE : place + 2 * WIDE, :] = height
        out[place + 2 * WIDE : place + 3 * WIDE, :] = mask[edge, :].astype(jnp.float32)


def pack_levels(flow, fluid, left, right, low, high):
    parts, levels, columns, _ = flow.shape
    rows = columns + 2 * WINDOW
    skip = WIDE - WINDOW
    first = lax.axis_index("gx") == 0
    last = lax.axis_index("gx") == lax.axis_size("gx") - 1
    for out, start in ((low, 0), (high, levels - DEEP)):
        place = 0
        for part in range(parts + 1):
            for number in range(DEEP):
                level = start + number
                if part >= parts - 1 and number == (DEEP - 1 if start == 0 else 0):
                    continue
                own = flow.at[part, level] if part < parts else fluid.at[level]
                at = (part * levels + level) * WIDE
                before = left[at + skip : at + WIDE, :]
                after = right[at : at + WINDOW, :]
                if part == parts:
                    before = jnp.where(first, jnp.inf, before)
                    after = jnp.where(last, jnp.inf, after)
                out[place : place + WINDOW, :] = before
                out[place + WINDOW : place + WINDOW + columns, :] = own[...]
                out[place + WINDOW + columns : place + rows, :] = after
                place += rows


def assemble(flow, fluid, bed, thickness, mask, left, right, state, planes):
    parts, levels, columns, _ = flow.shape
    rows = columns + 2 * WINDOW
    lead = MARGIN + WINDOW
    first = lax.axis_index("gx") == 0
    last = lax.axis_index("gx") == lax.axis_size("gx") - 1
    for part in range(parts + 1):
        for level in range(levels):
            at = (part * levels + level) * WIDE
            own = flow[part, level] if part < parts else fluid[level]
            before = left[at : at + WIDE, :]
            after = right[at : at + WIDE, :]
            if part == parts:
                before = jnp.where(first, jnp.inf, before)
                after = jnp.where(last, jnp.inf, after)
            state[part, DEEP + level, lead - WIDE : lead, :] = before
            state[part, DEEP + level, lead : lead + columns, :] = own
            state[part, DEEP + level, lead + columns : lead + columns + WIDE, :] = after
    at = (parts + 1) * levels * WIDE
    for number, own in enumerate((bed[...] + thickness[...], thickness[...], mask[...].astype(jnp.float32))):
        spot = at + number * WIDE
        planes[number, lead - WIDE : lead, :] = left[spot : spot + WIDE, :]
        planes[number, lead : lead + columns, :] = own
        planes[number, lead + columns : lead + columns + WIDE, :] = right[spot : spot + WIDE, :]


def along_y(field):
    lane = lax.broadcasted_iota(jnp.int32, field.shape, 1)
    end = field.shape[1] - 1
    upper = jnp.where(lane < end, pltpu.roll(field, end, 1), 0.0)
    lower = jnp.where(lane > 0, pltpu.roll(field, 1, 1), 0.0)
    return upper - lower


def evolve(state_in, planes, below, above, density, out, message, state, stress, extra, slopes, marks):
    parts, levels, columns, lanes = out.shape
    rows = columns + 2 * WINDOW
    deep = levels + 2 * DEEP
    win = slice(MARGIN, MARGIN + rows)
    ahead = slice(MARGIN + 1, MARGIN + rows + 1)
    behind = slice(MARGIN - 1, MARGIN + rows - 1)
    lowest = lax.axis_index("gz") == 0
    highest = lax.axis_index("gz") == lax.axis_size("gz") - 1

    for part in range(parts + 1):
        for level in range(levels):
            state[part, DEEP + level] = state_in[part, DEEP + level]
    for source, start, outside in ((below, 0, lowest), (above, DEEP + levels, highest)):
        place = 0
        for part in range(parts + 1):
            for number in range(DEEP):
                if part >= parts - 1 and number == (0 if start == 0 else DEEP - 1):
                    continue
                plane = source[place : place + rows, :]
                if part == parts:
                    plane = jnp.where(outside, jnp.inf, plane)
                state[part, start + number, win, :] = plane
                place += rows

    slopes[0] = 4.0 * (planes[0, ahead, :] - planes[0, behind, :])
    slopes[1] = 4.0 * along_y(planes[0, win, :])
    kind = planes[2, win, :]
    ice = jnp.where(kind > 0.5, 1.0, 0.0)
    marks[0] = jnp.where(lowest, 0.0, ice)
    marks[1] = ice
    marks[2] = jnp.where(highest, 0.0, ice)
    marks[3] = jnp.zeros_like(ice)
    marks[4] = jnp.where(lowest & (kind > 0.5) & (kind < 1.5), 16.0, 0.0)

    def strain(k, carry):
        def across(part):
            return state[part, k, ahead, :] - state[part, k, behind, :]

        def upward(part):
            return state[part, k + 1, win, :] - state[part, k - 1, win, :]

        xx = across(0)
        yy = along_y(state[1, k, win, :])
        zz = upward(2)
        xy = along_y(state[0, k, win, :]) + across(1)
        xz = upward(0) + across(2)
        yz = upward(1) + along_y(state[2, k, win, :])
        second = 2.0 * (xx * xx + yy * yy + zz * zz) + (xy * xy + xz * xz + yz * yz)
        base = state[4, k, win, :] * (second * 0.0625 + REGULAR)
        root = jnp.exp2(jnp.log2(base) * (-1.0 / 3.0))
        pressure = state[3, k, win, :]
        push = 4.0 * pressure
        twice = 2.0 * root
        stress[0, k, win, :] = twice * xx - push
        stress[1, k, win, :] = twice * yy - push
        stress[2, k, win, :] = twice * zz - push
        stress[3, k, win, :] = root * xy
        stress[4, k, win, :] = root * xz
        stress[5, k, win, :] = root * yz
        extra[0, k] = 0.05 * (base * (root * root))
        extra[1, k] = pressure - (0.05 * root) * (xx + yy + zz)
        return carry

    def forces(k):
        def across(which):
            return stress[which, k, ahead, :] - stress[which, k, behind, :]

        def upward(which):
            return stress[which, k + 1, win, :] - stress[which, k - 1, win, :]

        def sideways(which):
            return along_y(stress[which, k, win, :])

        factor = extra[0, k]
        inside = marks[(k >= DEEP).astype(jnp.int32) + (k >= DEEP + levels).astype(jnp.int32)] > 0.5
        drag = marks[3 + (k == DEEP).astype(jnp.int32)]
        u = state[0, k, win, :]
        v = state[1, k, win, :]
        w = state[2, k, win, :]
        force_x = across(0) + sideways(3) + upward(4) - slopes[0] - drag * u
        force_y = across(3) + sideways(1) + upward(5) - slopes[1] - drag * v
        force_z = across(4) + sideways(5) + upward(2)
        return (
            jnp.where(inside, u + factor * force_x, 0.0),
            jnp.where(inside, v + factor * force_y, 0.0),
            jnp.where(inside, w + factor * force_z, 0.0),
            jnp.where(inside, extra[1, k], 0.0),
        )

    def first(k, carry):
        for part, value in enumerate(forces(k)):
            state[part, k, win, :] = value
        return carry

    own = slice(WINDOW, WINDOW + columns)

    def second(k, carry):
        values = forces(k)
        for part, value in enumerate(values):
            out[part, k - DEEP] = value[own, :]
        return carry[0] + values[0], carry[1] + values[1]

    lax.fori_loop(1, deep - 1, strain, 0)
    lax.fori_loop(2, deep - 2, first, 0)
    lax.fori_loop(3, deep - 3, strain, 0)
    nothing = jnp.zeros((rows, lanes), jnp.float32)
    sum_u, sum_v = lax.fori_loop(DEEP, deep - DEEP, second, (nothing, nothing))

    half = 0.5 / (levels * lax.axis_size("gz"))
    height = planes[1, win, :]
    slopes[0] = height * sum_u
    flux_y = along_y(height * sum_v)
    flux_x = slopes[0, WINDOW + 1 : WINDOW + columns + 1, :] - slopes[0, WINDOW - 1 : WINDOW + columns - 1, :]
    spread = half * (flux_x + flux_y[own, :])
    weight = jnp.sum(density[...], axis=0)
    for target in range(message.shape[0]):
        message[target, :columns, :] = spread
        message[target, columns:, :] = weight


def finish(message, density, thickness, smb, grown, burden):
    devices = message.shape[0]
    levels, columns, _ = density.shape
    place = lax.axis_index("gz")
    spread = message[0, :columns, :]
    over = jnp.where(place < 0, message[0, columns:, :], 0.0)
    for device in range(1, devices):
        spread = spread + message[device, :columns, :]
        over = over + jnp.where(place < device, message[device, columns:, :], 0.0)
    new = thickness[...] + 0.5 * (smb[...] - spread)
    grown[...] = new
    scaled = new * (1.0 / (levels * devices))
    for level in range(levels - 1, -1, -1):
        here = density[level]
        burden[level] = scaled * (over + 0.5 * here)
        over = over + here


def shifts(count):
    up = [(i, i + 1) for i in range(count - 1)]
    return up, [(j, i) for i, j in up]


def body(flow, fluid, density, thickness, bed, smb, mask):
    parts, levels, columns, lanes = flow.shape
    rows = columns + 2 * WINDOW
    deep = levels + 2 * DEEP
    tall = rows + 2 * MARGIN
    right_way, left_way = shifts(lax.axis_size("gx"))
    up_way, down_way = shifts(lax.axis_size("gz"))

    side = f32(((parts + 1) * levels + 3) * WIDE, lanes)
    to_left, to_right = call(pack_columns, (side, side))(flow, fluid, bed, thickness, mask)
    left = lax.ppermute(to_right, "gx", right_way)
    right = lax.ppermute(to_left, "gx", left_way)

    face = f32(((parts + 1) * DEEP - 2) * rows, lanes)
    to_below, to_above = call(pack_levels, (face, face))(flow, fluid, left, right)
    below = lax.ppermute(to_above, "gz", up_way)
    above = lax.ppermute(to_below, "gz", down_way)

    wide = f32(parts + 1, deep, tall, lanes)
    state, planes = call(
        assemble,
        (wide, f32(3, tall, lanes)),
        cost=pl.CostEstimate(flops=10_000_000, bytes_accessed=4_000_000, transcendentals=0),
    )(flow, fluid, bed, thickness, mask, left, right)

    message = f32(lax.axis_size("gz"), 2 * columns, lanes)
    moved, message = call(
        evolve,
        (f32(*flow.shape), message),
        scratch=[
            pltpu.VMEM((parts + 1, deep, tall, lanes), jnp.float32),
            pltpu.VMEM((6, deep, tall, lanes), jnp.float32),
            pltpu.VMEM((2, deep, rows, lanes), jnp.float32),
            pltpu.VMEM((2, rows, lanes), jnp.float32),
            pltpu.VMEM((5, rows, lanes), jnp.float32),
        ],
    )(state, planes, below, above, density)
    message = lax.all_to_all(message, "gz", split_axis=0, concat_axis=0, tiled=True)
    grown, burden = call(finish, (f32(columns, lanes), f32(*density.shape)))(message, density, thickness, smb)
    return moved, grown, burden


def solution(mesh):
    level_split = P("gz", "gx", None)
    flat = P("gx", None)
    return jax.shard_map(
        body,
        mesh=mesh,
        in_specs=(P(None, "gz", "gx", None), level_split, level_split, flat, flat, flat, flat),
        out_specs=(P(None, "gz", "gx", None), flat, level_split),
        check_vma=False,
    )
```

time: 113 us -> 50.4 us (0.45)
  the two profiles are of different devices: /device:TPU:256 before, /device:TPU:248 now
where the time goes in v1:
time: 50.4 us; the launch traced here: 49.9 us
  blocking collectives  16.7 us (33%)
  waiting for transfers between devices  11.9 us (24%)
  starting transfers between devices  9.35 us (19%)
  Pallas kernels  7.16 us (14%)
  local copies, waits for them, and re-layouts  4.1 us (8%)
  between operations  0.7 us (1%)
    all_to_all x1, blocking collectives, body(): lax.all_to_all(message, 'gz', split_axis=0, concat_axis=0, tiled=True)  16.7 us
    ppermute x1, waiting for transfers between devices, body(): right = lax.ppermute(to_left, 'gx', left_way)  7.65 us
    pallas_call x1, Pallas kernels, body(): call(evolve, (f32(*flow.shape), message), scratch=[pltpu.VMEM((parts + 1,...  6.27 us
    ppermute x1, starting transfers between devices, body(): left = lax.ppermute(to_right, 'gx', right_way)  4.83 us
    unnamed x14, local copies, waits for them, and re-layouts  4.1 us
    ppermute x1, waiting for transfers between devices, body(): above = lax.ppermute(to_below, 'gz', down_way)  3.89 us
    ppermute x1, starting transfers between devices, body(): right = lax.ppermute(to_left, 'gx', left_way)  1.92 us
    ppermute x1, starting transfers between devices, body(): below = lax.ppermute(to_above, 'gz', up_way)  1.31 us
  transfers between devices with their start and end apart: 4, of which 3 were waited for; matrix products, arithmetic and copies ran while one was open for 0% of the time, Pallas kernels for 0%

profile of v1, /device:TPU:248, one launch (start us, length us, event | category | flops | bytes accessed | tf_op | source)
XLA Modules:
  0.0 49.9 jit_solution(3821315201466614936)
XLA Ops:
  0.6 0.0 copy-start
  0.6 1.0 %copy-done = f32[4,8,32,128]{3,2,1,0:T(8,128)S(1)} copy-done((f32[4,8,32,128]{3,2,1,0:T(8,128)S(1)}, f32[4,8,32,128]{3,2,1,0:T(8,128)}, u32[]{:S(2)}) %copy-start) | copy-done | bytes 524312
  1.7 0.0 copy-start.1
  1.7 0.9 %copy-done.1 = f32[8,32,128]{2,1,0:T(8,128)S(1)} copy-done((f32[8,32,128]{2,1,0:T(8,128)S(1)}, f32[8,32,128]{2,1,0:T(8,128)}, u32[]{:S(2)}) %copy-start.1) | copy-done | bytes 131096
  2.6 0.0 copy-start.3
  2.6 0.7 %copy-done.3 = f32[32,128]{1,0:T(8,128)S(1)} copy-done((f32[32,128]{1,0:T(8,128)S(1)}, f32[32,128]{1,0:T(8,128)}, u32[]{:S(2)}) %copy-start.3) | copy-done | bytes 16408
  3.3 0.0 copy-start.4
  3.3 0.7 %copy-done.4 = f32[32,128]{1,0:T(8,128)S(1)} copy-done((f32[32,128]{1,0:T(8,128)S(1)}, f32[32,128]{1,0:T(8,128)}, u32[]{:S(2)}) %copy-start.4) | copy-done | bytes 16408
  4.0 0.0 copy-start.5
  4.0 0.7 %copy-done.5 = s32[32,128]{1,0:T(8,128)S(1)} copy-done((s32[32,128]{1,0:T(8,128)S(1)}, s32[32,128]{1,0:T(8,128)}, u32[]{:S(2)}) %copy-start.5) | copy-done | bytes 16408
  4.7 0.0 copy-start.2
  4.8 4.8 %collective-permute-start = (f32[215,128]{1,0:T(8,128)S(1)}, f32[215,128]{1,0:T(8,128)S(1)}, u32[]{:S(2)}, u32[]{:S(2)}) collective-permute-start(f32[215,128]{1,0:T(8,128)S(1)} %get-tuple-element.13), channel_id=1, source_target_pairs={{0,8},{8,16},{16,24},{24,32},{32,40},{40,48},{48,56},{56,64},{64,7... | collective-permute-start | bytes 330248 | tf_op jit(solution)/shard_map/ppermute | solution.py:264
  9.6 1.9 %collective-permute-start.1 = (f32[215,128]{1,0:T(8,128)S(1)}, f32[215,128]{1,0:T(8,128)S(1)}, u32[]{:S(2)}, u32[]{:S(2)}) collective-permute-start(f32[215,128]{1,0:T(8,128)S(1)} %get-tuple-element.14), channel_id=1, source_target_pairs={{8,0},{16,8},{24,16},{32,24},{40,32},{48,40},{56,48},{64,56},{72,6... | collective-permute-start | bytes 330248 | tf_op jit(solution)/shard_map/ppermute | solution.py:265
  11.5 0.4 collective-permute-done.left
  11.9 7.7 %collective-permute-done.1.right = f32[215,128]{1,0:T(8,128)S(1)} collective-permute-done((f32[215,128]{1,0:T(8,128)S(1)}, f32[215,128]{1,0:T(8,128)S(1)}, u32[]{:S(2)}, u32[]{:S(2)}) %collective-permute-start.1) | collective-permute-done | bytes 110112 | tf_op jit(solution)/shard_map/ppermute | solution.py:265
  19.6 0.1 shard_map.96
  19.6 1.3 %collective-permute-start.2 = (f32[720,128]{1,0:T(8,128)S(1)}, f32[720,128]{1,0:T(8,128)S(1)}, u32[]{:S(2)}, u32[]{:S(2)}) collective-permute-start(f32[720,128]{1,0:T(8,128)S(1)} %get-tuple-element.17), channel_id=1, source_target_pairs={{0,1},{1,2},{2,3},{3,4},{4,5},{5,6},{6,7},{8,9},{9,10},{10,11},{11... | collective-permute-start | bytes 1105928 | tf_op jit(solution)/shard_map/ppermute | solution.py:269
  21.0 0.0 copy-start.6
  21.0 1.3 %collective-permute-start.3 = (f32[720,128]{1,0:T(8,128)S(1)}, f32[720,128]{1,0:T(8,128)S(1)}, u32[]{:S(2)}, u32[]{:S(2)}) collective-permute-start(f32[720,128]{1,0:T(8,128)S(1)} %get-tuple-element.18), channel_id=1, source_target_pairs={{1,0},{2,1},{3,2},{4,3},{5,4},{6,5},{7,6},{9,8},{10,9},{11,10},{12... | collective-permute-start | bytes 1105928 | tf_op jit(solution)/shard_map/ppermute | solution.py:270
  22.3 0.1 shard_map.95
  22.4 0.0 collective-permute-done.2.below
  22.4 3.9 %collective-permute-done.3.above = f32[720,128]{1,0:T(8,128)S(1)} collective-permute-done((f32[720,128]{1,0:T(8,128)S(1)}, f32[720,128]{1,0:T(8,128)S(1)}, u32[]{:S(2)}, u32[]{:S(2)}) %collective-permute-start.3) | collective-permute-done | bytes 368672 | tf_op jit(solution)/shard_map/ppermute | solution.py:270
  26.3 0.0 copy-done.2
  26.3 6.3 %shard_map.97 = (f32[4,8,32,128]{3,2,1,0:T(8,128)}, f32[8,64,128]{2,1,0:T(8,128)S(1)}) custom-call(f32[5,16,56,128]{3,2,1,0:T(8,128)S(1)} %get-tuple-element.15.state_in, f32[3,56,128]{2,1,0:T(8,128)S(1)} %get-tuple-element.16.planes, f32[720,128]{1,0:T(8,128)S(1)} %collective-permute-done.2.below, f32[720,128]{1,0:T(8,128)S(1)} %collective-permute-done.3.above, ...), custom_call_target="tpu_custom_call" | custom-call | tf_op jit(solution)/shard_map/pallas_call | solution.py:280
  32.5 16.7 %all_to_all.5.message = f32[8,64,128]{2,1,0:T(8,128)S(1)} all-to-all(f32[8,64,128]{2,1,0:T(8,128)S(1)} %get-tuple-element.20), channel_id=1, replica_groups=mesh['gx'=64,'gz'=8] {'gz'}, dimensions={0} | all-to-all | bytes 524288 | tf_op jit(solution)/shard_map/all_to_all | solution.py:291
  49.2 0.0 copy-done.6
  49.2 0.7 %shard_map.98 = (f32[32,128]{1,0:T(8,128)}, f32[8,32,128]{2,1,0:T(8,128)}) custom-call(f32[8,64,128]{2,1,0:T(8,128)S(1)} %all_to_all.5.message, f32[8,32,128]{2,1,0:T(8,128)S(1)} %copy-done.2, f32[32,128]{1,0:T(8,128)S(1)} %copy-done.3, f32[32,128]{1,0:T(8,128)S(1)} %copy-done.6), custom_call_target="tpu_custom_call" | custom-call | tf_op jit(solution)/shard_map/pallas_call | solution.py:292
  (1 shorter events, 0.0 us)
Async XLA Ops:
  0.6 1.0 %copy-start = (f32[4,8,32,128]{3,2,1,0:T(8,128)S(1)}, f32[4,8,32,128]{3,2,1,0:T(8,128)}, u32[]{:S(2)}) copy-start(f32[4,8,32,128]{3,2,1,0:T(8,128)} %flow.5) | copy-start | bytes 1572868
  1.7 0.9 %copy-start.1 = (f32[8,32,128]{2,1,0:T(8,128)S(1)}, f32[8,32,128]{2,1,0:T(8,128)}, u32[]{:S(2)}) copy-start(f32[8,32,128]{2,1,0:T(8,128)} %fluid.5) | copy-start | bytes 393220
  2.6 0.7 %copy-start.3 = (f32[32,128]{1,0:T(8,128)S(1)}, f32[32,128]{1,0:T(8,128)}, u32[]{:S(2)}) copy-start(f32[32,128]{1,0:T(8,128)} %thickness.5) | copy-start | bytes 49156
  3.3 0.7 %copy-start.4 = (f32[32,128]{1,0:T(8,128)S(1)}, f32[32,128]{1,0:T(8,128)}, u32[]{:S(2)}) copy-start(f32[32,128]{1,0:T(8,128)} %bed.3) | copy-start | bytes 49156
  4.0 0.7 %copy-start.5 = (s32[32,128]{1,0:T(8,128)S(1)}, s32[32,128]{1,0:T(8,128)}, u32[]{:S(2)}) copy-start(s32[32,128]{1,0:T(8,128)} %mask.3) | copy-start | bytes 49156
  4.7 21.5 %copy-start.2 = (f32[8,32,128]{2,1,0:T(8,128)S(1)}, f32[8,32,128]{2,1,0:T(8,128)}, u32[]{:S(2)}) copy-start(f32[8,32,128]{2,1,0:T(8,128)} %density.3) | copy-start | bytes 393220
  4.8 7.1 %collective-permute-start = (f32[215,128]{1,0:T(8,128)S(1)}, f32[215,128]{1,0:T(8,128)S(1)}, u32[]{:S(2)}, u32[]{:S(2)}) collective-permute-start(f32[215,128]{1,0:T(8,128)S(1)} %get-tuple-element.13), channel_id=1, source_target_pairs={{0,8},{8,16},{16,24},{24,32},{32,40},{40,48},{48,56},{56,64},{64,7... | collective-permute-start | bytes 330248 | tf_op jit(solution)/shard_map/ppermute | solution.py:264
  9.6 10.0 %collective-permute-start.1 = (f32[215,128]{1,0:T(8,128)S(1)}, f32[215,128]{1,0:T(8,128)S(1)}, u32[]{:S(2)}, u32[]{:S(2)}) collective-permute-start(f32[215,128]{1,0:T(8,128)S(1)} %get-tuple-element.14), channel_id=1, source_target_pairs={{8,0},{16,8},{24,16},{32,24},{40,32},{48,40},{56,48},{64,56},{72,6... | collective-permute-start | bytes 330248 | tf_op jit(solution)/shard_map/ppermute | solution.py:265
  19.6 2.7 %collective-permute-start.2 = (f32[720,128]{1,0:T(8,128)S(1)}, f32[720,128]{1,0:T(8,128)S(1)}, u32[]{:S(2)}, u32[]{:S(2)}) collective-permute-start(f32[720,128]{1,0:T(8,128)S(1)} %get-tuple-element.17), channel_id=1, source_target_pairs={{0,1},{1,2},{2,3},{3,4},{4,5},{5,6},{6,7},{8,9},{9,10},{10,11},{11... | collective-permute-start | bytes 1105928 | tf_op jit(solution)/shard_map/ppermute | solution.py:269
  21.0 28.3 %copy-start.6 = (f32[32,128]{1,0:T(8,128)S(1)}, f32[32,128]{1,0:T(8,128)}, u32[]{:S(2)}) copy-start(f32[32,128]{1,0:T(8,128)} %smb.1) | copy-start | bytes 49156
  21.0 5.3 %collective-permute-start.3 = (f32[720,128]{1,0:T(8,128)S(1)}, f32[720,128]{1,0:T(8,128)S(1)}, u32[]{:S(2)}, u32[]{:S(2)}) collective-permute-start(f32[720,128]{1,0:T(8,128)S(1)} %get-tuple-element.18), channel_id=1, source_target_pairs={{1,0},{2,1},{3,2},{4,3},{5,4},{6,5},{7,6},{9,8},{10,9},{11,10},{12... | collective-permute-start | bytes 1105928 | tf_op jit(solution)/shard_map/ppermute | solution.py:270

commit v2 on v1

v2 whole, which is shorter than its diff:
```python
import functools

import jax
import jax.numpy as jnp
from jax import lax
from jax.experimental import pallas as pl
from jax.experimental.pallas import tpu as pltpu
from jax.sharding import PartitionSpec as P

REGULAR = 0.01

DEEP = 4
WIDE = 5
WINDOW = 4
MARGIN = 8
VMEM_LIMIT = 24 * 1024 * 1024


def call(kernel, outs, scratch=(), **specs):
    return pl.pallas_call(
        kernel,
        out_shape=outs,
        scratch_shapes=scratch,
        compiler_params=pltpu.CompilerParams(vmem_limit_bytes=VMEM_LIMIT),
        **specs,
    )


def f32(*shape):
    return jax.ShapeDtypeStruct(shape, jnp.float32)


def even(axis):
    return lax.rem(lax.axis_index(axis), 2) == 0


def face_planes(parts):
    for part in range(parts + 1):
        for number in range(DEEP if part < parts - 1 else DEEP - 1):
            yield part, number


def face_starts(part, parts, levels):
    return 0, levels - (DEEP if part < parts - 1 else DEEP - 1)


def pack_columns(
    flow_far, fluid_far, bed_far, thickness_far, mask_far,
    to_near, to_next, state, planes, flow, fluid, bed, thickness, mask, arrived,
):
    far = (flow_far, fluid_far, bed_far, thickness_far, mask_far)
    near = (flow, fluid, bed, thickness, mask)
    copies = [pltpu.make_async_copy(a, b, arrived.at[i]) for i, (a, b) in enumerate(zip(far, near, strict=True))]
    for copy in copies:
        copy.start()
    for copy in copies:
        copy.wait()
    parts, levels, columns, _ = flow.shape
    upward = even("gx")
    height = thickness[...]
    flat = (bed[...] + height, height, mask[...].astype(jnp.float32))
    place = 0

    def put(low, high):
        to_near[place : place + WIDE, :] = jnp.where(upward, high, low)
        to_next[place : place + WIDE, :] = jnp.where(upward, low, high)
        return place + WIDE

    for part in range(parts + 1):
        for level in range(levels):
            plane = flow.at[part, level] if part < parts else fluid.at[level]
            place = put(plane[:WIDE, :], plane[columns - WIDE :, :])
    for plane in flat:
        place = put(plane[:WIDE, :], plane[columns - WIDE :, :])
    lead = MARGIN + WINDOW
    for part in range(parts + 1):
        for level in range(levels):
            plane = flow.at[part, level] if part < parts else fluid.at[level]
            state[part, DEEP + level, lead : lead + columns, :] = plane[...]
    for number, plane in enumerate(flat):
        planes[number, lead : lead + columns, :] = plane


def unpaired(axis):
    place = lax.axis_index(axis)
    return (place == 0) | (place == lax.axis_size(axis) - 1)


def beside(near, next_, place, fluid_plane):
    inner = near[place : place + WIDE, :]
    beyond = next_[place : place + WIDE, :]
    if fluid_plane:
        beyond = jnp.where(unpaired("gx"), jnp.inf, beyond)
    return jnp.where(even("gx"), beyond, inner), jnp.where(even("gx"), inner, beyond)


def pack_levels(parts, levels, columns, state_in, planes_in, next_, near, state, planes, to_near, to_next):
    upward = even("gz")
    lead = MARGIN + WINDOW
    tail = lead + columns
    rows = columns + 2 * WINDOW
    for part in range(parts + 1):
        for level in range(levels):
            before, after = beside(near, next_, (part * levels + level) * WIDE, part == parts)
            state[part, DEEP + level, :, :] = state_in[part, DEEP + level]
            state[part, DEEP + level, lead - WIDE : lead, :] = before
            state[part, DEEP + level, tail : tail + WIDE, :] = after
    for number in range(planes.shape[0]):
        before, after = beside(near, next_, ((parts + 1) * levels + number) * WIDE, False)
        planes[number, :, :] = planes_in[number]
        planes[number, lead - WIDE : lead, :] = before
        planes[number, tail : tail + WIDE, :] = after
    for index, (part, number) in enumerate(face_planes(parts)):
        low, high = (DEEP + start + number for start in face_starts(part, parts, levels))
        spot = slice(index * rows, (index + 1) * rows)
        for out, level in ((to_near, jnp.where(upward, high, low)), (to_next, jnp.where(upward, low, high))):
            out[spot, :] = state[part, level, MARGIN : MARGIN + rows, :]


def along_y(field):
    lane = lax.broadcasted_iota(jnp.int32, field.shape, 1)
    end = field.shape[1] - 1
    upper = jnp.where(lane < end, pltpu.roll(field, end, 1), 0.0)
    lower = jnp.where(lane > 0, pltpu.roll(field, 1, 1), 0.0)
    return upper - lower


def evolve(state_in, planes, face_next, face_near, density, out, message, state, stress, extra, slopes, marks):
    parts, levels, columns, lanes = out.shape
    rows = columns + 2 * WINDOW
    deep = levels + 2 * DEEP
    win = slice(MARGIN, MARGIN + rows)
    ahead = slice(MARGIN + 1, MARGIN + rows + 1)
    behind = slice(MARGIN - 1, MARGIN + rows - 1)
    lowest = lax.axis_index("gz") == 0
    highest = lax.axis_index("gz") == lax.axis_size("gz") - 1
    upward = even("gz")

    for part in range(parts + 1):
        for level in range(levels):
            state[part, DEEP + level] = state_in[part, DEEP + level]
    for face, above in ((face_near, upward), (face_next, ~upward)):
        for index, (part, number) in enumerate(face_planes(parts)):
            plane = face[rows * index : rows * (index + 1), :]
            if part == parts and face is face_next:
                plane = jnp.where(unpaired("gz"), jnp.inf, plane)
            level = number + jnp.where(above, DEEP + levels, 0 if part < parts - 1 else 1)
            state[part, level, win, :] = plane

    slopes[0] = 4.0 * (planes[0, ahead, :] - planes[0, behind, :])
    slopes[1] = 4.0 * along_y(planes[0, win, :])
    kind = planes[2, win, :]
    ice = jnp.where(kind > 0.5, 1.0, 0.0)
    marks[0] = jnp.where(lowest, 0.0, ice)
    marks[1] = ice
    marks[2] = jnp.where(highest, 0.0, ice)
    marks[3] = jnp.zeros_like(ice)
    marks[4] = jnp.where(lowest & (kind > 0.5) & (kind < 1.5), 16.0, 0.0)

    def strain(k, carry):
        def across(part):
            return state[part, k, ahead, :] - state[part, k, behind, :]

        def upward(part):
            return state[part, k + 1, win, :] - state[part, k - 1, win, :]

        xx = across(0)
        yy = along_y(state[1, k, win, :])
        zz = upward(2)
        xy = along_y(state[0, k, win, :]) + across(1)
        xz = upward(0) + across(2)
        yz = upward(1) + along_y(state[2, k, win, :])
        second = 2.0 * (xx * xx + yy * yy + zz * zz) + (xy * xy + xz * xz + yz * yz)
        base = state[4, k, win, :] * (second * 0.0625 + REGULAR)
        root = jnp.exp2(jnp.log2(base) * (-1.0 / 3.0))
        pressure = state[3, k, win, :]
        push = 4.0 * pressure
        twice = 2.0 * root
        stress[0, k, win, :] = twice * xx - push
        stress[1, k, win, :] = twice * yy - push
        stress[2, k, win, :] = twice * zz - push
        stress[3, k, win, :] = root * xy
        stress[4, k, win, :] = root * xz
        stress[5, k, win, :] = root * yz
        extra[0, k] = 0.05 * (base * (root * root))
        extra[1, k] = pressure - (0.05 * root) * (xx + yy + zz)
        return carry

    def forces(k):
        def across(which):
            return stress[which, k, ahead, :] - stress[which, k, behind, :]

        def upward(which):
            return stress[which, k + 1, win, :] - stress[which, k - 1, win, :]

        def sideways(which):
            return along_y(stress[which, k, win, :])

        factor = extra[0, k]
        inside = marks[(k >= DEEP).astype(jnp.int32) + (k >= DEEP + levels).astype(jnp.int32)] > 0.5
        drag = marks[3 + (k == DEEP).astype(jnp.int32)]
        u = state[0, k, win, :]
        v = state[1, k, win, :]
        w = state[2, k, win, :]
        force_x = across(0) + sideways(3) + upward(4) - slopes[0] - drag * u
        force_y = across(3) + sideways(1) + upward(5) - slopes[1] - drag * v
        force_z = across(4) + sideways(5) + upward(2)
        return (
            jnp.where(inside, u + factor * force_x, 0.0),
            jnp.where(inside, v + factor * force_y, 0.0),
            jnp.where(inside, w + factor * force_z, 0.0),
            jnp.where(inside, extra[1, k], 0.0),
        )

    def first(k, carry):
        for part, value in enumerate(forces(k)):
            state[part, k, win, :] = value
        return carry

    own = slice(WINDOW, WINDOW + columns)

    def second(k, carry):
        values = forces(k)
        for part, value in enumerate(values):
            out[part, k - DEEP] = value[own, :]
        return carry[0] + values[0], carry[1] + values[1]

    lax.fori_loop(1, deep - 1, strain, 0)
    lax.fori_loop(2, deep - 2, first, 0)
    lax.fori_loop(3, deep - 3, strain, 0)
    nothing = jnp.zeros((rows, lanes), jnp.float32)
    sum_u, sum_v = lax.fori_loop(DEEP, deep - DEEP, second, (nothing, nothing))

    half = 0.5 / (levels * lax.axis_size("gz"))
    height = planes[1, win, :]
    slopes[0] = height * sum_u
    flux_y = along_y(height * sum_v)
    flux_x = slopes[0, WINDOW + 1 : WINDOW + columns + 1, :] - slopes[0, WINDOW - 1 : WINDOW + columns - 1, :]
    spread = half * (flux_x + flux_y[own, :])
    weight = jnp.sum(density[...], axis=0)
    for target in range(message.shape[0]):
        message[target, :columns, :] = spread
        message[target, columns:, :] = weight


def finish(message, density, thickness, smb, moved, grown, burden, out, sent):
    copy = pltpu.make_async_copy(moved, out, sent)
    copy.start()
    devices = message.shape[0]
    levels, columns, _ = density.shape
    place = lax.axis_index("gz")
    spread = message[0, :columns, :]
    over = jnp.where(place < 0, message[0, columns:, :], 0.0)
    for device in range(1, devices):
        spread = spread + message[device, :columns, :]
        over = over + jnp.where(place < device, message[device, columns:, :], 0.0)
    new = thickness[...] + 0.5 * (smb[...] - spread)
    grown[...] = new
    scaled = new * (1.0 / (levels * devices))
    for level in range(levels - 1, -1, -1):
        here = density[level]
        burden[level] = scaled * (over + 0.5 * here)
        over = over + here
    copy.wait()


def traded(to_near, to_next, axis):
    count = lax.axis_size(axis)
    pairs = [(i, i ^ 1) for i in range(count)]
    next_ = lax.ppermute(to_next, axis, [(i + 1, j + 1) for i, j in pairs[: count - 2]])
    near = lax.ppermute(to_near, axis, pairs)
    return near, next_


def body(flow, fluid, density, thickness, bed, smb, mask):
    parts, levels, columns, lanes = flow.shape
    rows = columns + 2 * WINDOW
    deep = levels + 2 * DEEP
    tall = rows + 2 * MARGIN
    side = f32(((parts + 1) * levels + 3) * WIDE, lanes)
    face = f32(((parts + 1) * DEEP - 2) * rows, lanes)
    wide = (parts + 1, deep, tall, lanes)
    flat = (3, tall, lanes)
    inputs = (flow, fluid, bed, thickness, mask)
    to_near, to_next, state, planes = call(
        pack_columns,
        (side, side, f32(*wide), f32(*flat)),
        in_specs=[pl.BlockSpec(memory_space=pltpu.HBM)] * len(inputs),
        scratch=[pltpu.VMEM(each.shape, each.dtype) for each in inputs] + [pltpu.SemaphoreType.DMA((len(inputs),))],
    )(*(pltpu.with_memory_space_constraint(each, pltpu.HBM) for each in inputs))
    near, next_ = traded(to_near, to_next, "gx")

    state, planes, to_near, to_next = call(
        functools.partial(pack_levels, parts, levels, columns),
        (f32(*wide), f32(*flat), face, face),
    )(state, planes, next_, near)
    face_near, face_next = traded(to_near, to_next, "gz")

    message = f32(lax.axis_size("gz"), 2 * columns, lanes)
    moved, message = call(
        evolve,
        (f32(*flow.shape), message),
        scratch=[
            pltpu.VMEM(wide, jnp.float32),
            pltpu.VMEM((6, deep, tall, lanes), jnp.float32),
            pltpu.VMEM((2, deep, rows, lanes), jnp.float32),
            pltpu.VMEM((2, rows, lanes), jnp.float32),
            pltpu.VMEM((5, rows, lanes), jnp.float32),
        ],
    )(state, planes, face_next, face_near, density)
    message = lax.all_to_all(message, "gz", split_axis=0, concat_axis=0, tiled=True)
    inner = pl.BlockSpec(memory_space=pltpu.VMEM)
    grown, burden, moved = call(
        finish,
        (f32(columns, lanes), f32(*density.shape), f32(*flow.shape)),
        out_specs=[inner, inner, pl.BlockSpec(memory_space=pltpu.HBM)],
        scratch=[pltpu.SemaphoreType.DMA],
    )(message, density, thickness, smb, moved)
    return moved, grown, burden


def solution(mesh):
    level_split = P("gz", "gx", None)
    flat = P("gx", None)
    return jax.shard_map(
        body,
        mesh=mesh,
        in_specs=(P(None, "gz", "gx", None), level_split, level_split, flat, flat, flat, flat),
        out_specs=(P(None, "gz", "gx", None), flat, level_split),
        check_vma=False,
    )
```

time: 50.4 us -> 41.9 us (0.83)
  the two profiles are of different devices: /device:TPU:248 before, /device:TPU:448 now
where the time goes in v2:
time: 41.9 us; the launch traced here: 41.6 us
  blocking collectives  13.7 us (33%)
  starting transfers between devices  12.7 us (30%)
  Pallas kernels  8.45 us (20%)
  waiting for transfers between devices  6 us (14%)
  between operations  0.72 us (2%)
    all_to_all x1, blocking collectives, body(): lax.all_to_all(message, 'gz', split_axis=0, concat_axis=0, tiled=True)  13.7 us
    ppermute x2, starting transfers between devices, traded(): near = lax.ppermute(to_near, axis, pairs)  6.66 us
    ppermute x2, starting transfers between devices, traded(): lax.ppermute(to_next, axis, [(i + 1, j + 1) for i, j in pairs[:count - 2]])  6.05 us
    pallas_call x1, Pallas kernels, body(): call(evolve, (f32(*flow.shape), message), scratch=[pltpu.VMEM(wide, jnp.f...  5.59 us
    ppermute x2, waiting for transfers between devices, traded(): near = lax.ppermute(to_near, axis, pairs)  4.5 us
    ppermute x2, waiting for transfers between devices, traded(): lax.ppermute(to_next, axis, [(i + 1, j + 1) for i, j in pairs[:count - 2]])  1.5 us
    pallas_call x1, Pallas kernels, body(): call(finish, (f32(columns, lanes), f32(*density.shape), f32(*flow.shape))...  1.46 us
    pallas_call x1, Pallas kernels, body(): call(pack_columns, (side, side, f32(*wide), f32(*flat)), in_specs=[pl.Blo...  1.23 us
  transfers between devices with their start and end apart: 4, of which 3 were waited for; matrix products, arithmetic and copies ran while one was open for 0% of the time, Pallas kernels for 0%

profile of v2, /device:TPU:448, one launch (start us, length us, event | category | flops | bytes accessed | tf_op | source)
XLA Modules:
  0.0 41.6 jit_solution(3406884390054207905)
XLA Ops:
  0.6 0.0 copy-start
  0.6 1.2 %shard_map.94 = (f32[215,128]{1,0:T(8,128)S(1)}, f32[215,128]{1,0:T(8,128)S(1)}, f32[5,16,56,128]{3,2,1,0:T(8,128)S(1)}, f32[3,56,128]{2,1,0:T(8,128)S(1)}) custom-call(f32[4,8,32,128]{3,2,1,0:T(8,128)} %flow_far.1, f32[8,32,128]{2,1,0:T(8,128)} %fluid_far.1, f32[32,128]{1,0:T(8,128)} %bed_far.1, f32[32,128]{1,0:T(8,128)} %thickness.1, s32[32,128]{1,0:T(8,128)} %mask_far.1), custom_call_target="tpu_custom_call" | custom-call | tf_op jit(solution)/shard_map/pallas_call | solution.py:285
  1.9 5.4 %collective-permute-start = (f32[215,128]{1,0:T(8,128)S(1)}, f32[215,128]{1,0:T(8,128)S(1)}, u32[]{:S(2)}, u32[]{:S(2)}) collective-permute-start(f32[215,128]{1,0:T(8,128)S(1)} %get-tuple-element.18), channel_id=1, source_target_pairs={{8,16},{16,8},{24,32},{32,24},{40,48},{48,40},{56,64},{64,56},{72,... | collective-permute-start | bytes 330248 | tf_op jit(solution)/shard_map/ppermute | solution.py:270
  7.2 1.9 %collective-permute-start.1 = (f32[215,128]{1,0:T(8,128)S(1)}, f32[215,128]{1,0:T(8,128)S(1)}, u32[]{:S(2)}, u32[]{:S(2)}) collective-permute-start(f32[215,128]{1,0:T(8,128)S(1)} %get-tuple-element.19), channel_id=1, source_target_pairs={{0,8},{8,0},{16,24},{24,16},{32,40},{40,32},{48,56},{56,48},{64,72... | collective-permute-start | bytes 330248 | tf_op jit(solution)/shard_map/ppermute | solution.py:271
  9.2 1.5 %collective-permute-done.next_ = f32[215,128]{1,0:T(8,128)S(1)} collective-permute-done((f32[215,128]{1,0:T(8,128)S(1)}, f32[215,128]{1,0:T(8,128)S(1)}, u32[]{:S(2)}, u32[]{:S(2)}) %collective-permute-start) | collective-permute-done | bytes 110112 | tf_op jit(solution)/shard_map/ppermute | solution.py:270
  10.7 3.2 %collective-permute-done.1.near = f32[215,128]{1,0:T(8,128)S(1)} collective-permute-done((f32[215,128]{1,0:T(8,128)S(1)}, f32[215,128]{1,0:T(8,128)S(1)}, u32[]{:S(2)}, u32[]{:S(2)}) %collective-permute-start.1) | collective-permute-done | bytes 110112 | tf_op jit(solution)/shard_map/ppermute | solution.py:271
  13.9 0.2 shard_map.95
  14.1 0.0 copy-start.1
  14.1 0.0 copy-start.2
  14.1 0.7 %collective-permute-start.2 = (f32[720,128]{1,0:T(8,128)S(1)}, f32[720,128]{1,0:T(8,128)S(1)}, u32[]{:S(2)}, u32[]{:S(2)}) collective-permute-start(f32[720,128]{1,0:T(8,128)S(1)} %get-tuple-element.22), channel_id=1, source_target_pairs={{1,2},{2,1},{3,4},{4,3},{5,6},{6,5},{9,10},{10,9},{11,12},{12,11},... | collective-permute-start | bytes 1105928 | tf_op jit(solution)/shard_map/ppermute | solution.py:270
  14.8 4.7 %collective-permute-start.3 = (f32[720,128]{1,0:T(8,128)S(1)}, f32[720,128]{1,0:T(8,128)S(1)}, u32[]{:S(2)}, u32[]{:S(2)}) collective-permute-start(f32[720,128]{1,0:T(8,128)S(1)} %get-tuple-element.23), channel_id=1, source_target_pairs={{0,1},{1,0},{2,3},{3,2},{4,5},{5,4},{6,7},{7,6},{8,9},{9,8},{10,11... | collective-permute-start | bytes 1105928 | tf_op jit(solution)/shard_map/ppermute | solution.py:271
  19.5 0.0 collective-permute-done.2.face_next
  19.5 1.3 %collective-permute-done.3.face_near = f32[720,128]{1,0:T(8,128)S(1)} collective-permute-done((f32[720,128]{1,0:T(8,128)S(1)}, f32[720,128]{1,0:T(8,128)S(1)}, u32[]{:S(2)}, u32[]{:S(2)}) %collective-permute-start.3) | collective-permute-done | bytes 368672 | tf_op jit(solution)/shard_map/ppermute | solution.py:271
  20.8 0.0 copy-done
  20.8 5.6 %shard_map.96 = (f32[4,8,32,128]{3,2,1,0:T(8,128)S(1)}, f32[8,64,128]{2,1,0:T(8,128)S(1)}) custom-call(f32[5,16,56,128]{3,2,1,0:T(8,128)S(1)} %get-tuple-element.20.state_in, f32[3,56,128]{2,1,0:T(8,128)S(1)} %get-tuple-element.21.planes, f32[720,128]{1,0:T(8,128)S(1)} %collective-permute-done.2.face_next, f32[720,128]{1,0:T(8,128)S(1)} %collective-permute-done.3.face_near, ...), custom_call_target="tpu_custom_call" | custom-call | tf_op jit(solution)/shard_map/pallas_call | solution.py:300
  26.4 13.7 %all_to_all.5.message = f32[8,64,128]{2,1,0:T(8,128)S(1)} all-to-all(f32[8,64,128]{2,1,0:T(8,128)S(1)} %get-tuple-element.24), channel_id=1, replica_groups=mesh['gx'=64,'gz'=8] {'gz'}, dimensions={0} | all-to-all | bytes 524288 | tf_op jit(solution)/shard_map/all_to_all | solution.py:311
  40.2 0.0 copy-done.1
  40.2 0.0 copy-done.2
  40.2 1.5 %shard_map.97 = (f32[32,128]{1,0:T(8,128)}, f32[8,32,128]{2,1,0:T(8,128)}, f32[4,8,32,128]{3,2,1,0:T(8,128)}) custom-call(f32[8,64,128]{2,1,0:T(8,128)S(1)} %all_to_all.5.message, f32[8,32,128]{2,1,0:T(8,128)S(1)} %copy-done, f32[32,128]{1,0:T(8,128)S(1)} %copy-done.1, f32[32,128]{1,0:T(8,128)S(1)} %copy-done.2, f32[4,8,32,128]{3,2,1,0:T(8,128)S(1)} %get-tuple-element.25.moved), custom_call_target="tpu_custom_call" | custom-call | tf_op jit(solution)/shard_map/pallas_call | solution.py:313
Async XLA Ops:
  0.6 20.2 %copy-start = (f32[8,32,128]{2,1,0:T(8,128)S(1)}, f32[8,32,128]{2,1,0:T(8,128)}, u32[]{:S(2)}) copy-start(f32[8,32,128]{2,1,0:T(8,128)} %density.3) | copy-start | bytes 393220
  1.9 8.8 %collective-permute-start = (f32[215,128]{1,0:T(8,128)S(1)}, f32[215,128]{1,0:T(8,128)S(1)}, u32[]{:S(2)}, u32[]{:S(2)}) collective-permute-start(f32[215,128]{1,0:T(8,128)S(1)} %get-tuple-element.18), channel_id=1, source_target_pairs={{8,16},{16,8},{24,32},{32,24},{40,48},{48,40},{56,64},{64,56},{72,... | collective-permute-start | bytes 330248 | tf_op jit(solution)/shard_map/ppermute | solution.py:270
  7.2 6.6 %collective-permute-start.1 = (f32[215,128]{1,0:T(8,128)S(1)}, f32[215,128]{1,0:T(8,128)S(1)}, u32[]{:S(2)}, u32[]{:S(2)}) collective-permute-start(f32[215,128]{1,0:T(8,128)S(1)} %get-tuple-element.19), channel_id=1, source_target_pairs={{0,8},{8,0},{16,24},{24,16},{32,40},{40,32},{48,56},{56,48},{64,72... | collective-permute-start | bytes 330248 | tf_op jit(solution)/shard_map/ppermute | solution.py:271
  14.1 26.1 %copy-start.1 = (f32[32,128]{1,0:T(8,128)S(1)}, f32[32,128]{1,0:T(8,128)}, u32[]{:S(2)}) copy-start(f32[32,128]{1,0:T(8,128)} %thickness.1) | copy-start | bytes 49156
  14.1 26.1 %copy-start.2 = (f32[32,128]{1,0:T(8,128)S(1)}, f32[32,128]{1,0:T(8,128)}, u32[]{:S(2)}) copy-start(f32[32,128]{1,0:T(8,128)} %smb.1) | copy-start | bytes 49156
  14.1 5.4 %collective-permute-start.2 = (f32[720,128]{1,0:T(8,128)S(1)}, f32[720,128]{1,0:T(8,128)S(1)}, u32[]{:S(2)}, u32[]{:S(2)}) collective-permute-start(f32[720,128]{1,0:T(8,128)S(1)} %get-tuple-element.22), channel_id=1, source_target_pairs={{1,2},{2,1},{3,4},{4,3},{5,6},{6,5},{9,10},{10,9},{11,12},{12,11},... | collective-permute-start | bytes 1105928 | tf_op jit(solution)/shard_map/ppermute | solution.py:270
  14.8 6.0 %collective-permute-start.3 = (f32[720,128]{1,0:T(8,128)S(1)}, f32[720,128]{1,0:T(8,128)S(1)}, u32[]{:S(2)}, u32[]{:S(2)}) collective-permute-start(f32[720,128]{1,0:T(8,128)S(1)} %get-tuple-element.23), channel_id=1, source_target_pairs={{0,1},{1,0},{2,3},{3,2},{4,5},{5,4},{6,7},{7,6},{8,9},{9,8},{10,11... | collective-permute-start | bytes 1105928 | tf_op jit(solution)/shard_map/ppermute | solution.py:271

commit v3 on v2

--- a/solution.py
+++ b/solution.py
@@ -14,6 +14,8 @@
 WINDOW = 4
 MARGIN = 8
 VMEM_LIMIT = 24 * 1024 * 1024
+WIDEN_COST = 5_000_000_000
+STORE_COST = 5_000_000
 
 
 def call(kernel, outs, scratch=(), **specs):
@@ -44,9 +46,9 @@
     return 0, levels - (DEEP if part < parts - 1 else DEEP - 1)
 
 
-def pack_columns(
+def prepare(
     flow_far, fluid_far, bed_far, thickness_far, mask_far,
-    to_near, to_next, state, planes, flow, fluid, bed, thickness, mask, arrived,
+    to_near, to_next, face_near, face_next, state, planes, flow, fluid, bed, thickness, mask, arrived,
 ):
     far = (flow_far, fluid_far, bed_far, thickness_far, mask_far)
     near = (flow, fluid, bed, thickness, mask)
@@ -72,6 +74,13 @@
             place = put(plane[:WIDE, :], plane[columns - WIDE :, :])
     for plane in flat:
         place = put(plane[:WIDE, :], plane[columns - WIDE :, :])
+    above = even("gz")
+    for index, (part, number) in enumerate(face_planes(parts)):
+        low, high = (start + number for start in face_starts(part, parts, levels))
+        whole = flow.at[part] if part < parts else fluid
+        spot = slice(index * columns, (index + 1) * columns)
+        face_near[spot, :] = whole[jnp.where(above, high, low)]
+        face_next[spot, :] = whole[jnp.where(above, low, high)]
     lead = MARGIN + WINDOW
     for part in range(parts + 1):
         for level in range(levels):
@@ -94,11 +103,22 @@
     return jnp.where(even("gx"), beyond, inner), jnp.where(even("gx"), inner, beyond)
 
 
-def pack_levels(parts, levels, columns, state_in, planes_in, next_, near, state, planes, to_near, to_next):
+def pack_corners(parts, levels, next_, near, to_near, to_next):
     upward = even("gz")
+    for index, (part, number) in enumerate(face_planes(parts)):
+        low, high = (
+            beside(near, next_, (part * levels + start + number) * WIDE, part == parts)
+            for start in face_starts(part, parts, levels)
+        )
+        for side, cut in ((0, slice(WIDE - WINDOW, WIDE)), (1, slice(0, WINDOW))):
+            spot = slice((2 * index + side) * WINDOW, (2 * index + side + 1) * WINDOW)
+            to_near[spot, :] = jnp.where(upward, high[side], low[side])[cut, :]
+            to_next[spot, :] = jnp.where(upward, low[side], high[side])[cut, :]
+
+
+def widen(parts, levels, columns, state_in, planes_in, next_, near, state, planes):
     lead = MARGIN + WINDOW
     tail = lead + columns
-    rows = columns + 2 * WINDOW
     for part in range(parts + 1):
         for level in range(levels):
             before, after = beside(near, next_, (part * levels + level) * WIDE, part == parts)
@@ -110,11 +130,6 @@
         planes[number, :, :] = planes_in[number]
         planes[number, lead - WIDE : lead, :] = before
         planes[number, tail : tail + WIDE, :] = after
-    for index, (part, number) in enumerate(face_planes(parts)):
-        low, high = (DEEP + start + number for start in face_starts(part, parts, levels))
-        spot = slice(index * rows, (index + 1) * rows)
-        for out, level in ((to_near, jnp.where(upward, high, low)), (to_next, jnp.where(upward, low, high))):
-            out[spot, :] = state[part, level, MARGIN : MARGIN + rows, :]
 
 
 def along_y(field):
@@ -125,7 +140,10 @@
     return upper - lower
 
 
-def evolve(state_in, planes, face_next, face_near, density, out, message, state, stress, extra, slopes, marks):
+def evolve(
+    state_in, planes, edge_next, edge_near, face_next, face_near, density,
+    out, message, state, stress, extra, slopes, marks,
+):
     parts, levels, columns, lanes = out.shape
     rows = columns + 2 * WINDOW
     deep = levels + 2 * DEEP
@@ -135,17 +153,22 @@
     lowest = lax.axis_index("gz") == 0
     highest = lax.axis_index("gz") == lax.axis_size("gz") - 1
     upward = even("gz")
+    lead = MARGIN + WINDOW
+    tail = lead + columns
 
     for part in range(parts + 1):
         for level in range(levels):
             state[part, DEEP + level] = state_in[part, DEEP + level]
-    for face, above in ((face_near, upward), (face_next, ~upward)):
+    for face, edge, above in ((face_near, edge_near, upward), (face_next, edge_next, ~upward)):
         for index, (part, number) in enumerate(face_planes(parts)):
-            plane = face[rows * index : rows * (index + 1), :]
+            middle = face[columns * index : columns * (index + 1), :]
+            sides = edge[2 * WINDOW * index : 2 * WINDOW * (index + 1), :]
             if part == parts and face is face_next:
-                plane = jnp.where(unpaired("gz"), jnp.inf, plane)
+                middle, sides = (jnp.where(unpaired("gz"), jnp.inf, each) for each in (middle, sides))
             level = number + jnp.where(above, DEEP + levels, 0 if part < parts - 1 else 1)
-            state[part, level, win, :] = plane
+            state[part, level, lead - WINDOW : lead, :] = sides[:WINDOW, :]
+            state[part, level, lead:tail, :] = middle
+            state[part, level, tail : tail + WINDOW, :] = sides[WINDOW:, :]
 
     slopes[0] = 4.0 * (planes[0, ahead, :] - planes[0, behind, :])
     slopes[1] = 4.0 * along_y(planes[0, win, :])
@@ -225,11 +248,11 @@
             out[part, k - DEEP] = value[own, :]
         return carry[0] + values[0], carry[1] + values[1]
 
-    lax.fori_loop(1, deep - 1, strain, 0)
-    lax.fori_loop(2, deep - 2, first, 0)
-    lax.fori_loop(3, deep - 3, strain, 0)
+    lax.fori_loop(1, deep - 1, strain, 0, unroll=True)
+    lax.fori_loop(2, deep - 2, first, 0, unroll=True)
+    lax.fori_loop(3, deep - 3, strain, 0, unroll=True)
     nothing = jnp.zeros((rows, lanes), jnp.float32)
-    sum_u, sum_v = lax.fori_loop(DEEP, deep - DEEP, second, (nothing, nothing))
+    sum_u, sum_v = lax.fori_loop(DEEP, deep - DEEP, second, (nothing, nothing), unroll=True)
 
     half = 0.5 / (levels * lax.axis_size("gz"))
     height = planes[1, win, :]
@@ -243,9 +266,13 @@
         message[target, columns:, :] = weight
 
 
-def finish(message, density, thickness, smb, moved, grown, burden, out, sent):
+def store(moved, out, sent):
     copy = pltpu.make_async_copy(moved, out, sent)
     copy.start()
+    copy.wait()
+
+
+def finish(message, density, thickness, smb, grown, burden):
     devices = message.shape[0]
     levels, columns, _ = density.shape
     place = lax.axis_index("gz")
@@ -261,7 +288,6 @@
         here = density[level]
         burden[level] = scaled * (over + 0.5 * here)
         over = over + here
-    copy.wait()
 
 
 def traded(to_near, to_next, axis):
@@ -278,23 +304,27 @@
     deep = levels + 2 * DEEP
     tall = rows + 2 * MARGIN
     side = f32(((parts + 1) * levels + 3) * WIDE, lanes)
-    face = f32(((parts + 1) * DEEP - 2) * rows, lanes)
+    faces = (parts + 1) * DEEP - 2
+    face = f32(faces * columns, lanes)
+    edge = f32(faces * 2 * WINDOW, lanes)
     wide = (parts + 1, deep, tall, lanes)
     flat = (3, tall, lanes)
     inputs = (flow, fluid, bed, thickness, mask)
-    to_near, to_next, state, planes = call(
-        pack_columns,
-        (side, side, f32(*wide), f32(*flat)),
+    to_near, to_next, face_near, face_next, state, planes = call(
+        prepare,
+        (side, side, face, face, f32(*wide), f32(*flat)),
         in_specs=[pl.BlockSpec(memory_space=pltpu.HBM)] * len(inputs),
         scratch=[pltpu.VMEM(each.shape, each.dtype) for each in inputs] + [pltpu.SemaphoreType.DMA((len(inputs),))],
     )(*(pltpu.with_memory_space_constraint(each, pltpu.HBM) for each in inputs))
     near, next_ = traded(to_near, to_next, "gx")
-
-    state, planes, to_near, to_next = call(
-        functools.partial(pack_levels, parts, levels, columns),
-        (f32(*wide), f32(*flat), face, face),
+    face_near, face_next = traded(face_near, face_next, "gz")
+    to_near, to_next = call(functools.partial(pack_corners, parts, levels), (edge, edge))(next_, near)
+    edge_near, edge_next = traded(to_near, to_next, "gz")
+    state, planes = call(
+        functools.partial(widen, parts, levels, columns),
+        (f32(*wide), f32(*flat)),
+        cost_estimate=pl.CostEstimate(flops=WIDEN_COST, bytes_accessed=WIDEN_COST, transcendentals=0),
     )(state, planes, next_, near)
-    face_near, face_next = traded(to_near, to_next, "gz")
 
     message = f32(lax.axis_size("gz"), 2 * columns, lanes)
     moved, message = call(
@@ -307,15 +337,16 @@
             pltpu.VMEM((2, rows, lanes), jnp.float32),
             pltpu.VMEM((5, rows, lanes), jnp.float32),
         ],
-    )(state, planes, face_next, face_near, density)
+    )(state, planes, edge_next, edge_near, face_next, face_near, density)
     message = lax.all_to_all(message, "gz", split_axis=0, concat_axis=0, tiled=True)
-    inner = pl.BlockSpec(memory_space=pltpu.VMEM)
-    grown, burden, moved = call(
-        finish,
-        (f32(columns, lanes), f32(*density.shape), f32(*flow.shape)),
-        out_specs=[inner, inner, pl.BlockSpec(memory_space=pltpu.HBM)],
+    moved = call(
+        store,
+        f32(*flow.shape),
+        out_specs=pl.BlockSpec(memory_space=pltpu.HBM),
         scratch=[pltpu.SemaphoreType.DMA],
-    )(message, density, thickness, smb, moved)
+        cost_estimate=pl.CostEstimate(flops=0, bytes_accessed=STORE_COST, transcendentals=0),
+    )(moved)
+    grown, burden = call(finish, (f32(columns, lanes), f32(*density.shape)))(message, density, thickness, smb)
     return moved, grown, burden
 
 

time: 41.9 us -> 36.5 us (0.87)
  the two profiles are of different devices: /device:TPU:448 before, /device:TPU:464 now
where the time goes in v3:
time: 36.5 us; the launch traced here: 36.1 us
  starting transfers between devices  22.4 us (61%)
  waiting for transfers between devices  7.43 us (20%)
  Pallas kernels  5.49 us (15%)
  between operations  0.76 us (2%)
    ppermute x3, starting transfers between devices, traded(): near = lax.ppermute(to_near, axis, pairs)  15.3 us
    all_to_all x1, waiting for transfers between devices, body(): lax.all_to_all(message, 'gz', split_axis=0, concat_axis=0, tiled=True)  6.67 us
    ppermute x3, starting transfers between devices, traded(): lax.ppermute(to_next, axis, [(i + 1, j + 1) for i, j in pairs[:count - 2]])  3.7 us
    all_to_all x1, starting transfers between devices, body(): lax.all_to_all(message, 'gz', split_axis=0, concat_axis=0, tiled=True)  3.41 us
    pallas_call x1, Pallas kernels, body(): call(evolve, (f32(*flow.shape), message), scratch=[pltpu.VMEM(wide, jnp.f...  2.59 us
    pallas_call x1, Pallas kernels, body(): call(prepare, (side, side, face, face, f32(*wide), f32(*flat)), in_specs=...  1.23 us
    pallas_call x1, Pallas kernels, body(): call(store, f32(*flow.shape), out_specs=pl.BlockSpec(memory_space=pltpu.H...  0.8 us
    ppermute x3, waiting for transfers between devices, traded(): near = lax.ppermute(to_near, axis, pairs)  0.75 us
  transfers between devices with their start and end apart: 7, of which 2 were waited for; matrix products, arithmetic and copies ran while one was open for 0% of the time, Pallas kernels for 3%

profile of v3, /device:TPU:464, one launch (start us, length us, event | category | flops | bytes accessed | tf_op | source)
XLA Modules:
  0.0 36.1 jit_solution(10839733000633632694)
XLA Ops:
  0.6 1.2 %shard_map.94 = (f32[215,128]{1,0:T(8,128)S(1)}, f32[215,128]{1,0:T(8,128)S(1)}, f32[576,128]{1,0:T(8,128)S(1)}, f32[576,128]{1,0:T(8,128)S(1)}, f32[5,16,56,128...) custom-call(f32[4,8,32,128]{3,2,1,0:T(8,128)} %flow_far.1, f32[8,32,128]{2,1,0:T(8,128)} %fluid_far.1, f32[32,128]{1,0:T(8,128)} %bed_far.1, ...), custom_call_target="tpu_custom_call" | custom-call | tf_op jit(solution)/shard_map/pallas_call | solution.py:313
  1.9 2.4 %collective-permute-start = (f32[215,128]{1,0:T(8,128)S(1)}, f32[215,128]{1,0:T(8,128)S(1)}, u32[]{:S(2)}, u32[]{:S(2)}) collective-permute-start(f32[215,128]{1,0:T(8,128)S(1)} %get-tuple-element.19), channel_id=1, source_target_pairs={{8,16},{16,8},{24,32},{32,24},{40,48},{48,40},{56,64},{64,56},{72,... | collective-permute-start | bytes 330248 | tf_op jit(solution)/shard_map/ppermute | solution.py:296
  4.2 5.8 %collective-permute-start.1 = (f32[215,128]{1,0:T(8,128)S(1)}, f32[215,128]{1,0:T(8,128)S(1)}, u32[]{:S(2)}, u32[]{:S(2)}) collective-permute-start(f32[215,128]{1,0:T(8,128)S(1)} %get-tuple-element.20), channel_id=1, source_target_pairs={{0,8},{8,0},{16,24},{24,16},{32,40},{40,32},{48,56},{56,48},{64,72... | collective-permute-start | bytes 330248 | tf_op jit(solution)/shard_map/ppermute | solution.py:297
  10.1 0.7 %collective-permute-start.4 = (f32[576,128]{1,0:T(8,128)S(1)}, f32[576,128]{1,0:T(8,128)S(1)}, u32[]{:S(2)}, u32[]{:S(2)}) collective-permute-start(f32[576,128]{1,0:T(8,128)S(1)} %get-tuple-element.25), channel_id=1, source_target_pairs={{1,2},{2,1},{3,4},{4,3},{5,6},{6,5},{9,10},{10,9},{11,12},{12,11},... | collective-permute-start | bytes 884744 | tf_op jit(solution)/shard_map/ppermute | solution.py:296
  10.8 4.7 %collective-permute-start.5 = (f32[576,128]{1,0:T(8,128)S(1)}, f32[576,128]{1,0:T(8,128)S(1)}, u32[]{:S(2)}, u32[]{:S(2)}) collective-permute-start(f32[576,128]{1,0:T(8,128)S(1)} %get-tuple-element.26), channel_id=1, source_target_pairs={{0,1},{1,0},{2,3},{3,2},{4,5},{5,4},{6,7},{7,6},{8,9},{9,8},{10,11... | collective-permute-start | bytes 884744 | tf_op jit(solution)/shard_map/ppermute | solution.py:297
  15.5 0.0 collective-permute-done.next_
  15.5 0.0 collective-permute-done.1.near
  15.6 0.7 %collective-permute-start.2 = (f32[144,128]{1,0:T(8,128)S(1)}, f32[144,128]{1,0:T(8,128)S(1)}, u32[]{:S(2)}, u32[]{:S(2)}) collective-permute-start(f32[144,128]{1,0:T(8,128)S(1)} %get-tuple-element.23), channel_id=1, source_target_pairs={{1,2},{2,1},{3,4},{4,3},{5,6},{6,5},{9,10},{10,9},{11,12},{12,11},... | collective-permute-start | bytes 221192 | tf_op jit(solution)/shard_map/ppermute | solution.py:296
  16.2 4.8 %collective-permute-start.3 = (f32[144,128]{1,0:T(8,128)S(1)}, f32[144,128]{1,0:T(8,128)S(1)}, u32[]{:S(2)}, u32[]{:S(2)}) collective-permute-start(f32[144,128]{1,0:T(8,128)S(1)} %get-tuple-element.24), channel_id=1, source_target_pairs={{0,1},{1,0},{2,3},{3,2},{4,5},{5,4},{6,7},{7,6},{8,9},{9,8},{10,11... | collective-permute-start | bytes 221192 | tf_op jit(solution)/shard_map/ppermute | solution.py:297
  21.0 0.0 copy-start
  21.0 0.1 shard_map.95
  21.2 0.0 collective-permute-done.2.edge_next
  21.2 0.7 %collective-permute-done.3.edge_near = f32[144,128]{1,0:T(8,128)S(1)} collective-permute-done((f32[144,128]{1,0:T(8,128)S(1)}, f32[144,128]{1,0:T(8,128)S(1)}, u32[]{:S(2)}, u32[]{:S(2)}) %collective-permute-start.3) | collective-permute-done | bytes 73760 | tf_op jit(solution)/shard_map/ppermute | solution.py:297
  21.9 0.0 collective-permute-done.4.face_next
  21.9 0.0 collective-permute-done.5.face_near
  21.9 0.0 copy-done
  21.9 0.0 copy-start.1
  21.9 0.0 copy-start.2
  21.9 2.6 %shard_map.97 = (f32[4,8,32,128]{3,2,1,0:T(8,128)S(1)}, f32[8,64,128]{2,1,0:T(8,128)}) custom-call(f32[5,16,56,128]{3,2,1,0:T(8,128)S(1)} %get-tuple-element.21.state_in, f32[3,56,128]{2,1,0:T(8,128)S(1)} %get-tuple-element.22.planes, f32[144,128]{1,0:T(8,128)S(1)} %collective-permute-done.2.edge_next, f32[144,128]{1,0:T(8,128)S(1)} %collective-permute-done.3.edge_near, ...), custom_call_target="tpu_custom_call" | custom-call | tf_op jit(solution)/shard_map/pallas_call | solution.py:330
  24.5 3.4 %all-to-all-start = ((f32[8,64,128]{2,1,0:T(8,128)}), f32[8,64,128]{2,1,0:T(8,128)S(1)}, u32[]{:S(2)}, u32[]{:S(2)}) async-start(f32[8,64,128]{2,1,0:T(8,128)} %get-tuple-element.28), calls=%async_computation | async-start | bytes 524288 | tf_op jit(solution)/shard_map/all_to_all | solution.py:341
  27.9 0.8 %shard_map.98 = f32[4,8,32,128]{3,2,1,0:T(8,128)} custom-call(f32[4,8,32,128]{3,2,1,0:T(8,128)S(1)} %get-tuple-element.27.moved), custom_call_target="tpu_custom_call" | custom-call | bytes 5000000 | tf_op jit(solution)/shard_map/pallas_call | solution.py:342
  28.8 6.7 %all-to-all-done.message = f32[8,64,128]{2,1,0:T(8,128)S(1)} async-done(((f32[8,64,128]{2,1,0:T(8,128)}), f32[8,64,128]{2,1,0:T(8,128)S(1)}, u32[]{:S(2)}, u32[]{:S(2)}) %all-to-all-start) | async-done | bytes 262176 | tf_op jit(solution)/shard_map/all_to_all | solution.py:341
  35.4 0.0 copy-done.1
  35.4 0.0 copy-done.2
  35.4 0.7 %shard_map.99 = (f32[32,128]{1,0:T(8,128)}, f32[8,32,128]{2,1,0:T(8,128)}) custom-call(f32[8,64,128]{2,1,0:T(8,128)S(1)} %all-to-all-done.message, f32[8,32,128]{2,1,0:T(8,128)S(1)} %copy-done, f32[32,128]{1,0:T(8,128)S(1)} %copy-done.1, f32[32,128]{1,0:T(8,128)S(1)} %copy-done.2), custom_call_target="tpu_custom_call" | custom-call | tf_op jit(solution)/shard_map/pallas_call | solution.py:349
  (1 shorter events, 0.0 us)
Async XLA Ops:
  1.9 13.6 %collective-permute-start = (f32[215,128]{1,0:T(8,128)S(1)}, f32[215,128]{1,0:T(8,128)S(1)}, u32[]{:S(2)}, u32[]{:S(2)}) collective-permute-start(f32[215,128]{1,0:T(8,128)S(1)} %get-tuple-element.19), channel_id=1, source_target_pairs={{8,16},{16,8},{24,32},{32,24},{40,48},{48,40},{56,64},{64,56},{72,... | collective-permute-start | bytes 330248 | tf_op jit(solution)/shard_map/ppermute | solution.py:296
  4.2 11.3 %collective-permute-start.1 = (f32[215,128]{1,0:T(8,128)S(1)}, f32[215,128]{1,0:T(8,128)S(1)}, u32[]{:S(2)}, u32[]{:S(2)}) collective-permute-start(f32[215,128]{1,0:T(8,128)S(1)} %get-tuple-element.20), channel_id=1, source_target_pairs={{0,8},{8,0},{16,24},{24,16},{32,40},{40,32},{48,56},{56,48},{64,72... | collective-permute-start | bytes 330248 | tf_op jit(solution)/shard_map/ppermute | solution.py:297
  10.1 11.8 %collective-permute-start.4 = (f32[576,128]{1,0:T(8,128)S(1)}, f32[576,128]{1,0:T(8,128)S(1)}, u32[]{:S(2)}, u32[]{:S(2)}) collective-permute-start(f32[576,128]{1,0:T(8,128)S(1)} %get-tuple-element.25), channel_id=1, source_target_pairs={{1,2},{2,1},{3,4},{4,3},{5,6},{6,5},{9,10},{10,9},{11,12},{12,11},... | collective-permute-start | bytes 884744 | tf_op jit(solution)/shard_map/ppermute | solution.py:296
  10.8 11.2 %collective-permute-start.5 = (f32[576,128]{1,0:T(8,128)S(1)}, f32[576,128]{1,0:T(8,128)S(1)}, u32[]{:S(2)}, u32[]{:S(2)}) collective-permute-start(f32[576,128]{1,0:T(8,128)S(1)} %get-tuple-element.26), channel_id=1, source_target_pairs={{0,1},{1,0},{2,3},{3,2},{4,5},{5,4},{6,7},{7,6},{8,9},{9,8},{10,11... | collective-permute-start | bytes 884744 | tf_op jit(solution)/shard_map/ppermute | solution.py:297
  15.6 5.6 %collective-permute-start.2 = (f32[144,128]{1,0:T(8,128)S(1)}, f32[144,128]{1,0:T(8,128)S(1)}, u32[]{:S(2)}, u32[]{:S(2)}) collective-permute-start(f32[144,128]{1,0:T(8,128)S(1)} %get-tuple-element.23), channel_id=1, source_target_pairs={{1,2},{2,1},{3,4},{4,3},{5,6},{6,5},{9,10},{10,9},{11,12},{12,11},... | collective-permute-start | bytes 221192 | tf_op jit(solution)/shard_map/ppermute | solution.py:296
  16.2 5.7 %collective-permute-start.3 = (f32[144,128]{1,0:T(8,128)S(1)}, f32[144,128]{1,0:T(8,128)S(1)}, u32[]{:S(2)}, u32[]{:S(2)}) collective-permute-start(f32[144,128]{1,0:T(8,128)S(1)} %get-tuple-element.24), channel_id=1, source_target_pairs={{0,1},{1,0},{2,3},{3,2},{4,5},{5,4},{6,7},{7,6},{8,9},{9,8},{10,11... | collective-permute-start | bytes 221192 | tf_op jit(solution)/shard_map/ppermute | solution.py:297
  21.0 0.9 %copy-start = (f32[8,32,128]{2,1,0:T(8,128)S(1)}, f32[8,32,128]{2,1,0:T(8,128)}, u32[]{:S(2)}) copy-start(f32[8,32,128]{2,1,0:T(8,128)} %density.3) | copy-start | bytes 393220
  21.9 13.5 %copy-start.1 = (f32[32,128]{1,0:T(8,128)S(1)}, f32[32,128]{1,0:T(8,128)}, u32[]{:S(2)}) copy-start(f32[32,128]{1,0:T(8,128)} %thickness.1) | copy-start | bytes 49156
  21.9 13.5 %copy-start.2 = (f32[32,128]{1,0:T(8,128)S(1)}, f32[32,128]{1,0:T(8,128)}, u32[]{:S(2)}) copy-start(f32[32,128]{1,0:T(8,128)} %smb.1) | copy-start | bytes 49156
  24.5 10.9 %all-to-all-start = ((f32[8,64,128]{2,1,0:T(8,128)}), f32[8,64,128]{2,1,0:T(8,128)S(1)}, u32[]{:S(2)}, u32[]{:S(2)}) async-start(f32[8,64,128]{2,1,0:T(8,128)} %get-tuple-element.28), calls=%async_computation | async-start | bytes 524288 | tf_op jit(solution)/shard_map/all_to_all | solution.py:341

commit v4 on v3

v4 whole, which is shorter than its diff:
```python
import jax
import jax.numpy as jnp
from jax import lax
from jax.experimental import pallas as pl
from jax.experimental.pallas import tpu as pltpu
from jax.sharding import PartitionSpec as P

REGULAR = 0.01

DEEP = 4
WIDE = 5
WINDOW = 4
MARGIN = 8
VMEM_LIMIT = 24 * 1024 * 1024
INNER_COST = 5_000_000_000
STORE_COST = 5_000_000


def call(kernel, outs, scratch=(), **specs):
    return pl.pallas_call(
        kernel,
        out_shape=outs,
        scratch_shapes=scratch,
        compiler_params=pltpu.CompilerParams(vmem_limit_bytes=VMEM_LIMIT),
        **specs,
    )


def f32(*shape):
    return jax.ShapeDtypeStruct(shape, jnp.float32)


def even(axis):
    return lax.rem(lax.axis_index(axis), 2) == 0


def face_planes(parts):
    for part in range(parts + 1):
        for number in range(DEEP if part < parts - 1 else DEEP - 1):
            yield part, number


def face_starts(part, parts, levels):
    return 0, levels - (DEEP if part < parts - 1 else DEEP - 1)


def prepare(
    flow_far, fluid_far, bed_far, thickness_far, mask_far, density_far,
    to_near, to_next, to_level, state, planes, weight, flow, fluid, bed, thickness, mask, density, arrived,
):
    far = (flow_far, fluid_far, bed_far, thickness_far, mask_far, density_far)
    near = (flow, fluid, bed, thickness, mask, density)
    copies = [pltpu.make_async_copy(a, b, arrived.at[i]) for i, (a, b) in enumerate(zip(far, near, strict=True))]
    for copy in copies:
        copy.start()
    for copy in copies:
        copy.wait()
    parts, levels, columns, _ = flow.shape
    upward = even("gx")
    height = thickness[...]
    flat = (bed[...] + height, height, mask[...].astype(jnp.float32))
    place = 0

    def put(low, high):
        to_near[place : place + WIDE, :] = jnp.where(upward, high, low)
        to_next[place : place + WIDE, :] = jnp.where(upward, low, high)
        return place + WIDE

    for part in range(parts + 1):
        for level in range(levels):
            plane = flow.at[part, level] if part < parts else fluid.at[level]
            place = put(plane[:WIDE, :], plane[columns - WIDE :, :])
    for plane in flat:
        place = put(plane[:WIDE, :], plane[columns - WIDE :, :])
    above = even("gz")
    for index, (part, number) in enumerate(face_planes(parts)):
        low, high = (start + number for start in face_starts(part, parts, levels))
        whole = flow.at[part] if part < parts else fluid
        spot = slice(index * columns, (index + 1) * columns)
        to_level[spot, :] = whole[jnp.where(above, low, high)]
    lead = MARGIN + WINDOW
    for part in range(parts + 1):
        for level in range(levels):
            plane = flow.at[part, level] if part < parts else fluid.at[level]
            state[part, level, lead : lead + columns, :] = plane[...]
    for number, plane in enumerate(flat):
        planes[number, lead : lead + columns, :] = plane
    weight[...] = jnp.sum(density[...], axis=0)


def unpaired(axis):
    place = lax.axis_index(axis)
    return (place == 0) | (place == lax.axis_size(axis) - 1)


def beside(near, next_, place, fluid_plane):
    inner = near[place : place + WIDE, :]
    beyond = next_[place : place + WIDE, :]
    if fluid_plane:
        beyond = jnp.where(unpaired("gx"), jnp.inf, beyond)
    return jnp.where(even("gx"), beyond, inner), jnp.where(even("gx"), inner, beyond)


def widen(state_in, planes_in, weight, next_, near, state, planes, to_next, to_near):
    parts, levels, tall, _ = state_in.shape
    parts -= 1
    rows = tall - 2 * MARGIN
    lead = MARGIN + WINDOW
    tail = MARGIN + rows - WINDOW
    upward = even("gz")
    for part in range(parts + 1):
        for level in range(levels):
            before, after = beside(near, next_, (part * levels + level) * WIDE, part == parts)
            state[part, level, :, :] = state_in[part, level]
            state[part, level, lead - WIDE : lead, :] = before
            state[part, level, tail : tail + WIDE, :] = after
    for number in range(planes.shape[0]):
        before, after = beside(near, next_, ((parts + 1) * levels + number) * WIDE, False)
        planes[number, :, :] = planes_in[number]
        planes[number, lead - WIDE : lead, :] = before
        planes[number, tail : tail + WIDE, :] = after
    count = 0
    for index, (part, number) in enumerate(face_planes(parts)):
        low, high = (start + number for start in face_starts(part, parts, levels))
        to_near[index * rows : (index + 1) * rows, :] = state[
            part, jnp.where(upward, high, low), MARGIN : MARGIN + rows, :
        ]
        level = jnp.where(upward, low, high)
        spot = 2 * WINDOW * index
        to_next[spot : spot + WINDOW, :] = state[part, level, MARGIN:lead, :]
        to_next[spot + WINDOW : spot + 2 * WINDOW, :] = state[part, level, tail : tail + WINDOW, :]
        count = index + 1
    to_near[count * rows :, :] = weight[...]


def along_y(field):
    lane = lax.broadcasted_iota(jnp.int32, field.shape, 1)
    end = field.shape[1] - 1
    upper = jnp.where(lane < end, pltpu.roll(field, end, 1), 0.0)
    lower = jnp.where(lane > 0, pltpu.roll(field, 1, 1), 0.0)
    return upper - lower


def window(rows):
    return tuple(slice(MARGIN + shift, MARGIN + shift + rows) for shift in (0, 1, -1))


def strain(rows, cells, k, stress, extra):
    win, ahead, behind = window(rows)

    def across(part):
        return cells(part, k)[ahead, :] - cells(part, k)[behind, :]

    def upward(part):
        return cells(part, k + 1)[win, :] - cells(part, k - 1)[win, :]

    def sideways(part):
        return along_y(cells(part, k)[win, :])

    xx = across(0)
    yy = sideways(1)
    zz = upward(2)
    xy = sideways(0) + across(1)
    xz = upward(0) + across(2)
    yz = upward(1) + sideways(2)
    second = 2.0 * (xx * xx + yy * yy + zz * zz) + (xy * xy + xz * xz + yz * yz)
    base = cells(4, k)[win, :] * (second * 0.0625 + REGULAR)
    root = jnp.exp2(jnp.log2(base) * (-1.0 / 3.0))
    pressure = cells(3, k)[win, :]
    push = 4.0 * pressure
    twice = 2.0 * root
    stress(0, k)[win, :] = twice * xx - push
    stress(1, k)[win, :] = twice * yy - push
    stress(2, k)[win, :] = twice * zz - push
    stress(3, k)[win, :] = root * xy
    stress(4, k)[win, :] = root * xz
    stress(5, k)[win, :] = root * yz
    extra(0, k)[...] = 0.05 * (base * (root * root))
    extra(1, k)[...] = pressure - (0.05 * root) * (xx + yy + zz)


def moved_on(rows, cells, stress, extra, k, slopes, ice, drag):
    win, ahead, behind = window(rows)

    def across(which):
        return stress(which, k)[ahead, :] - stress(which, k)[behind, :]

    def upward(which):
        return stress(which, k + 1)[win, :] - stress(which, k - 1)[win, :]

    def sideways(which):
        return along_y(stress(which, k)[win, :])

    factor = extra(0, k)[...]
    inside = ice[...] > 0.5
    u, v, w = (cells(part, k)[win, :] for part in range(3))
    force_x = across(0) + sideways(3) + upward(4) - slopes[0]
    force_y = across(3) + sideways(1) + upward(5) - slopes[1]
    force_z = across(4) + sideways(5) + upward(2)
    if drag is not None:
        force_x = force_x - drag[...] * u
        force_y = force_y - drag[...] * v
    return (
        jnp.where(inside, u + factor * force_x, 0.0),
        jnp.where(inside, v + factor * force_y, 0.0),
        jnp.where(inside, w + factor * force_z, 0.0),
        jnp.where(inside, extra(1, k)[...], 0.0),
    )


def shared(rows, planes, slopes, marks):
    win, ahead, behind = window(rows)
    lowest = lax.axis_index("gz") == 0
    highest = lax.axis_index("gz") == lax.axis_size("gz") - 1
    slopes[0] = 4.0 * (planes[0, ahead, :] - planes[0, behind, :])
    slopes[1] = 4.0 * along_y(planes[0, win, :])
    kind = planes[2, win, :]
    ice = jnp.where(kind > 0.5, 1.0, 0.0)
    marks[0] = jnp.where(lowest, 0.0, ice)
    marks[1] = ice
    marks[2] = jnp.where(highest, 0.0, ice)
    marks[3] = jnp.where(lowest & (kind > 0.5) & (kind < 1.5), 16.0, 0.0)


def inner(state, planes, stress, extra, fresh, slopes, marks):
    levels, tall, _ = state.shape[1:]
    rows = tall - 2 * MARGIN
    win, _, _ = window(rows)

    def cells(part, k):
        return state.at[part, k - DEEP]

    def stresses(which, k):
        return stress.at[which, k - DEEP - 1]

    def extras(which, k):
        return extra.at[which, k - DEEP - 1]

    shared(rows, planes, slopes, marks)
    for k in range(DEEP + 1, DEEP + levels - 1):
        strain(rows, cells, k, stresses, extras)
    for k in range(DEEP + 2, DEEP + levels - 2):
        for part, value in enumerate(moved_on(rows, cells, stresses, extras, k, slopes, marks.at[1], None)):
            fresh[part, k - DEEP - 2, win, :] = value


def evolve(
    own, planes, weight, stress_in, extra_in, fresh, face_next, edge_next, face_near,
    out, message, beyond, later, stress, extra, slopes, marks,
):
    parts, levels, columns, lanes = out.shape
    rows = columns + 2 * WINDOW
    deep = levels + 2 * DEEP
    win, _, _ = window(rows)
    upward = even("gz")
    lead = MARGIN + WINDOW
    tail = lead + columns

    count = 0
    for index, (part, number) in enumerate(face_planes(parts)):
        lower = 0 if part < parts - 1 else 1
        whole = face_near[rows * index : rows * (index + 1), :]
        beyond[part, number + jnp.where(upward, DEEP, lower), win, :] = whole
        middle = face_next[columns * index : columns * (index + 1), :]
        sides = edge_next[2 * WINDOW * index : 2 * WINDOW * (index + 1), :]
        if part == parts:
            middle, sides = (jnp.where(unpaired("gz"), jnp.inf, each) for each in (middle, sides))
        level = number + jnp.where(upward, lower, DEEP)
        beyond[part, level, lead - WINDOW : lead, :] = sides[:WINDOW, :]
        beyond[part, level, lead:tail, :] = middle
        beyond[part, level, tail : tail + WINDOW, :] = sides[WINDOW:, :]
        count = index + 1
    shared(rows, planes, slopes, marks)

    def before(part, k):
        if DEEP <= k < DEEP + levels:
            return own.at[part, k - DEEP]
        return beyond.at[part, k if k < DEEP else k - levels]

    def between(part, k):
        if part == parts:
            return before(part, k)
        if DEEP + 2 <= k < DEEP + levels - 2:
            return fresh.at[part, k - DEEP - 2]
        return later.at[part, k]

    def is_inner(k):
        return DEEP + 1 <= k < DEEP + levels - 1

    def stress_one(which, k):
        return stress_in.at[which, k - DEEP - 1] if is_inner(k) else stress.at[which, k]

    def extra_one(which, k):
        return extra_in.at[which, k - DEEP - 1] if is_inner(k) else extra.at[which, k]

    def stress_two(which, k):
        return stress.at[which, k]

    def extra_two(which, k):
        return extra.at[which, k]

    for k in range(1, deep - 1):
        if not is_inner(k):
            strain(rows, before, k, stress_one, extra_one)
    for k in range(2, deep - 2):
        if DEEP + 2 <= k < DEEP + levels - 2:
            continue
        ice = marks.at[0 if k < DEEP else 1 if k < DEEP + levels else 2]
        drag = marks.at[3] if k == DEEP else None
        for part, value in enumerate(moved_on(rows, before, stress_one, extra_one, k, slopes, ice, drag)):
            later[part, k, win, :] = value
    for k in range(3, deep - 3):
        strain(rows, between, k, stress_two, extra_two)
    cut = slice(WINDOW, WINDOW + columns)
    sum_u = sum_v = jnp.zeros((rows, lanes), jnp.float32)
    for k in range(DEEP, DEEP + levels):
        drag = marks.at[3] if k == DEEP else None
        values = moved_on(rows, between, stress_two, extra_two, k, slopes, marks.at[1], drag)
        for part, value in enumerate(values):
            out[part, k - DEEP] = value[cut, :]
        sum_u, sum_v = sum_u + values[0], sum_v + values[1]

    half = 0.5 / (levels * lax.axis_size("gz"))
    height = planes[1, win, :]
    slopes[0] = height * sum_u
    flux_y = along_y(height * sum_v)
    flux_x = slopes[0, WINDOW + 1 : WINDOW + columns + 1, :] - slopes[0, WINDOW - 1 : WINDOW + columns - 1, :]
    spread = half * (flux_x + flux_y[cut, :])
    both = weight[...] + face_near[count * rows :, :]
    part_of_both = jnp.where(upward, both[: columns // 2, :], both[columns // 2 :, :])
    for target in range(message.shape[0]):
        message[target, :columns, :] = spread
        message[target, columns:, :] = part_of_both


def store(moved, out, sent):
    copy = pltpu.make_async_copy(moved, out, sent)
    copy.start()
    copy.wait()


def finish(message, density, thickness, smb, other, grown, burden):
    devices = message.shape[0]
    levels, columns, _ = density.shape
    count = other.shape[0] - columns
    place = lax.axis_index("gz")
    spread = message[0, :columns, :]
    for device in range(1, devices):
        spread = spread + message[device, :columns, :]
    over = jnp.where(even("gz"), other[count:, :], 0.0)
    for device in range(2, devices, 2):
        both = jnp.concatenate([message[device, columns:, :], message[device + 1, columns:, :]], axis=0)
        over = over + jnp.where(place < device, both, 0.0)
    new = thickness[...] + 0.5 * (smb[...] - spread)
    grown[...] = new
    scaled = new * (1.0 / (levels * devices))
    for level in range(levels - 1, -1, -1):
        here = density[level]
        burden[level] = scaled * (over + 0.5 * here)
        over = over + here


def pairs_of(axis):
    near = [(i, i ^ 1) for i in range(lax.axis_size(axis))]
    return near, [(i + 1, j + 1) for i, j in near[:-2]]


def body(flow, fluid, density, thickness, bed, smb, mask):
    parts, levels, columns, lanes = flow.shape
    rows = columns + 2 * WINDOW
    deep = levels + 2 * DEEP
    tall = rows + 2 * MARGIN
    near_x, next_x = pairs_of("gx")
    near_z, next_z = pairs_of("gz")

    side = f32(((parts + 1) * levels + 3) * WIDE, lanes)
    faces = (parts + 1) * DEEP - 2
    wide = f32(parts + 1, levels, tall, lanes)
    flat = f32(3, tall, lanes)
    plane = f32(columns, lanes)
    inputs = (flow, fluid, bed, thickness, mask, density)
    to_near, to_next, to_level, state, planes, weight = call(
        prepare,
        (side, side, f32(faces * columns, lanes), wide, flat, plane),
        in_specs=[pl.BlockSpec(memory_space=pltpu.HBM)] * len(inputs),
        scratch=[pltpu.VMEM(each.shape, each.dtype) for each in inputs] + [pltpu.SemaphoreType.DMA((len(inputs),))],
    )(*(pltpu.with_memory_space_constraint(each, pltpu.HBM) for each in inputs))
    next_ = lax.ppermute(to_next, "gx", next_x)
    near = lax.ppermute(to_near, "gx", near_x)
    face_next = lax.ppermute(to_level, "gz", next_z)

    state, planes, to_next, to_near = call(
        widen, (wide, flat, f32(faces * 2 * WINDOW, lanes), f32(faces * rows + columns, lanes))
    )(state, planes, weight, next_, near)
    edge_next = lax.ppermute(to_next, "gz", next_z)
    face_near = lax.ppermute(to_near, "gz", near_z)

    stress, extra, fresh = call(
        inner,
        (f32(6, levels - 2, tall, lanes), f32(2, levels - 2, rows, lanes), f32(parts, levels - 4, tall, lanes)),
        scratch=[pltpu.VMEM((2, rows, lanes), jnp.float32), pltpu.VMEM((4, rows, lanes), jnp.float32)],
        cost_estimate=pl.CostEstimate(flops=INNER_COST, bytes_accessed=INNER_COST, transcendentals=0),
    )(state, planes)

    message = f32(lax.axis_size("gz"), columns + columns // 2, lanes)
    moved, message = call(
        evolve,
        (f32(*flow.shape), message),
        scratch=[
            pltpu.VMEM((parts + 1, 2 * DEEP, tall, lanes), jnp.float32),
            pltpu.VMEM((parts, deep, tall, lanes), jnp.float32),
            pltpu.VMEM((6, deep, tall, lanes), jnp.float32),
            pltpu.VMEM((2, deep, rows, lanes), jnp.float32),
            pltpu.VMEM((2, rows, lanes), jnp.float32),
            pltpu.VMEM((4, rows, lanes), jnp.float32),
        ],
    )(state, planes, weight, stress, extra, fresh, face_next, edge_next, face_near)
    message = lax.all_to_all(message, "gz", split_axis=0, concat_axis=0, tiled=True)
    moved = call(
        store,
        f32(*flow.shape),
        out_specs=pl.BlockSpec(memory_space=pltpu.HBM),
        scratch=[pltpu.SemaphoreType.DMA],
        cost_estimate=pl.CostEstimate(flops=0, bytes_accessed=STORE_COST, transcendentals=0),
    )(moved)
    grown, burden = call(finish, (plane, f32(*density.shape)))(message, density, thickness, smb, face_near)
    return moved, grown, burden


def solution(mesh):
    level_split = P("gz", "gx", None)
    flat = P("gx", None)
    return jax.shard_map(
        body,
        mesh=mesh,
        in_specs=(P(None, "gz", "gx", None), level_split, level_split, flat, flat, flat, flat),
        out_specs=(P(None, "gz", "gx", None), flat, level_split),
        check_vma=False,
    )
```

time: 36.5 us -> 35.1 us (0.962)
  the two profiles are of different devices: /device:TPU:464 before, /device:TPU:448 now
where the time goes in v4:
time: 35.1 us; the launch traced here: 34.8 us
  starting transfers between devices  17.5 us (50%)
  waiting for transfers between devices  10.8 us (31%)
  Pallas kernels  5.68 us (16%)
  between operations  0.72 us (2%)
    all_to_all x1, waiting for transfers between devices, body(): lax.all_to_all(message, 'gz', split_axis=0, concat_axis=0, tiled=True)  6.03 us
    ppermute x1, starting transfers between devices, body(): next_ = lax.ppermute(to_next, 'gx', next_x)  5.37 us
    ppermute x1, starting transfers between devices, body(): face_near = lax.ppermute(to_near, 'gz', near_z)  4.76 us
    all_to_all x1, starting transfers between devices, body(): lax.all_to_all(message, 'gz', split_axis=0, concat_axis=0, tiled=True)  4.15 us
    ppermute x1, waiting for transfers between devices, body(): near = lax.ppermute(to_near, 'gx', near_x)  3.21 us
    pallas_call x1, Pallas kernels, body(): call(evolve, (f32(*flow.shape), message), scratch=[pltpu.VMEM((parts + 1,...  2.2 us
    ppermute x1, starting transfers between devices, body(): near = lax.ppermute(to_near, 'gx', near_x)  1.92 us
    pallas_call x1, Pallas kernels, body(): call(prepare, (side, side, f32(faces * columns, lanes), wide, flat, plane...  1.31 us
  transfers between devices with their start and end apart: 6, of which 4 were waited for; matrix products, arithmetic and copies ran while one was open for 0% of the time, Pallas kernels for 4%

profile of v4, /device:TPU:448, one launch (start us, length us, event | category | flops | bytes accessed | tf_op | source)
XLA Modules:
  0.0 34.8 jit_solution(16880154330422973334)
XLA Ops:
  0.6 1.3 %shard_map.94 = (f32[215,128]{1,0:T(8,128)S(1)}, f32[215,128]{1,0:T(8,128)S(1)}, f32[576,128]{1,0:T(8,128)S(1)}, f32[5,8,56,128]{3,2,1,0:T(8,128)S(1)}, f32[3,56...) custom-call(f32[4,8,32,128]{3,2,1,0:T(8,128)} %flow_far.1, f32[8,32,128]{2,1,0:T(8,128)} %fluid_far.1, f32[32,128]{1,0:T(8,128)} %bed_far.1, ...), custom_call_target="tpu_custom_call" | custom-call | tf_op jit(solution)/shard_map/pallas_call | solution.py:382
  1.9 5.4 %collective-permute-start = (f32[215,128]{1,0:T(8,128)S(1)}, f32[215,128]{1,0:T(8,128)S(1)}, u32[]{:S(2)}, u32[]{:S(2)}) collective-permute-start(f32[215,128]{1,0:T(8,128)S(1)} %get-tuple-element.23), channel_id=1, source_target_pairs={{8,16},{16,8},{24,32},{32,24},{40,48},{48,40},{56,64},{64,56},{72,... | collective-permute-start | bytes 330248 | tf_op jit(solution)/shard_map/ppermute | solution.py:388
  7.3 1.9 %collective-permute-start.1 = (f32[215,128]{1,0:T(8,128)S(1)}, f32[215,128]{1,0:T(8,128)S(1)}, u32[]{:S(2)}, u32[]{:S(2)}) collective-permute-start(f32[215,128]{1,0:T(8,128)S(1)} %get-tuple-element.24), channel_id=1, source_target_pairs={{0,8},{8,0},{16,24},{24,16},{32,40},{40,32},{48,56},{56,48},{64,72... | collective-permute-start | bytes 330248 | tf_op jit(solution)/shard_map/ppermute | solution.py:389
  9.2 0.7 %collective-permute-start.2 = (f32[576,128]{1,0:T(8,128)S(1)}, f32[576,128]{1,0:T(8,128)S(1)}, u32[]{:S(2)}, u32[]{:S(2)}) collective-permute-start(f32[576,128]{1,0:T(8,128)S(1)} %get-tuple-element.30), channel_id=1, source_target_pairs={{1,2},{2,1},{3,4},{4,3},{5,6},{6,5},{9,10},{10,9},{11,12},{12,11},... | collective-permute-start | bytes 884744 | tf_op jit(solution)/shard_map/ppermute | solution.py:390
  9.9 0.8 %collective-permute-done.next_ = f32[215,128]{1,0:T(8,128)S(1)} collective-permute-done((f32[215,128]{1,0:T(8,128)S(1)}, f32[215,128]{1,0:T(8,128)S(1)}, u32[]{:S(2)}, u32[]{:S(2)}) %collective-permute-start) | collective-permute-done | bytes 110112 | tf_op jit(solution)/shard_map/ppermute | solution.py:388
  10.7 3.2 %collective-permute-done.1.near = f32[215,128]{1,0:T(8,128)S(1)} collective-permute-done((f32[215,128]{1,0:T(8,128)S(1)}, f32[215,128]{1,0:T(8,128)S(1)}, u32[]{:S(2)}, u32[]{:S(2)}) %collective-permute-start.1) | collective-permute-done | bytes 110112 | tf_op jit(solution)/shard_map/ppermute | solution.py:389
  14.0 0.2 shard_map.95
  14.1 0.7 %collective-permute-start.3 = (f32[144,128]{1,0:T(8,128)S(1)}, f32[144,128]{1,0:T(8,128)S(1)}, u32[]{:S(2)}, u32[]{:S(2)}) collective-permute-start(f32[144,128]{1,0:T(8,128)S(1)} %get-tuple-element.31), channel_id=1, source_target_pairs={{1,2},{2,1},{3,4},{4,3},{5,6},{6,5},{9,10},{10,9},{11,12},{12,11},... | collective-permute-start | bytes 221192 | tf_op jit(solution)/shard_map/ppermute | solution.py:395
  14.8 4.8 %collective-permute-start.4 = (f32[752,128]{1,0:T(8,128)S(1)}, f32[752,128]{1,0:T(8,128)S(1)}, u32[]{:S(2)}, u32[]{:S(2)}) collective-permute-start(f32[752,128]{1,0:T(8,128)S(1)} %get-tuple-element.32), channel_id=1, source_target_pairs={{0,1},{1,0},{2,3},{3,2},{4,5},{5,4},{6,7},{7,6},{8,9},{9,8},{10,11... | collective-permute-start | bytes 1155080 | tf_op jit(solution)/shard_map/ppermute | solution.py:396
  19.6 0.5 %shard_map.96 = (f32[6,6,56,128]{3,2,1,0:T(8,128)S(1)}, f32[2,6,40,128]{3,2,1,0:T(8,128)S(1)}, f32[4,4,56,128]{3,2,1,0:T(8,128)S(1)}) custom-call(f32[5,8,56,128]{3,2,1,0:T(8,128)S(1)} %get-tuple-element.25.state.own, f32[3,56,128]{2,1,0:T(8,128)S(1)} %get-tuple-element.26.planes), custom_call_target="tpu_custom_call" | custom-call | flops 5000000000 | bytes 5000000000 | tf_op jit(solution)/shard_map/pallas_call | solution.py:398
  20.1 0.0 collective-permute-done.3.edge_next
  20.1 0.0 collective-permute-done.2.face_next
  20.1 0.8 %collective-permute-done.4.face_near.other = f32[752,128]{1,0:T(8,128)S(1)} collective-permute-done((f32[752,128]{1,0:T(8,128)S(1)}, f32[752,128]{1,0:T(8,128)S(1)}, u32[]{:S(2)}, u32[]{:S(2)}) %collective-permute-start.4) | collective-permute-done | bytes 385056 | tf_op jit(solution)/shard_map/ppermute | solution.py:396
  20.9 2.2 %shard_map.97 = (f32[4,8,32,128]{3,2,1,0:T(8,128)S(1)}, f32[8,48,128]{2,1,0:T(8,128)}) custom-call(f32[5,8,56,128]{3,2,1,0:T(8,128)S(1)} %get-tuple-element.25.state.own, f32[3,56,128]{2,1,0:T(8,128)S(1)} %get-tuple-element.26.planes, f32[32,128]{1,0:T(8,128)S(1)} %get-tuple-element.22.weight, f32[6,6,56,128]{3,2,1,0:T(8,128)S(1)} %get-tuple-element.27.stress_in, ...), custom_call_target="tpu_custom_call" | custom-call | tf_op jit(solution)/shard_map/pallas_call | solution.py:406
  23.1 0.0 copy-start
  23.1 0.0 copy-start.1
  23.1 0.0 copy-start.2
  23.1 4.2 %all-to-all-start = ((f32[8,48,128]{2,1,0:T(8,128)}), f32[8,48,128]{2,1,0:T(8,128)S(1)}, u32[]{:S(2)}, u32[]{:S(2)}) async-start(f32[8,48,128]{2,1,0:T(8,128)} %get-tuple-element.34), calls=%async_computation | async-start | bytes 393216 | tf_op jit(solution)/shard_map/all_to_all | solution.py:418
  27.2 0.8 %shard_map.98 = f32[4,8,32,128]{3,2,1,0:T(8,128)} custom-call(f32[4,8,32,128]{3,2,1,0:T(8,128)S(1)} %get-tuple-element.33.moved), custom_call_target="tpu_custom_call" | custom-call | bytes 5000000 | tf_op jit(solution)/shard_map/pallas_call | solution.py:419
  28.1 6.0 %all-to-all-done.message = f32[8,48,128]{2,1,0:T(8,128)S(1)} async-done(((f32[8,48,128]{2,1,0:T(8,128)}), f32[8,48,128]{2,1,0:T(8,128)S(1)}, u32[]{:S(2)}, u32[]{:S(2)}) %all-to-all-start) | async-done | bytes 196640 | tf_op jit(solution)/shard_map/all_to_all | solution.py:418
  34.1 0.0 copy-done
  34.1 0.0 copy-done.1
  34.1 0.0 copy-done.2
  34.1 0.7 %shard_map.99 = (f32[32,128]{1,0:T(8,128)}, f32[8,32,128]{2,1,0:T(8,128)}) custom-call(f32[8,48,128]{2,1,0:T(8,128)S(1)} %all-to-all-done.message, f32[8,32,128]{2,1,0:T(8,128)S(1)} %copy-done, f32[32,128]{1,0:T(8,128)S(1)} %copy-done.1, f32[32,128]{1,0:T(8,128)S(1)} %copy-done.2, f32[752,128]{1,0:T(8,128)S(1)} %collective-permute-done.4.face_near.other), custom_call_target="tpu_custom_call" | custom-call | tf_op jit(solution)/shard_map/pallas_call | solution.py:426
Async XLA Ops:
  1.9 8.8 %collective-permute-start = (f32[215,128]{1,0:T(8,128)S(1)}, f32[215,128]{1,0:T(8,128)S(1)}, u32[]{:S(2)}, u32[]{:S(2)}) collective-permute-start(f32[215,128]{1,0:T(8,128)S(1)} %get-tuple-element.23), channel_id=1, source_target_pairs={{8,16},{16,8},{24,32},{32,24},{40,48},{48,40},{56,64},{64,56},{72,... | collective-permute-start | bytes 330248 | tf_op jit(solution)/shard_map/ppermute | solution.py:388
  7.3 6.6 %collective-permute-start.1 = (f32[215,128]{1,0:T(8,128)S(1)}, f32[215,128]{1,0:T(8,128)S(1)}, u32[]{:S(2)}, u32[]{:S(2)}) collective-permute-start(f32[215,128]{1,0:T(8,128)S(1)} %get-tuple-element.24), channel_id=1, source_target_pairs={{0,8},{8,0},{16,24},{24,16},{32,40},{40,32},{48,56},{56,48},{64,72... | collective-permute-start | bytes 330248 | tf_op jit(solution)/shard_map/ppermute | solution.py:389
  9.2 10.8 %collective-permute-start.2 = (f32[576,128]{1,0:T(8,128)S(1)}, f32[576,128]{1,0:T(8,128)S(1)}, u32[]{:S(2)}, u32[]{:S(2)}) collective-permute-start(f32[576,128]{1,0:T(8,128)S(1)} %get-tuple-element.30), channel_id=1, source_target_pairs={{1,2},{2,1},{3,4},{4,3},{5,6},{6,5},{9,10},{10,9},{11,12},{12,11},... | collective-permute-start | bytes 884744 | tf_op jit(solution)/shard_map/ppermute | solution.py:390
  14.1 6.0 %collective-permute-start.3 = (f32[144,128]{1,0:T(8,128)S(1)}, f32[144,128]{1,0:T(8,128)S(1)}, u32[]{:S(2)}, u32[]{:S(2)}) collective-permute-start(f32[144,128]{1,0:T(8,128)S(1)} %get-tuple-element.31), channel_id=1, source_target_pairs={{1,2},{2,1},{3,4},{4,3},{5,6},{6,5},{9,10},{10,9},{11,12},{12,11},... | collective-permute-start | bytes 221192 | tf_op jit(solution)/shard_map/ppermute | solution.py:395
  14.8 6.1 %collective-permute-start.4 = (f32[752,128]{1,0:T(8,128)S(1)}, f32[752,128]{1,0:T(8,128)S(1)}, u32[]{:S(2)}, u32[]{:S(2)}) collective-permute-start(f32[752,128]{1,0:T(8,128)S(1)} %get-tuple-element.32), channel_id=1, source_target_pairs={{0,1},{1,0},{2,3},{3,2},{4,5},{5,4},{6,7},{7,6},{8,9},{9,8},{10,11... | collective-permute-start | bytes 1155080 | tf_op jit(solution)/shard_map/ppermute | solution.py:396
  23.1 11.0 %copy-start = (f32[8,32,128]{2,1,0:T(8,128)S(1)}, f32[8,32,128]{2,1,0:T(8,128)}, u32[]{:S(2)}) copy-start(f32[8,32,128]{2,1,0:T(8,128)} %density.1) | copy-start | bytes 393220
  23.1 11.0 %copy-start.1 = (f32[32,128]{1,0:T(8,128)S(1)}, f32[32,128]{1,0:T(8,128)}, u32[]{:S(2)}) copy-start(f32[32,128]{1,0:T(8,128)} %thickness.1) | copy-start | bytes 49156
  23.1 11.0 %copy-start.2 = (f32[32,128]{1,0:T(8,128)S(1)}, f32[32,128]{1,0:T(8,128)}, u32[]{:S(2)}) copy-start(f32[32,128]{1,0:T(8,128)} %smb.1) | copy-start | bytes 49156
  23.1 11.0 %all-to-all-start = ((f32[8,48,128]{2,1,0:T(8,128)}), f32[8,48,128]{2,1,0:T(8,128)S(1)}, u32[]{:S(2)}, u32[]{:S(2)}) async-start(f32[8,48,128]{2,1,0:T(8,128)} %get-tuple-element.34), calls=%async_computation | async-start | bytes 393216 | tf_op jit(solution)/shard_map/all_to_all | solution.py:418

commit v5 on v4

--- a/solution.py
+++ b/solution.py
@@ -10,10 +10,10 @@
 DEEP = 4
 WIDE = 5
 WINDOW = 4
+FLAT = (4, 1, 3)
 MARGIN = 8
 VMEM_LIMIT = 24 * 1024 * 1024
 INNER_COST = 5_000_000_000
-STORE_COST = 5_000_000
 
 
 def call(kernel, outs, scratch=(), **specs):
@@ -28,6 +28,18 @@
 
 def f32(*shape):
     return jax.ShapeDtypeStruct(shape, jnp.float32)
+
+
+def side_planes(parts, levels):
+    place = 0
+    for part in range(parts + 1):
+        for level in range(levels):
+            width = WIDE if part < parts - 1 else WINDOW
+            yield part, level, width, place
+            place += width
+    for number, width in enumerate(FLAT):
+        yield parts + 1, number, width, place
+        place += width
 
 
 def even(axis):
@@ -59,19 +71,11 @@
     upward = even("gx")
     height = thickness[...]
     flat = (bed[...] + height, height, mask[...].astype(jnp.float32))
-    place = 0
-
-    def put(low, high):
-        to_near[place : place + WIDE, :] = jnp.where(upward, high, low)
-        to_next[place : place + WIDE, :] = jnp.where(upward, low, high)
-        return place + WIDE
-
-    for part in range(parts + 1):
-        for level in range(levels):
-            plane = flow.at[part, level] if part < parts else fluid.at[level]
-            place = put(plane[:WIDE, :], plane[columns - WIDE :, :])
-    for plane in flat:
-        place = put(plane[:WIDE, :], plane[columns - WIDE :, :])
+    for part, level, width, place in side_planes(parts, levels):
+        plane = flow.at[part, level] if part < parts else fluid.at[level] if part == parts else flat[level]
+        low, high = plane[:width, :], plane[columns - width :, :]
+        to_near[place : place + width, :] = jnp.where(upward, high, low)
+        to_next[place : place + width, :] = jnp.where(upward, low, high)
     above = even("gz")
     for index, (part, number) in enumerate(face_planes(parts)):
         low, high = (start + number for start in face_starts(part, parts, levels))
@@ -93,9 +97,9 @@
     return (place == 0) | (place == lax.axis_size(axis) - 1)
 
 
-def beside(near, next_, place, fluid_plane):
-    inner = near[place : place + WIDE, :]
-    beyond = next_[place : place + WIDE, :]
+def beside(near, next_, place, width, fluid_plane):
+    inner = near[place : place + width, :]
+    beyond = next_[place : place + width, :]
     if fluid_plane:
         beyond = jnp.where(unpaired("gx"), jnp.inf, beyond)
     return jnp.where(even("gx"), beyond, inner), jnp.where(even("gx"), inner, beyond)
@@ -108,17 +112,13 @@
     lead = MARGIN + WINDOW
     tail = MARGIN + rows - WINDOW
     upward = even("gz")
-    for part in range(parts + 1):
-        for level in range(levels):
-            before, after = beside(near, next_, (part * levels + level) * WIDE, part == parts)
-            state[part, level, :, :] = state_in[part, level]
-            state[part, level, lead - WIDE : lead, :] = before
-            state[part, level, tail : tail + WIDE, :] = after
-    for number in range(planes.shape[0]):
-        before, after = beside(near, next_, ((parts + 1) * levels + number) * WIDE, False)
-        planes[number, :, :] = planes_in[number]
-        planes[number, lead - WIDE : lead, :] = before
-        planes[number, tail : tail + WIDE, :] = after
+    for part, level, width, place in side_planes(parts, levels):
+        before, after = beside(near, next_, place, width, part == parts)
+        source, target = (state_in, state) if part <= parts else (planes_in, planes)
+        spot = (part, level) if part <= parts else (level,)
+        target[spot] = source[spot]
+        target[(*spot, slice(lead - width, lead), slice(None))] = before
+        target[(*spot, slice(tail, tail + width), slice(None))] = after
     count = 0
     for index, (part, number) in enumerate(face_planes(parts)):
         low, high = (start + number for start in face_starts(part, parts, levels))
@@ -333,13 +333,12 @@
         message[target, columns:, :] = part_of_both
 
 
-def store(moved, out, sent):
-    copy = pltpu.make_async_copy(moved, out, sent)
-    copy.start()
-    copy.wait()
-
-
-def finish(message, density, thickness, smb, other, grown, burden):
+def finish(message, density, thickness, smb, other, moved, far_moved, far_grown, far_burden, grown, burden, sent):
+    copies = [
+        pltpu.make_async_copy(a, b, sent.at[i])
+        for i, (a, b) in enumerate(((moved, far_moved), (grown, far_grown), (burden, far_burden)))
+    ]
+    copies[0].start()
     devices = message.shape[0]
     levels, columns, _ = density.shape
     count = other.shape[0] - columns
@@ -353,11 +352,15 @@
         over = over + jnp.where(place < device, both, 0.0)
     new = thickness[...] + 0.5 * (smb[...] - spread)
     grown[...] = new
+    copies[1].start()
     scaled = new * (1.0 / (levels * devices))
     for level in range(levels - 1, -1, -1):
         here = density[level]
         burden[level] = scaled * (over + 0.5 * here)
         over = over + here
+    copies[2].start()
+    for copy in copies:
+        copy.wait()
 
 
 def pairs_of(axis):
@@ -373,7 +376,8 @@
     near_x, next_x = pairs_of("gx")
     near_z, next_z = pairs_of("gz")
 
-    side = f32(((parts + 1) * levels + 3) * WIDE, lanes)
+    *_, (_, _, width, place) = side_planes(parts, levels)
+    side = f32(place + width, lanes)
     faces = (parts + 1) * DEEP - 2
     wide = f32(parts + 1, levels, tall, lanes)
     flat = f32(3, tall, lanes)
@@ -416,14 +420,17 @@
         ],
     )(state, planes, weight, stress, extra, fresh, face_next, edge_next, face_near)
     message = lax.all_to_all(message, "gz", split_axis=0, concat_axis=0, tiled=True)
-    moved = call(
-        store,
-        f32(*flow.shape),
-        out_specs=pl.BlockSpec(memory_space=pltpu.HBM),
-        scratch=[pltpu.SemaphoreType.DMA],
-        cost_estimate=pl.CostEstimate(flops=0, bytes_accessed=STORE_COST, transcendentals=0),
-    )(moved)
-    grown, burden = call(finish, (plane, f32(*density.shape)))(message, density, thickness, smb, face_near)
+    deep_plane = f32(*density.shape)
+    moved, grown, burden = call(
+        finish,
+        (f32(*flow.shape), plane, deep_plane),
+        out_specs=[pl.BlockSpec(memory_space=pltpu.HBM)] * 3,
+        scratch=[
+            pltpu.VMEM(plane.shape, jnp.float32),
+            pltpu.VMEM(deep_plane.shape, jnp.float32),
+            pltpu.SemaphoreType.DMA((3,)),
+        ],
+    )(message, density, thickness, smb, face_near, moved)
     return moved, grown, burden
 
 

time: 35.1 us -> 34.1 us (0.972)
  blocking collectives: 0 us -> 10.7 us
  waiting for transfers between devices: 10.8 us -> 4.69 us
  starting transfers between devices: 17.5 us -> 13.4 us
  Pallas kernels: 5.68 us -> 4.35 us
    all_to_all x0 -> x1, blocking collectives: none -> 10.7 us  [body(): lax.all_to_all(message, 'gz', split_axis=0, concat_axis=0, tiled=True)]
    all_to_all x1 -> x0, waiting for transfers between devices: 6.03 us -> none  [body(): lax.all_to_all(message, 'gz', split_axis=0, concat_axis=0, tiled=True)]
    all_to_all x1 -> x0, starting transfers between devices: 4.15 us -> none  [body(): lax.all_to_all(message, 'gz', split_axis=0, concat_axis=0, tiled=True)]
    pallas_call x1, Pallas kernels: 2.2 us -> 1.52 us  [body(): call(evolve, (f32(*flow.shape), message), scratch=[pltpu.VMEM((parts + 1,...]
    pallas_call x2 -> x1, Pallas kernels: 1.49 us -> 0.86 us  [body(): call(finish, (f32(*flow.shape), plane, deep_plane), out_specs=[pl.BlockSp...]
  transfers between devices with their start and end apart: 6 -> 5, of which waited for: 4 -> 3; matrix products, arithmetic and copies ran while one was open for 0% -> 0% of each run, Pallas kernels for 4% -> 2%
where the time goes in v5:
time: 34.1 us; the launch traced here: 33.8 us
  starting transfers between devices  13.4 us (39%)
  blocking collectives  10.7 us (31%)
  waiting for transfers between devices  4.69 us (14%)
  Pallas kernels  4.35 us (13%)
  between operations  0.72 us (2%)
    all_to_all x1, blocking collectives, body(): lax.all_to_all(message, 'gz', split_axis=0, concat_axis=0, tiled=True)  10.7 us
    ppermute x1, starting transfers between devices, body(): next_ = lax.ppermute(to_next, 'gx', next_x)  5.37 us
    ppermute x1, starting transfers between devices, body(): face_near = lax.ppermute(to_near, 'gz', near_z)  4.76 us
    ppermute x1, waiting for transfers between devices, body(): near = lax.ppermute(to_near, 'gx', near_x)  3.26 us
    ppermute x1, starting transfers between devices, body(): near = lax.ppermute(to_near, 'gx', near_x)  1.92 us
    pallas_call x1, Pallas kernels, body(): call(evolve, (f32(*flow.shape), message), scratch=[pltpu.VMEM((parts + 1,...  1.52 us
    pallas_call x1, Pallas kernels, body(): call(prepare, (side, side, f32(faces * columns, lanes), wide, flat, plane...  1.31 us
    pallas_call x1, Pallas kernels, body(): call(finish, (f32(*flow.shape), plane, deep_plane), out_specs=[pl.BlockSp...  0.86 us
  transfers between devices with their start and end apart: 5, of which 3 were waited for; matrix products, arithmetic and copies ran while one was open for 0% of the time, Pallas kernels for 2%

profile of v5, /device:TPU:448, one launch (start us, length us, event | category | flops | bytes accessed | tf_op | source)
XLA Modules:
  0.0 33.8 jit_solution(2801373001366119023)
XLA Ops:
  0.6 1.3 %shard_map.94 = (f32[192,128]{1,0:T(8,128)S(1)}, f32[192,128]{1,0:T(8,128)S(1)}, f32[576,128]{1,0:T(8,128)S(1)}, f32[5,8,56,128]{3,2,1,0:T(8,128)S(1)}, f32[3,56...) custom-call(f32[4,8,32,128]{3,2,1,0:T(8,128)} %flow_far.1, f32[8,32,128]{2,1,0:T(8,128)} %fluid_far.1, f32[32,128]{1,0:T(8,128)} %bed_far.1, ...), custom_call_target="tpu_custom_call" | custom-call | tf_op jit(solution)/shard_map/pallas_call | solution.py:386
  1.9 5.4 %collective-permute-start = (f32[192,128]{1,0:T(8,128)S(1)}, f32[192,128]{1,0:T(8,128)S(1)}, u32[]{:S(2)}, u32[]{:S(2)}) collective-permute-start(f32[192,128]{1,0:T(8,128)S(1)} %get-tuple-element.21), channel_id=1, source_target_pairs={{8,16},{16,8},{24,32},{32,24},{40,48},{48,40},{56,64},{64,56},{72,... | collective-permute-start | bytes 294920 | tf_op jit(solution)/shard_map/ppermute | solution.py:392
  7.3 1.9 %collective-permute-start.1 = (f32[192,128]{1,0:T(8,128)S(1)}, f32[192,128]{1,0:T(8,128)S(1)}, u32[]{:S(2)}, u32[]{:S(2)}) collective-permute-start(f32[192,128]{1,0:T(8,128)S(1)} %get-tuple-element.22), channel_id=1, source_target_pairs={{0,8},{8,0},{16,24},{24,16},{32,40},{40,32},{48,56},{56,48},{64,72... | collective-permute-start | bytes 294920 | tf_op jit(solution)/shard_map/ppermute | solution.py:393
  9.2 0.7 %collective-permute-start.2 = (f32[576,128]{1,0:T(8,128)S(1)}, f32[576,128]{1,0:T(8,128)S(1)}, u32[]{:S(2)}, u32[]{:S(2)}) collective-permute-start(f32[576,128]{1,0:T(8,128)S(1)} %get-tuple-element.28), channel_id=1, source_target_pairs={{1,2},{2,1},{3,4},{4,3},{5,6},{6,5},{9,10},{10,9},{11,12},{12,11},... | collective-permute-start | bytes 884744 | tf_op jit(solution)/shard_map/ppermute | solution.py:394
  9.9 0.6 %collective-permute-done.next_ = f32[192,128]{1,0:T(8,128)S(1)} collective-permute-done((f32[192,128]{1,0:T(8,128)S(1)}, f32[192,128]{1,0:T(8,128)S(1)}, u32[]{:S(2)}, u32[]{:S(2)}) %collective-permute-start) | collective-permute-done | bytes 98336 | tf_op jit(solution)/shard_map/ppermute | solution.py:392
  10.6 3.3 %collective-permute-done.1.near = f32[192,128]{1,0:T(8,128)S(1)} collective-permute-done((f32[192,128]{1,0:T(8,128)S(1)}, f32[192,128]{1,0:T(8,128)S(1)}, u32[]{:S(2)}, u32[]{:S(2)}) %collective-permute-start.1) | collective-permute-done | bytes 98336 | tf_op jit(solution)/shard_map/ppermute | solution.py:393
  13.8 0.2 shard_map.95
  14.0 0.7 %collective-permute-start.3 = (f32[144,128]{1,0:T(8,128)S(1)}, f32[144,128]{1,0:T(8,128)S(1)}, u32[]{:S(2)}, u32[]{:S(2)}) collective-permute-start(f32[144,128]{1,0:T(8,128)S(1)} %get-tuple-element.29), channel_id=1, source_target_pairs={{1,2},{2,1},{3,4},{4,3},{5,6},{6,5},{9,10},{10,9},{11,12},{12,11},... | collective-permute-start | bytes 221192 | tf_op jit(solution)/shard_map/ppermute | solution.py:399
  14.7 4.8 %collective-permute-start.4 = (f32[752,128]{1,0:T(8,128)S(1)}, f32[752,128]{1,0:T(8,128)S(1)}, u32[]{:S(2)}, u32[]{:S(2)}) collective-permute-start(f32[752,128]{1,0:T(8,128)S(1)} %get-tuple-element.30), channel_id=1, source_target_pairs={{0,1},{1,0},{2,3},{3,2},{4,5},{5,4},{6,7},{7,6},{8,9},{9,8},{10,11... | collective-permute-start | bytes 1155080 | tf_op jit(solution)/shard_map/ppermute | solution.py:400
  19.4 0.5 %shard_map.96 = (f32[6,6,56,128]{3,2,1,0:T(8,128)S(1)}, f32[2,6,40,128]{3,2,1,0:T(8,128)S(1)}, f32[4,4,56,128]{3,2,1,0:T(8,128)S(1)}) custom-call(f32[5,8,56,128]{3,2,1,0:T(8,128)S(1)} %get-tuple-element.23.state.own, f32[3,56,128]{2,1,0:T(8,128)S(1)} %get-tuple-element.24.planes), custom_call_target="tpu_custom_call" | custom-call | flops 5000000000 | bytes 5000000000 | tf_op jit(solution)/shard_map/pallas_call | solution.py:402
  19.9 0.0 collective-permute-done.3.edge_next
  19.9 0.0 collective-permute-done.2.face_next
  20.0 0.8 %collective-permute-done.4.face_near.other = f32[752,128]{1,0:T(8,128)S(1)} collective-permute-done((f32[752,128]{1,0:T(8,128)S(1)}, f32[752,128]{1,0:T(8,128)S(1)}, u32[]{:S(2)}, u32[]{:S(2)}) %collective-permute-start.4) | collective-permute-done | bytes 385056 | tf_op jit(solution)/shard_map/ppermute | solution.py:400
  20.7 0.0 copy-start
  20.7 0.0 copy-start.1
  20.7 0.0 copy-start.2
  20.8 1.5 %shard_map.97 = (f32[4,8,32,128]{3,2,1,0:T(8,128)S(1)}, f32[8,48,128]{2,1,0:T(8,128)S(1)}) custom-call(f32[5,8,56,128]{3,2,1,0:T(8,128)S(1)} %get-tuple-element.23.state.own, f32[3,56,128]{2,1,0:T(8,128)S(1)} %get-tuple-element.24.planes, f32[32,128]{1,0:T(8,128)S(1)} %get-tuple-element.20.weight, f32[6,6,56,128]{3,2,1,0:T(8,128)S(1)} %get-tuple-element.25.stress_in, ...), custom_call_target="tpu_custom_call" | custom-call | tf_op jit(solution)/shard_map/pallas_call | solution.py:410
  22.3 10.7 %all_to_all.5.message = f32[8,48,128]{2,1,0:T(8,128)S(1)} all-to-all(f32[8,48,128]{2,1,0:T(8,128)S(1)} %get-tuple-element.31), channel_id=1, replica_groups=mesh['gx'=64,'gz'=8] {'gz'}, dimensions={0} | all-to-all | bytes 393216 | tf_op jit(solution)/shard_map/all_to_all | solution.py:422
  32.9 0.0 copy-done
  32.9 0.0 copy-done.1
  32.9 0.0 copy-done.2
  32.9 0.9 %shard_map.98 = (f32[4,8,32,128]{3,2,1,0:T(8,128)}, f32[32,128]{1,0:T(8,128)}, f32[8,32,128]{2,1,0:T(8,128)}) custom-call(f32[8,48,128]{2,1,0:T(8,128)S(1)} %all_to_all.5.message, f32[8,32,128]{2,1,0:T(8,128)S(1)} %copy-done, f32[32,128]{1,0:T(8,128)S(1)} %copy-done.1, f32[32,128]{1,0:T(8,128)S(1)} %copy-done.2, ...), custom_call_target="tpu_custom_call" | custom-call | tf_op jit(solution)/shard_map/pallas_call | solution.py:424
Async XLA Ops:
  1.9 8.6 %collective-permute-start = (f32[192,128]{1,0:T(8,128)S(1)}, f32[192,128]{1,0:T(8,128)S(1)}, u32[]{:S(2)}, u32[]{:S(2)}) collective-permute-start(f32[192,128]{1,0:T(8,128)S(1)} %get-tuple-element.21), channel_id=1, source_target_pairs={{8,16},{16,8},{24,32},{32,24},{40,48},{48,40},{56,64},{64,56},{72,... | collective-permute-start | bytes 294920 | tf_op jit(solution)/shard_map/ppermute | solution.py:392
  7.3 6.5 %collective-permute-start.1 = (f32[192,128]{1,0:T(8,128)S(1)}, f32[192,128]{1,0:T(8,128)S(1)}, u32[]{:S(2)}, u32[]{:S(2)}) collective-permute-start(f32[192,128]{1,0:T(8,128)S(1)} %get-tuple-element.22), channel_id=1, source_target_pairs={{0,8},{8,0},{16,24},{24,16},{32,40},{40,32},{48,56},{56,48},{64,72... | collective-permute-start | bytes 294920 | tf_op jit(solution)/shard_map/ppermute | solution.py:393
  9.2 10.7 %collective-permute-start.2 = (f32[576,128]{1,0:T(8,128)S(1)}, f32[576,128]{1,0:T(8,128)S(1)}, u32[]{:S(2)}, u32[]{:S(2)}) collective-permute-start(f32[576,128]{1,0:T(8,128)S(1)} %get-tuple-element.28), channel_id=1, source_target_pairs={{1,2},{2,1},{3,4},{4,3},{5,6},{6,5},{9,10},{10,9},{11,12},{12,11},... | collective-permute-start | bytes 884744 | tf_op jit(solution)/shard_map/ppermute | solution.py:394
  14.0 5.9 %collective-permute-start.3 = (f32[144,128]{1,0:T(8,128)S(1)}, f32[144,128]{1,0:T(8,128)S(1)}, u32[]{:S(2)}, u32[]{:S(2)}) collective-permute-start(f32[144,128]{1,0:T(8,128)S(1)} %get-tuple-element.29), channel_id=1, source_target_pairs={{1,2},{2,1},{3,4},{4,3},{5,6},{6,5},{9,10},{10,9},{11,12},{12,11},... | collective-permute-start | bytes 221192 | tf_op jit(solution)/shard_map/ppermute | solution.py:399
  14.7 6.1 %collective-permute-start.4 = (f32[752,128]{1,0:T(8,128)S(1)}, f32[752,128]{1,0:T(8,128)S(1)}, u32[]{:S(2)}, u32[]{:S(2)}) collective-permute-start(f32[752,128]{1,0:T(8,128)S(1)} %get-tuple-element.30), channel_id=1, source_target_pairs={{0,1},{1,0},{2,3},{3,2},{4,5},{5,4},{6,7},{7,6},{8,9},{9,8},{10,11... | collective-permute-start | bytes 1155080 | tf_op jit(solution)/shard_map/ppermute | solution.py:400
  20.7 12.2 %copy-start = (f32[8,32,128]{2,1,0:T(8,128)S(1)}, f32[8,32,128]{2,1,0:T(8,128)}, u32[]{:S(2)}) copy-start(f32[8,32,128]{2,1,0:T(8,128)} %density.1) | copy-start | bytes 393220
  20.7 12.2 %copy-start.1 = (f32[32,128]{1,0:T(8,128)S(1)}, f32[32,128]{1,0:T(8,128)}, u32[]{:S(2)}) copy-start(f32[32,128]{1,0:T(8,128)} %thickness.1) | copy-start | bytes 49156
  20.7 12.2 %copy-start.2 = (f32[32,128]{1,0:T(8,128)S(1)}, f32[32,128]{1,0:T(8,128)}, u32[]{:S(2)}) copy-start(f32[32,128]{1,0:T(8,128)} %smb.1) | copy-start | bytes 49156

commit v6 on v5

--- a/solution.py
+++ b/solution.py
@@ -48,17 +48,13 @@
 
 def face_planes(parts):
     for part in range(parts + 1):
-        for number in range(DEEP if part < parts - 1 else DEEP - 1):
-            yield part, number
-
-
-def face_starts(part, parts, levels):
-    return 0, levels - (DEEP if part < parts - 1 else DEEP - 1)
+        for far in range(1, DEEP + (part < parts - 1)):
+            yield part, far, (WIDE if part < parts - 1 else WINDOW) - far
 
 
 def prepare(
     flow_far, fluid_far, bed_far, thickness_far, mask_far, density_far,
-    to_near, to_next, to_level, state, planes, weight, flow, fluid, bed, thickness, mask, density, arrived,
+    to_near, to_next, flow, fluid, bed, thickness, mask, density, arrived,
 ):
     far = (flow_far, fluid_far, bed_far, thickness_far, mask_far, density_far)
     near = (flow, fluid, bed, thickness, mask, density)
@@ -76,20 +72,27 @@
         low, high = plane[:width, :], plane[columns - width :, :]
         to_near[place : place + width, :] = jnp.where(upward, high, low)
         to_next[place : place + width, :] = jnp.where(upward, low, high)
-    above = even("gz")
-    for index, (part, number) in enumerate(face_planes(parts)):
-        low, high = (start + number for start in face_starts(part, parts, levels))
+
+
+def lay(flow, fluid, bed, thickness, mask, density, to_below, to_above, state, planes, weight):
+    parts, levels, columns, _ = flow.shape
+    for index, (part, far, _) in enumerate(face_planes(parts)):
         whole = flow.at[part] if part < parts else fluid
         spot = slice(index * columns, (index + 1) * columns)
-        to_level[spot, :] = whole[jnp.where(above, low, high)]
+        to_below[spot, :] = whole[far - 1]
+        to_above[spot, :] = whole[levels - far]
     lead = MARGIN + WINDOW
     for part in range(parts + 1):
         for level in range(levels):
             plane = flow.at[part, level] if part < parts else fluid.at[level]
             state[part, level, lead : lead + columns, :] = plane[...]
-    for number, plane in enumerate(flat):
+    height = thickness[...]
+    for number, plane in enumerate((bed[...] + height, height, mask[...].astype(jnp.float32))):
         planes[number, lead : lead + columns, :] = plane
-    weight[...] = jnp.sum(density[...], axis=0)
+    total = jnp.sum(density[...], axis=0)
+    weight[...] = total
+    for out in (to_below, to_above):
+        out[out.shape[0] - columns :, :] = total
 
 
 def unpaired(axis):
@@ -105,13 +108,12 @@
     return jnp.where(even("gx"), beyond, inner), jnp.where(even("gx"), inner, beyond)
 
 
-def widen(state_in, planes_in, weight, next_, near, state, planes, to_next, to_near):
+def widen(state_in, planes_in, next_, near, state, planes, to_below, to_above):
     parts, levels, tall, _ = state_in.shape
     parts -= 1
     rows = tall - 2 * MARGIN
     lead = MARGIN + WINDOW
     tail = MARGIN + rows - WINDOW
-    upward = even("gz")
     for part, level, width, place in side_planes(parts, levels):
         before, after = beside(near, next_, place, width, part == parts)
         source, target = (state_in, state) if part <= parts else (planes_in, planes)
@@ -119,18 +121,12 @@
         target[spot] = source[spot]
         target[(*spot, slice(lead - width, lead), slice(None))] = before
         target[(*spot, slice(tail, tail + width), slice(None))] = after
-    count = 0
-    for index, (part, number) in enumerate(face_planes(parts)):
-        low, high = (start + number for start in face_starts(part, parts, levels))
-        to_near[index * rows : (index + 1) * rows, :] = state[
-            part, jnp.where(upward, high, low), MARGIN : MARGIN + rows, :
-        ]
-        level = jnp.where(upward, low, high)
-        spot = 2 * WINDOW * index
-        to_next[spot : spot + WINDOW, :] = state[part, level, MARGIN:lead, :]
-        to_next[spot + WINDOW : spot + 2 * WINDOW, :] = state[part, level, tail : tail + WINDOW, :]
-        count = index + 1
-    to_near[count * rows :, :] = weight[...]
+    place = 0
+    for part, far, width in face_planes(parts):
+        for out, level in ((to_below, far - 1), (to_above, levels - far)):
+            out[place : place + width, :] = state[part, level, lead - width : lead, :]
+            out[place + width : place + 2 * width, :] = state[part, level, tail : tail + width, :]
+        place += 2 * width
 
 
 def along_y(field):
@@ -245,31 +241,34 @@
 
 
 def evolve(
-    own, planes, weight, stress_in, extra_in, fresh, face_next, edge_next, face_near,
+    own, planes, weight, stress_in, extra_in, fresh, edge_below, edge_above, face_below, face_above,
     out, message, beyond, later, stress, extra, slopes, marks,
 ):
     parts, levels, columns, lanes = out.shape
     rows = columns + 2 * WINDOW
     deep = levels + 2 * DEEP
     win, _, _ = window(rows)
-    upward = even("gz")
     lead = MARGIN + WINDOW
     tail = lead + columns
 
-    count = 0
-    for index, (part, number) in enumerate(face_planes(parts)):
-        lower = 0 if part < parts - 1 else 1
-        whole = face_near[rows * index : rows * (index + 1), :]
-        beyond[part, number + jnp.where(upward, DEEP, lower), win, :] = whole
-        middle = face_next[columns * index : columns * (index + 1), :]
-        sides = edge_next[2 * WINDOW * index : 2 * WINDOW * (index + 1), :]
-        if part == parts:
-            middle, sides = (jnp.where(unpaired("gz"), jnp.inf, each) for each in (middle, sides))
-        level = number + jnp.where(upward, lower, DEEP)
-        beyond[part, level, lead - WINDOW : lead, :] = sides[:WINDOW, :]
-        beyond[part, level, lead:tail, :] = middle
-        beyond[part, level, tail : tail + WINDOW, :] = sides[WINDOW:, :]
-        count = index + 1
+    lowest = lax.axis_index("gz") == 0
+    highest = lax.axis_index("gz") == lax.axis_size("gz") - 1
+    faces = face_below.shape[0] - columns
+    place = 0
+    for index, (part, far, width) in enumerate(face_planes(parts)):
+        for face, edge, level, outside in (
+            (face_below, edge_below, DEEP - far, lowest),
+            (face_above, edge_above, DEEP + far - 1, highest),
+        ):
+            middle = face[columns * index : columns * (index + 1), :]
+            left = edge[place : place + width, :]
+            right = edge[place + width : place + 2 * width, :]
+            value = jnp.inf if part == parts else 0.0
+            middle, left, right = (jnp.where(outside, value, each) for each in (middle, left, right))
+            beyond[part, level, lead - width : lead, :] = left
+            beyond[part, level, lead:tail, :] = middle
+            beyond[part, level, tail : tail + width, :] = right
+        place += 2 * width
     shared(rows, planes, slopes, marks)
 
     def before(part, k):
@@ -326,14 +325,15 @@
     flux_y = along_y(height * sum_v)
     flux_x = slopes[0, WINDOW + 1 : WINDOW + columns + 1, :] - slopes[0, WINDOW - 1 : WINDOW + columns - 1, :]
     spread = half * (flux_x + flux_y[cut, :])
-    both = weight[...] + face_near[count * rows :, :]
-    part_of_both = jnp.where(upward, both[: columns // 2, :], both[columns // 2 :, :])
+    first = even("gz")
+    both = weight[...] + jnp.where(first, face_above[faces:, :], face_below[faces:, :])
+    part_of_both = jnp.where(first, both[: columns // 2, :], both[columns // 2 :, :])
     for target in range(message.shape[0]):
         message[target, :columns, :] = spread
         message[target, columns:, :] = part_of_both
 
 
-def finish(message, density, thickness, smb, other, moved, far_moved, far_grown, far_burden, grown, burden, sent):
+def finish(message, density, thickness, smb, face_above, moved, far_moved, far_grown, far_burden, grown, burden, sent):
     copies = [
         pltpu.make_async_copy(a, b, sent.at[i])
         for i, (a, b) in enumerate(((moved, far_moved), (grown, far_grown), (burden, far_burden)))
@@ -341,12 +341,12 @@
     copies[0].start()
     devices = message.shape[0]
     levels, columns, _ = density.shape
-    count = other.shape[0] - columns
+    count = face_above.shape[0] - columns
     place = lax.axis_index("gz")
     spread = message[0, :columns, :]
     for device in range(1, devices):
         spread = spread + message[device, :columns, :]
-    over = jnp.where(even("gz"), other[count:, :], 0.0)
+    over = jnp.where(even("gz"), face_above[count:, :], 0.0)
     for device in range(2, devices, 2):
         both = jnp.concatenate([message[device, columns:, :], message[device + 1, columns:, :]], axis=0)
         over = over + jnp.where(place < device, both, 0.0)
@@ -374,30 +374,35 @@
     deep = levels + 2 * DEEP
     tall = rows + 2 * MARGIN
     near_x, next_x = pairs_of("gx")
-    near_z, next_z = pairs_of("gz")
+    count = lax.axis_size("gz")
+    up = [(i, (i + 1) % count) for i in range(count)]
+    down = [(j, i) for i, j in up]
 
     *_, (_, _, width, place) = side_planes(parts, levels)
     side = f32(place + width, lanes)
     faces = (parts + 1) * DEEP - 2
+    corners = sum(2 * width for _, _, width in face_planes(parts))
     wide = f32(parts + 1, levels, tall, lanes)
     flat = f32(3, tall, lanes)
     plane = f32(columns, lanes)
     inputs = (flow, fluid, bed, thickness, mask, density)
-    to_near, to_next, to_level, state, planes, weight = call(
+    to_near, to_next, *inputs = call(
         prepare,
-        (side, side, f32(faces * columns, lanes), wide, flat, plane),
+        (side, side, *(jax.ShapeDtypeStruct(each.shape, each.dtype) for each in inputs)),
         in_specs=[pl.BlockSpec(memory_space=pltpu.HBM)] * len(inputs),
-        scratch=[pltpu.VMEM(each.shape, each.dtype) for each in inputs] + [pltpu.SemaphoreType.DMA((len(inputs),))],
+        scratch=[pltpu.SemaphoreType.DMA((len(inputs),))],
     )(*(pltpu.with_memory_space_constraint(each, pltpu.HBM) for each in inputs))
+    face = f32((faces + 1) * columns, lanes)
+    to_below, to_above, state, planes, weight = call(lay, (face, face, wide, flat, plane))(*inputs)
     next_ = lax.ppermute(to_next, "gx", next_x)
     near = lax.ppermute(to_near, "gx", near_x)
-    face_next = lax.ppermute(to_level, "gz", next_z)
-
-    state, planes, to_next, to_near = call(
-        widen, (wide, flat, f32(faces * 2 * WINDOW, lanes), f32(faces * rows + columns, lanes))
-    )(state, planes, weight, next_, near)
-    edge_next = lax.ppermute(to_next, "gz", next_z)
-    face_near = lax.ppermute(to_near, "gz", near_z)
+    face_below = lax.ppermute(to_above, "gz", up)
+    face_above = lax.ppermute(to_below, "gz", down)
+
+    edge = f32(corners, lanes)
+    state, planes, to_below, to_above = call(widen, (wide, flat, edge, edge))(state, planes, next_, near)
+    edge_below = lax.ppermute(to_above, "gz", up)
+    edge_above = lax.ppermute(to_below, "gz", down)
 
     stress, extra, fresh = call(
         inner,
@@ -418,7 +423,7 @@
             pltpu.VMEM((2, rows, lanes), jnp.float32),
             pltpu.VMEM((4, rows, lanes), jnp.float32),
         ],
-    )(state, planes, weight, stress, extra, fresh, face_next, edge_next, face_near)
+    )(state, planes, weight, stress, extra, fresh, edge_below, edge_above, face_below, face_above)
     message = lax.all_to_all(message, "gz", split_axis=0, concat_axis=0, tiled=True)
     deep_plane = f32(*density.shape)
     moved, grown, burden = call(
@@ -430,7 +435,7 @@
             pltpu.VMEM(deep_plane.shape, jnp.float32),
             pltpu.SemaphoreType.DMA((3,)),
         ],
-    )(message, density, thickness, smb, face_near, moved)
+    )(message, density, thickness, smb, face_above, moved)
     return moved, grown, burden
 
 

time: 34.1 us -> 33.3 us (0.977)
  the two profiles are of different devices: /device:TPU:448 before, /device:TPU:1 now
where the time goes in v6:
time: 33.3 us; the launch traced here: 33.1 us
  starting transfers between devices  14 us (42%)
  blocking collectives  12.1 us (36%)
  Pallas kernels  4.35 us (13%)
  waiting for transfers between devices  2 us (6%)
  between operations  0.72 us (2%)
    all_to_all x1, blocking collectives, body(): lax.all_to_all(message, 'gz', split_axis=0, concat_axis=0, tiled=True)  12.1 us
    ppermute x1, starting transfers between devices, body(): near = lax.ppermute(to_near, 'gx', near_x)  6.57 us
    ppermute x1, starting transfers between devices, body(): edge_below = lax.ppermute(to_above, 'gz', up)  2.46 us
    ppermute x1, starting transfers between devices, body(): face_below = lax.ppermute(to_above, 'gz', up)  2.34 us
    ppermute x1, starting transfers between devices, body(): edge_above = lax.ppermute(to_below, 'gz', down)  1.92 us
    ppermute x1, waiting for transfers between devices, body(): edge_above = lax.ppermute(to_below, 'gz', down)  1.8 us
    pallas_call x1, Pallas kernels, body(): call(evolve, (f32(*flow.shape), message), scratch=[pltpu.VMEM((parts + 1,...  1.52 us
    pallas_call x1, Pallas kernels, body(): call(prepare, (side, side, *(jax.ShapeDtypeStruct(each.shape, each.dtype)...  1.24 us
  transfers between devices with their start and end apart: 6, of which 2 were waited for; matrix products, arithmetic and copies ran while one was open for 0% of the time, Pallas kernels for 2%

profile of v6, /device:TPU:1, one launch (start us, length us, event | category | flops | bytes accessed | tf_op | source)
XLA Modules:
  0.0 33.1 jit_solution(616898596023051141)
XLA Ops:
  0.6 1.2 %shard_map.94 = (f32[192,128]{1,0:T(8,128)S(1)}, f32[192,128]{1,0:T(8,128)S(1)}, f32[4,8,32,128]{3,2,1,0:T(8,128)S(1)}, f32[8,32,128]{2,1,0:T(8,128)S(1)}, f32[3...) custom-call(f32[4,8,32,128]{3,2,1,0:T(8,128)} %flow_far.1, ...), custom_call_target="tpu_custom_call" | custom-call | tf_op jit(solution)/shard_map/pallas_call | solution.py:389
  1.9 0.7 %collective-permute-start = (f32[192,128]{1,0:T(8,128)S(1)}, f32[192,128]{1,0:T(8,128)S(1)}, u32[]{:S(2)}, u32[]{:S(2)}) collective-permute-start(f32[192,128]{1,0:T(8,128)S(1)} %get-tuple-element.33), channel_id=1, source_target_pairs={{8,16},{16,8},{24,32},{32,24},{40,48},{48,40},{56,64},{64,56},{72,... | collective-permute-start | bytes 294920 | tf_op jit(solution)/shard_map/ppermute | solution.py:397
  2.6 6.6 %collective-permute-start.1 = (f32[192,128]{1,0:T(8,128)S(1)}, f32[192,128]{1,0:T(8,128)S(1)}, u32[]{:S(2)}, u32[]{:S(2)}) collective-permute-start(f32[192,128]{1,0:T(8,128)S(1)} %get-tuple-element.34), channel_id=1, source_target_pairs={{0,8},{8,0},{16,24},{24,16},{32,40},{40,32},{48,56},{56,48},{64,72... | collective-permute-start | bytes 294920 | tf_op jit(solution)/shard_map/ppermute | solution.py:398
  9.1 0.1 shard_map.95
  9.2 2.3 %collective-permute-start.4 = (f32[608,128]{1,0:T(8,128)S(1)}, f32[608,128]{1,0:T(8,128)S(1)}, u32[]{:S(2)}, u32[]{:S(2)}) collective-permute-start(f32[608,128]{1,0:T(8,128)S(1)} %get-tuple-element.43), channel_id=1, source_target_pairs={{0,1},{1,2},{2,3},{3,4},{4,5},{5,6},{6,7},{7,0},{8,9},{9,10},{10,1... | collective-permute-start | bytes 933896 | tf_op jit(solution)/shard_map/ppermute | solution.py:399
  11.6 0.0 collective-permute-start.5
  11.6 0.0 collective-permute-done.next_
  11.6 0.0 collective-permute-done.1.near
  11.6 0.1 shard_map.96
  11.7 2.5 %collective-permute-start.2 = (f32[84,128]{1,0:T(8,128)S(1)}, f32[84,128]{1,0:T(8,128)S(1)}, u32[]{:S(2)}, u32[]{:S(2)}) collective-permute-start(f32[84,128]{1,0:T(8,128)S(1)} %get-tuple-element.41), channel_id=1, source_target_pairs={{0,1},{1,2},{2,3},{3,4},{4,5},{5,6},{6,7},{7,0},{8,9},{9,10},{10,1... | collective-permute-start | bytes 129032 | tf_op jit(solution)/shard_map/ppermute | solution.py:404
  14.2 1.9 %collective-permute-start.3 = (f32[84,128]{1,0:T(8,128)S(1)}, f32[84,128]{1,0:T(8,128)S(1)}, u32[]{:S(2)}, u32[]{:S(2)}) collective-permute-start(f32[84,128]{1,0:T(8,128)S(1)} %get-tuple-element.42), channel_id=1, source_target_pairs={{1,0},{2,1},{3,2},{4,3},{5,4},{6,5},{7,6},{0,7},{9,8},{10,9},{11,1... | collective-permute-start | bytes 129032 | tf_op jit(solution)/shard_map/ppermute | solution.py:405
  16.1 0.5 %shard_map.97 = (f32[6,6,56,128]{3,2,1,0:T(8,128)S(1)}, f32[2,6,40,128]{3,2,1,0:T(8,128)S(1)}, f32[4,4,56,128]{3,2,1,0:T(8,128)S(1)}) custom-call(f32[5,8,56,128]{3,2,1,0:T(8,128)S(1)} %get-tuple-element.35.state.own, f32[3,56,128]{2,1,0:T(8,128)S(1)} %get-tuple-element.36.planes), custom_call_target="tpu_custom_call" | custom-call | flops 5000000000 | bytes 5000000000 | tf_op jit(solution)/shard_map/pallas_call | solution.py:407
  16.6 0.2 collective-permute-done.2.edge_below
  16.8 1.8 %collective-permute-done.3.edge_above = f32[84,128]{1,0:T(8,128)S(1)} collective-permute-done((f32[84,128]{1,0:T(8,128)S(1)}, f32[84,128]{1,0:T(8,128)S(1)}, u32[]{:S(2)}, u32[]{:S(2)}) %collective-permute-start.3) | collective-permute-done | bytes 43040 | tf_op jit(solution)/shard_map/ppermute | solution.py:405
  18.6 0.0 collective-permute-done.4.face_below
  18.6 0.0 collective-permute-done.5.face_above
  18.6 0.0 copy-start
  18.6 0.0 copy-start.1
  18.6 0.0 copy-start.2
  18.6 1.5 %shard_map.98 = (f32[4,8,32,128]{3,2,1,0:T(8,128)S(1)}, f32[8,48,128]{2,1,0:T(8,128)S(1)}) custom-call(f32[5,8,56,128]{3,2,1,0:T(8,128)S(1)} %get-tuple-element.35.state.own, f32[3,56,128]{2,1,0:T(8,128)S(1)} %get-tuple-element.36.planes, f32[32,128]{1,0:T(8,128)S(1)} %get-tuple-element.37.weight, f32[6,6,56,128]{3,2,1,0:T(8,128)S(1)} %get-tuple-element.38.stress_in, ...), custom_call_target="tpu_custom_call" | custom-call | tf_op jit(solution)/shard_map/pallas_call | solution.py:415
  20.2 12.1 %all_to_all.5.message = f32[8,48,128]{2,1,0:T(8,128)S(1)} all-to-all(f32[8,48,128]{2,1,0:T(8,128)S(1)} %get-tuple-element.45), channel_id=1, replica_groups=mesh['gx'=64,'gz'=8] {'gz'}, dimensions={0} | all-to-all | bytes 393216 | tf_op jit(solution)/shard_map/all_to_all | solution.py:427
  32.2 0.0 copy-done
  32.2 0.0 copy-done.1
  32.2 0.0 copy-done.2
  32.2 0.9 %shard_map.99 = (f32[4,8,32,128]{3,2,1,0:T(8,128)}, f32[32,128]{1,0:T(8,128)}, f32[8,32,128]{2,1,0:T(8,128)}) custom-call(f32[8,48,128]{2,1,0:T(8,128)S(1)} %all_to_all.5.message, f32[8,32,128]{2,1,0:T(8,128)S(1)} %copy-done, f32[32,128]{1,0:T(8,128)S(1)} %copy-done.1, f32[32,128]{1,0:T(8,128)S(1)} %copy-done.2, ...), custom_call_target="tpu_custom_call" | custom-call | tf_op jit(solution)/shard_map/pallas_call | solution.py:429
Async XLA Ops:
  1.9 9.7 %collective-permute-start = (f32[192,128]{1,0:T(8,128)S(1)}, f32[192,128]{1,0:T(8,128)S(1)}, u32[]{:S(2)}, u32[]{:S(2)}) collective-permute-start(f32[192,128]{1,0:T(8,128)S(1)} %get-tuple-element.33), channel_id=1, source_target_pairs={{8,16},{16,8},{24,32},{32,24},{40,48},{48,40},{56,64},{64,56},{72,... | collective-permute-start | bytes 294920 | tf_op jit(solution)/shard_map/ppermute | solution.py:397
  2.6 9.0 %collective-permute-start.1 = (f32[192,128]{1,0:T(8,128)S(1)}, f32[192,128]{1,0:T(8,128)S(1)}, u32[]{:S(2)}, u32[]{:S(2)}) collective-permute-start(f32[192,128]{1,0:T(8,128)S(1)} %get-tuple-element.34), channel_id=1, source_target_pairs={{0,8},{8,0},{16,24},{24,16},{32,40},{40,32},{48,56},{56,48},{64,72... | collective-permute-start | bytes 294920 | tf_op jit(solution)/shard_map/ppermute | solution.py:398
  9.2 9.4 %collective-permute-start.4 = (f32[608,128]{1,0:T(8,128)S(1)}, f32[608,128]{1,0:T(8,128)S(1)}, u32[]{:S(2)}, u32[]{:S(2)}) collective-permute-start(f32[608,128]{1,0:T(8,128)S(1)} %get-tuple-element.43), channel_id=1, source_target_pairs={{0,1},{1,2},{2,3},{3,4},{4,5},{5,6},{6,7},{7,0},{8,9},{9,10},{10,1... | collective-permute-start | bytes 933896 | tf_op jit(solution)/shard_map/ppermute | solution.py:399
  11.6 7.0 %collective-permute-start.5 = (f32[608,128]{1,0:T(8,128)S(1)}, f32[608,128]{1,0:T(8,128)S(1)}, u32[]{:S(2)}, u32[]{:S(2)}) collective-permute-start(f32[608,128]{1,0:T(8,128)S(1)} %get-tuple-element.44), channel_id=1, source_target_pairs={{1,0},{2,1},{3,2},{4,3},{5,4},{6,5},{7,6},{0,7},{9,8},{10,9},{11,1... | collective-permute-start | bytes 933896 | tf_op jit(solution)/shard_map/ppermute | solution.py:400
  11.7 5.1 %collective-permute-start.2 = (f32[84,128]{1,0:T(8,128)S(1)}, f32[84,128]{1,0:T(8,128)S(1)}, u32[]{:S(2)}, u32[]{:S(2)}) collective-permute-start(f32[84,128]{1,0:T(8,128)S(1)} %get-tuple-element.41), channel_id=1, source_target_pairs={{0,1},{1,2},{2,3},{3,4},{4,5},{5,6},{6,7},{7,0},{8,9},{9,10},{10,1... | collective-permute-start | bytes 129032 | tf_op jit(solution)/shard_map/ppermute | solution.py:404
  14.2 4.4 %collective-permute-start.3 = (f32[84,128]{1,0:T(8,128)S(1)}, f32[84,128]{1,0:T(8,128)S(1)}, u32[]{:S(2)}, u32[]{:S(2)}) collective-permute-start(f32[84,128]{1,0:T(8,128)S(1)} %get-tuple-element.42), channel_id=1, source_target_pairs={{1,0},{2,1},{3,2},{4,3},{5,4},{6,5},{7,6},{0,7},{9,8},{10,9},{11,1... | collective-permute-start | bytes 129032 | tf_op jit(solution)/shard_map/ppermute | solution.py:405
  18.6 13.6 %copy-start = (f32[8,32,128]{2,1,0:T(8,128)S(1)}, f32[8,32,128]{2,1,0:T(8,128)}, u32[]{:S(2)}) copy-start(f32[8,32,128]{2,1,0:T(8,128)} %density.1) | copy-start | bytes 393220
  18.6 13.6 %copy-start.1 = (f32[32,128]{1,0:T(8,128)S(1)}, f32[32,128]{1,0:T(8,128)}, u32[]{:S(2)}) copy-start(f32[32,128]{1,0:T(8,128)} %thickness.1) | copy-start | bytes 49156
  18.6 13.6 %copy-start.2 = (f32[32,128]{1,0:T(8,128)S(1)}, f32[32,128]{1,0:T(8,128)}, u32[]{:S(2)}) copy-start(f32[32,128]{1,0:T(8,128)} %smb.1) | copy-start | bytes 49156

commit v7 on v6

--- a/solution.py
+++ b/solution.py
@@ -241,7 +241,7 @@
 
 
 def evolve(
-    own, planes, weight, stress_in, extra_in, fresh, edge_below, edge_above, face_below, face_above,
+    own, planes, weight, stress_in, extra_in, fresh, edge_above, edge_below, face_above, face_below,
     out, message, beyond, later, stress, extra, slopes, marks,
 ):
     parts, levels, columns, lanes = out.shape
@@ -423,7 +423,7 @@
             pltpu.VMEM((2, rows, lanes), jnp.float32),
             pltpu.VMEM((4, rows, lanes), jnp.float32),
         ],
-    )(state, planes, weight, stress, extra, fresh, edge_below, edge_above, face_below, face_above)
+    )(state, planes, weight, stress, extra, fresh, edge_above, edge_below, face_above, face_below)
     message = lax.all_to_all(message, "gz", split_axis=0, concat_axis=0, tiled=True)
     deep_plane = f32(*density.shape)
     moved, grown, burden = call(

time: 33.3 us -> 31.7 us (0.952)
  the two profiles are of different devices: /device:TPU:1 before, /device:TPU:448 now
where the time goes in v7:
time: 31.7 us; the launch traced here: 31.3 us
  starting transfers between devices  10.3 us (32%)
  blocking collectives  9.23 us (29%)
  waiting for transfers between devices  6.73 us (21%)
  Pallas kernels  4.34 us (14%)
  between operations  0.71 us (2%)
    all_to_all x1, blocking collectives, body(): lax.all_to_all(message, 'gz', split_axis=0, concat_axis=0, tiled=True)  9.23 us
    ppermute x1, starting transfers between devices, body(): next_ = lax.ppermute(to_next, 'gx', next_x)  5.37 us
    ppermute x1, waiting for transfers between devices, body(): edge_below = lax.ppermute(to_above, 'gz', up)  2.97 us
    ppermute x1, waiting for transfers between devices, body(): near = lax.ppermute(to_near, 'gx', near_x)  2.55 us
    ppermute x1, starting transfers between devices, body(): face_above = lax.ppermute(to_below, 'gz', down)  1.93 us
    ppermute x1, starting transfers between devices, body(): near = lax.ppermute(to_near, 'gx', near_x)  1.92 us
    pallas_call x1, Pallas kernels, body(): call(evolve, (f32(*flow.shape), message), scratch=[pltpu.VMEM((parts + 1,...  1.51 us
    pallas_call x1, Pallas kernels, body(): call(prepare, (side, side, *(jax.ShapeDtypeStruct(each.shape, each.dtype)...  1.24 us
  transfers between devices with their start and end apart: 6, of which 3 were waited for; matrix products, arithmetic and copies ran while one was open for 0% of the time, Pallas kernels for 2%

profile of v7, /device:TPU:448, one launch (start us, length us, event | category | flops | bytes accessed | tf_op | source)
XLA Modules:
  0.0 31.3 jit_solution(18048881863472614824)
XLA Ops:
  0.6 1.2 %shard_map.94 = (f32[192,128]{1,0:T(8,128)S(1)}, f32[192,128]{1,0:T(8,128)S(1)}, f32[4,8,32,128]{3,2,1,0:T(8,128)S(1)}, f32[8,32,128]{2,1,0:T(8,128)S(1)}, f32[3...) custom-call(f32[4,8,32,128]{3,2,1,0:T(8,128)} %flow_far.1, ...), custom_call_target="tpu_custom_call" | custom-call | tf_op jit(solution)/shard_map/pallas_call | solution.py:389
  1.9 5.4 %collective-permute-start = (f32[192,128]{1,0:T(8,128)S(1)}, f32[192,128]{1,0:T(8,128)S(1)}, u32[]{:S(2)}, u32[]{:S(2)}) collective-permute-start(f32[192,128]{1,0:T(8,128)S(1)} %get-tuple-element.33), channel_id=1, source_target_pairs={{8,16},{16,8},{24,32},{32,24},{40,48},{48,40},{56,64},{64,56},{72,... | collective-permute-start | bytes 294920 | tf_op jit(solution)/shard_map/ppermute | solution.py:397
  7.3 1.9 %collective-permute-start.1 = (f32[192,128]{1,0:T(8,128)S(1)}, f32[192,128]{1,0:T(8,128)S(1)}, u32[]{:S(2)}, u32[]{:S(2)}) collective-permute-start(f32[192,128]{1,0:T(8,128)S(1)} %get-tuple-element.34), channel_id=1, source_target_pairs={{0,8},{8,0},{16,24},{24,16},{32,40},{40,32},{48,56},{56,48},{64,72... | collective-permute-start | bytes 294920 | tf_op jit(solution)/shard_map/ppermute | solution.py:398
  9.2 0.1 shard_map.95
  9.3 1.9 %collective-permute-start.4 = (f32[608,128]{1,0:T(8,128)S(1)}, f32[608,128]{1,0:T(8,128)S(1)}, u32[]{:S(2)}, u32[]{:S(2)}) collective-permute-start(f32[608,128]{1,0:T(8,128)S(1)} %get-tuple-element.43), channel_id=1, source_target_pairs={{1,0},{2,1},{3,2},{4,3},{5,4},{6,5},{7,6},{0,7},{9,8},{10,9},{11,1... | collective-permute-start | bytes 933896 | tf_op jit(solution)/shard_map/ppermute | solution.py:400
  11.2 0.0 collective-permute-start.5
  11.2 0.0 collective-permute-done.next_
  11.2 2.5 %collective-permute-done.1.near = f32[192,128]{1,0:T(8,128)S(1)} collective-permute-done((f32[192,128]{1,0:T(8,128)S(1)}, f32[192,128]{1,0:T(8,128)S(1)}, u32[]{:S(2)}, u32[]{:S(2)}) %collective-permute-start.1) | collective-permute-done | bytes 98336 | tf_op jit(solution)/shard_map/ppermute | solution.py:398
  13.8 0.1 shard_map.96
  13.9 1.1 %collective-permute-start.2 = (f32[84,128]{1,0:T(8,128)S(1)}, f32[84,128]{1,0:T(8,128)S(1)}, u32[]{:S(2)}, u32[]{:S(2)}) collective-permute-start(f32[84,128]{1,0:T(8,128)S(1)} %get-tuple-element.41), channel_id=1, source_target_pairs={{1,0},{2,1},{3,2},{4,3},{5,4},{6,5},{7,6},{0,7},{9,8},{10,9},{11,1... | collective-permute-start | bytes 129032 | tf_op jit(solution)/shard_map/ppermute | solution.py:405
  15.0 0.0 collective-permute-start.3
  15.0 0.5 %shard_map.97 = (f32[6,6,56,128]{3,2,1,0:T(8,128)S(1)}, f32[2,6,40,128]{3,2,1,0:T(8,128)S(1)}, f32[4,4,56,128]{3,2,1,0:T(8,128)S(1)}) custom-call(f32[5,8,56,128]{3,2,1,0:T(8,128)S(1)} %get-tuple-element.35.state.own, f32[3,56,128]{2,1,0:T(8,128)S(1)} %get-tuple-element.36.planes), custom_call_target="tpu_custom_call" | custom-call | flops 5000000000 | bytes 5000000000 | tf_op jit(solution)/shard_map/pallas_call | solution.py:407
  15.5 1.2 %collective-permute-done.2.edge_above = f32[84,128]{1,0:T(8,128)S(1)} collective-permute-done((f32[84,128]{1,0:T(8,128)S(1)}, f32[84,128]{1,0:T(8,128)S(1)}, u32[]{:S(2)}, u32[]{:S(2)}) %collective-permute-start.2) | collective-permute-done | bytes 43040 | tf_op jit(solution)/shard_map/ppermute | solution.py:405
  16.7 3.0 %collective-permute-done.3.edge_below = f32[84,128]{1,0:T(8,128)S(1)} collective-permute-done((f32[84,128]{1,0:T(8,128)S(1)}, f32[84,128]{1,0:T(8,128)S(1)}, u32[]{:S(2)}, u32[]{:S(2)}) %collective-permute-start.3) | collective-permute-done | bytes 43040 | tf_op jit(solution)/shard_map/ppermute | solution.py:404
  19.7 0.0 collective-permute-done.4.face_above
  19.7 0.0 collective-permute-done.5.face_below
  19.7 0.0 copy-start
  19.7 0.0 copy-start.1
  19.7 0.0 copy-start.2
  19.7 1.5 %shard_map.98 = (f32[4,8,32,128]{3,2,1,0:T(8,128)S(1)}, f32[8,48,128]{2,1,0:T(8,128)S(1)}) custom-call(f32[5,8,56,128]{3,2,1,0:T(8,128)S(1)} %get-tuple-element.35.state.own, f32[3,56,128]{2,1,0:T(8,128)S(1)} %get-tuple-element.36.planes, f32[32,128]{1,0:T(8,128)S(1)} %get-tuple-element.37.weight, f32[6,6,56,128]{3,2,1,0:T(8,128)S(1)} %get-tuple-element.38.stress_in, ...), custom_call_target="tpu_custom_call" | custom-call | tf_op jit(solution)/shard_map/pallas_call | solution.py:415
  21.2 9.2 %all_to_all.5.message = f32[8,48,128]{2,1,0:T(8,128)S(1)} all-to-all(f32[8,48,128]{2,1,0:T(8,128)S(1)} %get-tuple-element.45), channel_id=1, replica_groups=mesh['gx'=64,'gz'=8] {'gz'}, dimensions={0} | all-to-all | bytes 393216 | tf_op jit(solution)/shard_map/all_to_all | solution.py:427
  30.4 0.0 copy-done
  30.4 0.0 copy-done.1
  30.5 0.0 copy-done.2
  30.5 0.9 %shard_map.99 = (f32[4,8,32,128]{3,2,1,0:T(8,128)}, f32[32,128]{1,0:T(8,128)}, f32[8,32,128]{2,1,0:T(8,128)}) custom-call(f32[8,48,128]{2,1,0:T(8,128)S(1)} %all_to_all.5.message, f32[8,32,128]{2,1,0:T(8,128)S(1)} %copy-done, f32[32,128]{1,0:T(8,128)S(1)} %copy-done.1, f32[32,128]{1,0:T(8,128)S(1)} %copy-done.2, ...), custom_call_target="tpu_custom_call" | custom-call | tf_op jit(solution)/shard_map/pallas_call | solution.py:429
Async XLA Ops:
  1.9 9.3 %collective-permute-start = (f32[192,128]{1,0:T(8,128)S(1)}, f32[192,128]{1,0:T(8,128)S(1)}, u32[]{:S(2)}, u32[]{:S(2)}) collective-permute-start(f32[192,128]{1,0:T(8,128)S(1)} %get-tuple-element.33), channel_id=1, source_target_pairs={{8,16},{16,8},{24,32},{32,24},{40,48},{48,40},{56,64},{64,56},{72,... | collective-permute-start | bytes 294920 | tf_op jit(solution)/shard_map/ppermute | solution.py:397
  7.3 6.5 %collective-permute-start.1 = (f32[192,128]{1,0:T(8,128)S(1)}, f32[192,128]{1,0:T(8,128)S(1)}, u32[]{:S(2)}, u32[]{:S(2)}) collective-permute-start(f32[192,128]{1,0:T(8,128)S(1)} %get-tuple-element.34), channel_id=1, source_target_pairs={{0,8},{8,0},{16,24},{24,16},{32,40},{40,32},{48,56},{56,48},{64,72... | collective-permute-start | bytes 294920 | tf_op jit(solution)/shard_map/ppermute | solution.py:398
  9.3 10.4 %collective-permute-start.4 = (f32[608,128]{1,0:T(8,128)S(1)}, f32[608,128]{1,0:T(8,128)S(1)}, u32[]{:S(2)}, u32[]{:S(2)}) collective-permute-start(f32[608,128]{1,0:T(8,128)S(1)} %get-tuple-element.43), channel_id=1, source_target_pairs={{1,0},{2,1},{3,2},{4,3},{5,4},{6,5},{7,6},{0,7},{9,8},{10,9},{11,1... | collective-permute-start | bytes 933896 | tf_op jit(solution)/shard_map/ppermute | solution.py:400
  11.2 8.4 %collective-permute-start.5 = (f32[608,128]{1,0:T(8,128)S(1)}, f32[608,128]{1,0:T(8,128)S(1)}, u32[]{:S(2)}, u32[]{:S(2)}) collective-permute-start(f32[608,128]{1,0:T(8,128)S(1)} %get-tuple-element.44), channel_id=1, source_target_pairs={{0,1},{1,2},{2,3},{3,4},{4,5},{5,6},{6,7},{7,0},{8,9},{9,10},{10,1... | collective-permute-start | bytes 933896 | tf_op jit(solution)/shard_map/ppermute | solution.py:399
  13.9 2.8 %collective-permute-start.2 = (f32[84,128]{1,0:T(8,128)S(1)}, f32[84,128]{1,0:T(8,128)S(1)}, u32[]{:S(2)}, u32[]{:S(2)}) collective-permute-start(f32[84,128]{1,0:T(8,128)S(1)} %get-tuple-element.41), channel_id=1, source_target_pairs={{1,0},{2,1},{3,2},{4,3},{5,4},{6,5},{7,6},{0,7},{9,8},{10,9},{11,1... | collective-permute-start | bytes 129032 | tf_op jit(solution)/shard_map/ppermute | solution.py:405
  15.0 4.7 %collective-permute-start.3 = (f32[84,128]{1,0:T(8,128)S(1)}, f32[84,128]{1,0:T(8,128)S(1)}, u32[]{:S(2)}, u32[]{:S(2)}) collective-permute-start(f32[84,128]{1,0:T(8,128)S(1)} %get-tuple-element.42), channel_id=1, source_target_pairs={{0,1},{1,2},{2,3},{3,4},{4,5},{5,6},{6,7},{7,0},{8,9},{9,10},{10,1... | collective-permute-start | bytes 129032 | tf_op jit(solution)/shard_map/ppermute | solution.py:404
  19.7 10.8 %copy-start = (f32[8,32,128]{2,1,0:T(8,128)S(1)}, f32[8,32,128]{2,1,0:T(8,128)}, u32[]{:S(2)}) copy-start(f32[8,32,128]{2,1,0:T(8,128)} %density.1) | copy-start | bytes 393220
  19.7 10.8 %copy-start.1 = (f32[32,128]{1,0:T(8,128)S(1)}, f32[32,128]{1,0:T(8,128)}, u32[]{:S(2)}) copy-start(f32[32,128]{1,0:T(8,128)} %thickness.1) | copy-start | bytes 49156
  19.7 10.8 %copy-start.2 = (f32[32,128]{1,0:T(8,128)S(1)}, f32[32,128]{1,0:T(8,128)}, u32[]{:S(2)}) copy-start(f32[32,128]{1,0:T(8,128)} %smb.1) | copy-start | bytes 49156

commit v8 on v7

--- a/solution.py
+++ b/solution.py
@@ -241,7 +241,7 @@
 
 
 def evolve(
-    own, planes, weight, stress_in, extra_in, fresh, edge_above, edge_below, face_above, face_below,
+    own, planes, weight, stress_in, extra_in, fresh, edge_below, edge_above, face_above, face_below,
     out, message, beyond, later, stress, extra, slopes, marks,
 ):
     parts, levels, columns, lanes = out.shape
@@ -423,7 +423,7 @@
             pltpu.VMEM((2, rows, lanes), jnp.float32),
             pltpu.VMEM((4, rows, lanes), jnp.float32),
         ],
-    )(state, planes, weight, stress, extra, fresh, edge_above, edge_below, face_above, face_below)
+    )(state, planes, weight, stress, extra, fresh, edge_below, edge_above, face_above, face_below)
     message = lax.all_to_all(message, "gz", split_axis=0, concat_axis=0, tiled=True)
     deep_plane = f32(*density.shape)
     moved, grown, burden = call(

time: 31.7 us -> 33.3 us (1.050)
  the two profiles are of different devices: /device:TPU:448 before, /device:TPU:1 now
where the time goes in v8:
time: 33.3 us; the launch traced here: 33.1 us
  starting transfers between devices  14 us (42%)
  blocking collectives  12.7 us (38%)
  Pallas kernels  4.34 us (13%)
  waiting for transfers between devices  1.35 us (4%)
  between operations  0.71 us (2%)
    all_to_all x1, blocking collectives, body(): lax.all_to_all(message, 'gz', split_axis=0, concat_axis=0, tiled=True)  12.7 us
    ppermute x1, starting transfers between devices, body(): near = lax.ppermute(to_near, 'gx', near_x)  6.57 us
    ppermute x1, starting transfers between devices, body(): edge_below = lax.ppermute(to_above, 'gz', up)  2.45 us
    ppermute x1, starting transfers between devices, body(): face_above = lax.ppermute(to_below, 'gz', down)  2.24 us
    ppermute x1, starting transfers between devices, body(): edge_above = lax.ppermute(to_below, 'gz', down)  1.92 us
    pallas_call x1, Pallas kernels, body(): call(evolve, (f32(*flow.shape), message), scratch=[pltpu.VMEM((parts + 1,...  1.52 us
    pallas_call x1, Pallas kernels, body(): call(prepare, (side, side, *(jax.ShapeDtypeStruct(each.shape, each.dtype)...  1.24 us
    ppermute x1, waiting for transfers between devices, body(): edge_above = lax.ppermute(to_below, 'gz', down)  1.15 us
  transfers between devices with their start and end apart: 6, of which 2 were waited for; matrix products, arithmetic and copies ran while one was open for 0% of the time, Pallas kernels for 2%

profile of v8, /device:TPU:1, one launch (start us, length us, event | category | flops | bytes accessed | tf_op | source)
XLA Modules:
  0.0 33.1 jit_solution(8933108103564486113)
XLA Ops:
  0.6 1.2 %shard_map.94 = (f32[192,128]{1,0:T(8,128)S(1)}, f32[192,128]{1,0:T(8,128)S(1)}, f32[4,8,32,128]{3,2,1,0:T(8,128)S(1)}, f32[8,32,128]{2,1,0:T(8,128)S(1)}, f32[3...) custom-call(f32[4,8,32,128]{3,2,1,0:T(8,128)} %flow_far.1, ...), custom_call_target="tpu_custom_call" | custom-call | tf_op jit(solution)/shard_map/pallas_call | solution.py:389
  1.9 0.7 %collective-permute-start = (f32[192,128]{1,0:T(8,128)S(1)}, f32[192,128]{1,0:T(8,128)S(1)}, u32[]{:S(2)}, u32[]{:S(2)}) collective-permute-start(f32[192,128]{1,0:T(8,128)S(1)} %get-tuple-element.33), channel_id=1, source_target_pairs={{8,16},{16,8},{24,32},{32,24},{40,48},{48,40},{56,64},{64,56},{72,... | collective-permute-start | bytes 294920 | tf_op jit(solution)/shard_map/ppermute | solution.py:397
  2.6 6.6 %collective-permute-start.1 = (f32[192,128]{1,0:T(8,128)S(1)}, f32[192,128]{1,0:T(8,128)S(1)}, u32[]{:S(2)}, u32[]{:S(2)}) collective-permute-start(f32[192,128]{1,0:T(8,128)S(1)} %get-tuple-element.34), channel_id=1, source_target_pairs={{0,8},{8,0},{16,24},{24,16},{32,40},{40,32},{48,56},{56,48},{64,72... | collective-permute-start | bytes 294920 | tf_op jit(solution)/shard_map/ppermute | solution.py:398
  9.1 0.1 shard_map.95
  9.2 2.2 %collective-permute-start.4 = (f32[608,128]{1,0:T(8,128)S(1)}, f32[608,128]{1,0:T(8,128)S(1)}, u32[]{:S(2)}, u32[]{:S(2)}) collective-permute-start(f32[608,128]{1,0:T(8,128)S(1)} %get-tuple-element.43), channel_id=1, source_target_pairs={{1,0},{2,1},{3,2},{4,3},{5,4},{6,5},{7,6},{0,7},{9,8},{10,9},{11,1... | collective-permute-start | bytes 933896 | tf_op jit(solution)/shard_map/ppermute | solution.py:400
  11.5 0.1 collective-permute-start.5
  11.6 0.0 collective-permute-done.next_
  11.6 0.0 collective-permute-done.1.near
  11.6 0.1 shard_map.96
  11.7 2.4 %collective-permute-start.2 = (f32[84,128]{1,0:T(8,128)S(1)}, f32[84,128]{1,0:T(8,128)S(1)}, u32[]{:S(2)}, u32[]{:S(2)}) collective-permute-start(f32[84,128]{1,0:T(8,128)S(1)} %get-tuple-element.41), channel_id=1, source_target_pairs={{0,1},{1,2},{2,3},{3,4},{4,5},{5,6},{6,7},{7,0},{8,9},{9,10},{10,1... | collective-permute-start | bytes 129032 | tf_op jit(solution)/shard_map/ppermute | solution.py:404
  14.2 1.9 %collective-permute-start.3 = (f32[84,128]{1,0:T(8,128)S(1)}, f32[84,128]{1,0:T(8,128)S(1)}, u32[]{:S(2)}, u32[]{:S(2)}) collective-permute-start(f32[84,128]{1,0:T(8,128)S(1)} %get-tuple-element.42), channel_id=1, source_target_pairs={{1,0},{2,1},{3,2},{4,3},{5,4},{6,5},{7,6},{0,7},{9,8},{10,9},{11,1... | collective-permute-start | bytes 129032 | tf_op jit(solution)/shard_map/ppermute | solution.py:405
  16.1 0.5 %shard_map.97 = (f32[6,6,56,128]{3,2,1,0:T(8,128)S(1)}, f32[2,6,40,128]{3,2,1,0:T(8,128)S(1)}, f32[4,4,56,128]{3,2,1,0:T(8,128)S(1)}) custom-call(f32[5,8,56,128]{3,2,1,0:T(8,128)S(1)} %get-tuple-element.35.state.own, f32[3,56,128]{2,1,0:T(8,128)S(1)} %get-tuple-element.36.planes), custom_call_target="tpu_custom_call" | custom-call | flops 5000000000 | bytes 5000000000 | tf_op jit(solution)/shard_map/pallas_call | solution.py:407
  16.6 0.2 collective-permute-done.2.edge_below
  16.8 1.1 %collective-permute-done.3.edge_above = f32[84,128]{1,0:T(8,128)S(1)} collective-permute-done((f32[84,128]{1,0:T(8,128)S(1)}, f32[84,128]{1,0:T(8,128)S(1)}, u32[]{:S(2)}, u32[]{:S(2)}) %collective-permute-start.3) | collective-permute-done | bytes 43040 | tf_op jit(solution)/shard_map/ppermute | solution.py:405
  18.0 0.0 collective-permute-done.4.face_above
  18.0 0.0 collective-permute-done.5.face_below
  18.0 0.0 copy-start
  18.0 0.0 copy-start.1
  18.0 0.0 copy-start.2
  18.0 1.5 %shard_map.98 = (f32[4,8,32,128]{3,2,1,0:T(8,128)S(1)}, f32[8,48,128]{2,1,0:T(8,128)S(1)}) custom-call(f32[5,8,56,128]{3,2,1,0:T(8,128)S(1)} %get-tuple-element.35.state.own, f32[3,56,128]{2,1,0:T(8,128)S(1)} %get-tuple-element.36.planes, f32[32,128]{1,0:T(8,128)S(1)} %get-tuple-element.37.weight, f32[6,6,56,128]{3,2,1,0:T(8,128)S(1)} %get-tuple-element.38.stress_in, ...), custom_call_target="tpu_custom_call" | custom-call | tf_op jit(solution)/shard_map/pallas_call | solution.py:415
  19.5 12.7 %all_to_all.5.message = f32[8,48,128]{2,1,0:T(8,128)S(1)} all-to-all(f32[8,48,128]{2,1,0:T(8,128)S(1)} %get-tuple-element.45), channel_id=1, replica_groups=mesh['gx'=64,'gz'=8] {'gz'}, dimensions={0} | all-to-all | bytes 393216 | tf_op jit(solution)/shard_map/all_to_all | solution.py:427
  32.2 0.0 copy-done
  32.2 0.0 copy-done.1
  32.2 0.0 copy-done.2
  32.2 0.9 %shard_map.99 = (f32[4,8,32,128]{3,2,1,0:T(8,128)}, f32[32,128]{1,0:T(8,128)}, f32[8,32,128]{2,1,0:T(8,128)}) custom-call(f32[8,48,128]{2,1,0:T(8,128)S(1)} %all_to_all.5.message, f32[8,32,128]{2,1,0:T(8,128)S(1)} %copy-done, f32[32,128]{1,0:T(8,128)S(1)} %copy-done.1, f32[32,128]{1,0:T(8,128)S(1)} %copy-done.2, ...), custom_call_target="tpu_custom_call" | custom-call | tf_op jit(solution)/shard_map/pallas_call | solution.py:429
Async XLA Ops:
  1.9 9.7 %collective-permute-start = (f32[192,128]{1,0:T(8,128)S(1)}, f32[192,128]{1,0:T(8,128)S(1)}, u32[]{:S(2)}, u32[]{:S(2)}) collective-permute-start(f32[192,128]{1,0:T(8,128)S(1)} %get-tuple-element.33), channel_id=1, source_target_pairs={{8,16},{16,8},{24,32},{32,24},{40,48},{48,40},{56,64},{64,56},{72,... | collective-permute-start | bytes 294920 | tf_op jit(solution)/shard_map/ppermute | solution.py:397
  2.6 9.1 %collective-permute-start.1 = (f32[192,128]{1,0:T(8,128)S(1)}, f32[192,128]{1,0:T(8,128)S(1)}, u32[]{:S(2)}, u32[]{:S(2)}) collective-permute-start(f32[192,128]{1,0:T(8,128)S(1)} %get-tuple-element.34), channel_id=1, source_target_pairs={{0,8},{8,0},{16,24},{24,16},{32,40},{40,32},{48,56},{56,48},{64,72... | collective-permute-start | bytes 294920 | tf_op jit(solution)/shard_map/ppermute | solution.py:398
  9.2 8.7 %collective-permute-start.4 = (f32[608,128]{1,0:T(8,128)S(1)}, f32[608,128]{1,0:T(8,128)S(1)}, u32[]{:S(2)}, u32[]{:S(2)}) collective-permute-start(f32[608,128]{1,0:T(8,128)S(1)} %get-tuple-element.43), channel_id=1, source_target_pairs={{1,0},{2,1},{3,2},{4,3},{5,4},{6,5},{7,6},{0,7},{9,8},{10,9},{11,1... | collective-permute-start | bytes 933896 | tf_op jit(solution)/shard_map/ppermute | solution.py:400
  11.5 6.5 %collective-permute-start.5 = (f32[608,128]{1,0:T(8,128)S(1)}, f32[608,128]{1,0:T(8,128)S(1)}, u32[]{:S(2)}, u32[]{:S(2)}) collective-permute-start(f32[608,128]{1,0:T(8,128)S(1)} %get-tuple-element.44), channel_id=1, source_target_pairs={{0,1},{1,2},{2,3},{3,4},{4,5},{5,6},{6,7},{7,0},{8,9},{9,10},{10,1... | collective-permute-start | bytes 933896 | tf_op jit(solution)/shard_map/ppermute | solution.py:399
  11.7 5.1 %collective-permute-start.2 = (f32[84,128]{1,0:T(8,128)S(1)}, f32[84,128]{1,0:T(8,128)S(1)}, u32[]{:S(2)}, u32[]{:S(2)}) collective-permute-start(f32[84,128]{1,0:T(8,128)S(1)} %get-tuple-element.41), channel_id=1, source_target_pairs={{0,1},{1,2},{2,3},{3,4},{4,5},{5,6},{6,7},{7,0},{8,9},{9,10},{10,1... | collective-permute-start | bytes 129032 | tf_op jit(solution)/shard_map/ppermute | solution.py:404
  14.2 3.8 %collective-permute-start.3 = (f32[84,128]{1,0:T(8,128)S(1)}, f32[84,128]{1,0:T(8,128)S(1)}, u32[]{:S(2)}, u32[]{:S(2)}) collective-permute-start(f32[84,128]{1,0:T(8,128)S(1)} %get-tuple-element.42), channel_id=1, source_target_pairs={{1,0},{2,1},{3,2},{4,3},{5,4},{6,5},{7,6},{0,7},{9,8},{10,9},{11,1... | collective-permute-start | bytes 129032 | tf_op jit(solution)/shard_map/ppermute | solution.py:405
  18.0 14.3 %copy-start = (f32[8,32,128]{2,1,0:T(8,128)S(1)}, f32[8,32,128]{2,1,0:T(8,128)}, u32[]{:S(2)}) copy-start(f32[8,32,128]{2,1,0:T(8,128)} %density.1) | copy-start | bytes 393220
  18.0 14.3 %copy-start.1 = (f32[32,128]{1,0:T(8,128)S(1)}, f32[32,128]{1,0:T(8,128)}, u32[]{:S(2)}) copy-start(f32[32,128]{1,0:T(8,128)} %thickness.1) | copy-start | bytes 49156
  18.0 14.3 %copy-start.2 = (f32[32,128]{1,0:T(8,128)S(1)}, f32[32,128]{1,0:T(8,128)}, u32[]{:S(2)}) copy-start(f32[32,128]{1,0:T(8,128)} %smb.1) | copy-start | bytes 49156
